TPU v7x, 256 devices: a whole 4x4x8 slice. The times are simulated.
256 devices in a mesh: rep: 16 (over x, z_lo, core), shard: 16 (over y, z_hi).
Axes of the slice: x: 4, y: 4, z: 8 (z_hi: 4, z_lo: 2; z = z_hi * 2 + z_lo), core: 2. Of those that a mesh axis runs over, the one named last changes fastest.
Arguments:
- hidden: bfloat16 [16, 4096, 8192], P('rep', 'shard'), may hold values from -6 to 6
- cotangent: bfloat16 [16, 4096, 512], P('rep', 'shard'), may hold values from -48 to 48
- norm_gain: float32 [8192], replicated, may hold values from 0.1 to 1.9
- params: float32 [16, 8192, 512], P('rep', 'shard'), may hold values from -6 to 6
- adam_first: float32 [16, 8192, 512], P('rep', 'shard'), may hold values from -4 to 4
- adam_second: float32 [16, 8192, 512], P('rep', 'shard'), may hold values from 0.25 to 4
- outer_anchor: float32 [16, 16, 32, 512], P('shard', 'rep'), may hold values from -6 to 6
- outer_momentum: float32 [16, 16, 32, 512], P('shard', 'rep'), may hold values from -4 to 4
- fragment: int32 [], replicated, may hold values from 0 to 3
- inner_step: int32 [], replicated, may hold values from 1 to 2048
Outputs:
- value_rows: bfloat16 [16, 4096, 512], P('rep', 'shard')
- new_params: float32 [16, 8192, 512], P('rep', 'shard')
- new_first: float32 [16, 8192, 512], P('rep', 'shard')
- new_second: float32 [16, 8192, 512], P('rep', 'shard')
- new_anchor: float32 [16, 16, 32, 512], P('shard', 'rep')
- new_momentum: float32 [16, 16, 32, 512], P('shard', 'rep')
All inputs are finite; a program needn't handle non-finite values.
Results may differ from a plain program's by a relative error of at most 0.0048.
The roundings to bfloat16 on the way count: a program that leaves them out, or rounds other values in their place, can miss the bound.
Values may be sent and summed in bfloat16 or wider, within the bound.
No kernel may reach another device: no remote copies, remote signals or barrier semaphores. Data moves between devices by JAX's collectives and lax.ppermute only.
A program may use at most 128 MiB of HBM per device.

v0:
```python
import math

import jax
import jax.numpy as jnp
from jax import lax
from jax.sharding import PartitionSpec as P

FRAG = 4


FIRST_DECAY = 0.9
SECOND_DECAY = 0.95
ADAM_EPSILON = 1e-08
PEAK_RATE = 0.125
WEIGHT_DECAY = 0.1
HORIZON_STEPS = 4096.0
OUTER_RATE = 0.7
OUTER_MOMENTUM = 0.9
NORM_EPSILON = 1e-05


def normalise(rows, gain):
    widened = rows.astype(jnp.float32)
    spread = jnp.mean(widened * widened, axis=-1, keepdims=True)
    return (widened * lax.rsqrt(spread + NORM_EPSILON) * gain).astype(jnp.bfloat16)


def adam_update(weights, gradient, first, second, inner_step):
    clock = inner_step.astype(jnp.float32)
    rate = PEAK_RATE * 0.5 * (1.0 + jnp.cos(math.pi * clock / HORIZON_STEPS))
    first_corr = 1.0 - jnp.power(FIRST_DECAY, clock)
    second_corr = 1.0 - jnp.power(SECOND_DECAY, clock)
    first_new = FIRST_DECAY * first + (1.0 - FIRST_DECAY) * gradient
    second_new = SECOND_DECAY * second + (1.0 - SECOND_DECAY) * gradient * gradient
    update = first_new / first_corr / (jnp.sqrt(second_new / second_corr) + ADAM_EPSILON)
    stepped = weights - rate * (update + WEIGHT_DECAY * weights)
    return (stepped, first_new, second_new)


def contract_tokens(left, right):
    return lax.dot_general(
        left, right, (((0,), (0,)), ((), ())), preferred_element_type=jnp.float32
    )


def local(
    hidden,
    cotangent,
    norm_gain,
    params,
    adam_first,
    adam_second,
    outer_anchor,
    outer_momentum,
    fragment,
    inner_step,
):
    tokens = hidden[0]
    cot_local = cotangent[0]
    weights = params[0]
    factor = tokens.shape[1] ** (-0.5)
    normed = normalise(tokens, norm_gain)
    weights_half = weights.astype(jnp.bfloat16)
    feature_block = normed
    summed = jnp.dot(
        feature_block,
        lax.all_gather(weights_half, "shard", axis=0, tiled=True),
        preferred_element_type=jnp.float32,
    )
    value_rows = (summed * factor).astype(jnp.bfloat16)
    feature_block = normed
    gradient = (
        lax.psum_scatter(
            contract_tokens(feature_block, cot_local), "shard", scatter_dimension=0, tiled=True
        )
        * factor
    )
    stepped, first_new, second_new = adam_update(
        weights, gradient, adam_first[0], adam_second[0], inner_step
    )
    frag_width = weights.shape[1] // FRAG
    frag_start = fragment * frag_width
    own_frag = lax.dynamic_slice_in_dim(weights, frag_start, frag_width, 1)
    anchor_local = outer_anchor[0, 0]
    moment_local = outer_momentum[0, 0]
    anchor_frag = lax.dynamic_slice_in_dim(anchor_local, frag_start, frag_width, 1)
    moment_frag = lax.dynamic_slice_in_dim(moment_local, frag_start, frag_width, 1)
    block_height = anchor_local.shape[0]
    replicas = lax.axis_size("rep")
    params_total = lax.psum(own_frag, "rep")
    anchor_rows, moment_rows = (
        lax.all_gather(anchor_frag, "rep", axis=0, tiled=True),
        lax.all_gather(moment_frag, "rep", axis=0, tiled=True),
    )
    delta_rows = anchor_rows - params_total / replicas
    moment_rows_new = OUTER_MOMENTUM * moment_rows + delta_rows
    anchor_rows_new = anchor_rows - OUTER_RATE * (delta_rows + OUTER_MOMENTUM * moment_rows_new)
    row_offset = lax.axis_index("rep") * block_height
    moment_new = lax.dynamic_slice_in_dim(moment_rows_new, row_offset, block_height, 0)
    anchor_new = lax.dynamic_slice_in_dim(anchor_rows_new, row_offset, block_height, 0)
    stepped_frag = lax.dynamic_slice_in_dim(stepped, frag_start, frag_width, 1)
    merged_frag = anchor_rows_new + (stepped_frag - own_frag)
    params_out = lax.dynamic_update_slice_in_dim(stepped, merged_frag, frag_start, 1)
    anchor_out = lax.dynamic_update_slice_in_dim(anchor_local, anchor_new, frag_start, 1)
    moment_out = lax.dynamic_update_slice_in_dim(moment_local, moment_new, frag_start, 1)
    return (
        value_rows[None],
        params_out[None],
        first_new[None],
        second_new[None],
        anchor_out[None, None],
        moment_out[None, None],
    )


def solution(mesh):
    in_specs = (
        P("rep", "shard", None),
        P("rep", "shard", None),
        P(),
        P("rep", "shard", None),
        P("rep", "shard", None),
        P("rep", "shard", None),
        P("shard", "rep", None, None),
        P("shard", "rep", None, None),
        P(),
        P(),
    )
    out_specs = (
        P("rep", "shard", None),
        P("rep", "shard", None),
        P("rep", "shard", None),
        P("rep", "shard", None),
        P("shard", "rep", None, None),
        P("shard", "rep", None, None),
    )
    return jax.shard_map(local, mesh=mesh, in_specs=in_specs, out_specs=out_specs, check_vma=False)
```

profile of v0, /device:TPU:2, one launch (start us, length us, event | category | flops | bytes accessed | tf_op | source)
XLA Modules:
  0.0 361.9 jit_solution(4929172203254512569)
XLA Ops:
  8.0 0.0 copy-start
  8.0 0.0 all-reduce.2.cloned.1.call-start
  8.1 0.9 copy.25
  8.9 0.8 copy.24
  10.4 1.7 dynamic-slice_bitcast_fusion
  12.1 0.0 all-reduce.2.cloned.1.call-update
  12.1 0.0 all-gather.4.cloned.1.call-start
  12.2 2.1 bitcast_convert_fusion
  14.3 0.0 all-gather.4.cloned.1.call-update
  14.3 0.0 reduce-scatter.2.cloned.1.call-start
  14.3 3.1 fusion.2
  17.5 10.4 %fusion.8 = f32[8192,512]{1,0:T(8,128)} fusion(bf16[1,256,8192]{2,1,0:T(8,128)(2,1)} %param.10, f32[8192]{0:T(1024)} %param.12, f32[256]{0:T(256)S(1)} %add_rsqrt_fusion, bf16[1,256,512]{2,1,0:T(8,128)(2,1)S(1)} %copy-done), kind=kOutput, calls=%fused_computation.10 | convolution fusion | flops 2155872256 | bytes 21267456 | tf_op jit(solution)/shard_map/dot_general | solution.py:41
  27.9 0.0 reduce-scatter.2.cloned.1.call-update
  28.8 22.4 %all-gather.1 = f32[1,1,512,128]{3,2,1,0:T(8,128)S(1)} all-gather(f32[1,1,32,128]{3,2,1,0:T(8,128)S(1)} %constant_dynamic-slice_fusion), channel_id=3, replica_groups=mesh['rep'=16,'shard'=16] {'rep'}, dimensions={2}, use_global_device_ids=true | all-gather | bytes 278528 | tf_op jit(solution)/shard_map/all_gather | solution.py:93
  51.2 18.1 %all-gather = f32[1,1,512,128]{3,2,1,0:T(8,128)S(1)} all-gather(f32[1,1,32,128]{3,2,1,0:T(8,128)S(1)} %constant_dynamic-slice_fusion.1), channel_id=2, replica_groups=mesh['rep'=16,'shard'=16] {'rep'}, dimensions={2}, use_global_device_ids=true | all-gather | bytes 278528 | tf_op jit(solution)/shard_map/all_gather | solution.py:92
  69.3 197.8 %all-reduce.2.cloned.1.call-done = f32[512,128]{1,0:T(8,128)} async-done(((f32[512,128]{1,0:T(8,128)}), f32[512,128]{1,0:T(8,128)}) %all-reduce.2.cloned.1.call-update) | async-done | bytes 262160 | tf_op jit(solution)/shard_map/psum | solution.py:90
  267.1 1.0 bitcast_add_fusion.2
  268.1 0.0 all-gather.4.cloned.1.call-done
  268.2 8.3 %fusion.22 = bf16[1,256,512]{2,1,0:T(8,128)(2,1)} fusion(bf16[8192,512]{1,0:T(8,128)(2,1)} %all-gather.4.cloned.1.call-done, bf16[1,256,8192]{2,1,0:T(8,128)(2,1)} %param.10, f32[8192]{0:T(1024)S(1)} %copy-done.7, f32[256]{0:T(256)S(1)} %add_rsqrt_fusion), kind=kOutput, calls=%fused_computation.18 | convolution fusion | flops 2156134400 | bytes 12878848 | tf_op jit(solution)/shard_map/dot_general | solution.py:65
  276.5 73.1 %reduce-scatter.2.cloned.1.call-done = f32[512,512]{1,0:T(8,128)} async-done(((f32[8192,512]{1,0:T(8,128)}), f32[512,512]{1,0:T(8,128)}) %reduce-scatter.2.cloned.1.call-update) | async-done | bytes 1048592 | tf_op jit(solution)/shard_map/reduce_scatter | solution.py:73
  349.6 3.7 %fusion.29 = (f32[1,512,512]{2,1,0:T(8,128)}, f32[512,512]{1,0:T(8,128)S(1)}, f32[1,512,512]{2,1,0:T(8,128)}) fusion(f32[512,512]{1,0:T(8,128)} %reduce-scatter.2.cloned.1.call-done, f32[1,512,512]{2,1,0:T(8,128)S(1)} %copy-done.3, f32[]{:T(128)S(6)} %sub.19, f32[]{:T(128)S(6)} %sub.18, f32[1,512,512]{2,1,0:T(8,128)} %param.14, f32[]{:T(128)S(6)} %mul_shard_map.4, ...), kind=kLoop, calls=%fused_computation.33 | loop fusion | flops 4194304 | bytes 7340044 | tf_op jit(solution)/shard_map/broadcast_in_dim | solution.py:110
  353.2 0.1 copy.17
  353.3 0.1 bitcast_dynamic-update-slice_fusion
  353.5 0.9 copy-done.2
  (19 shorter events, 0.1 us)
Async XLA Ops:
  8.0 9.5 %copy-start = (bf16[1,256,512]{2,1,0:T(8,128)(2,1)S(1)}, bf16[1,256,512]{2,1,0:T(8,128)(2,1)}, u32[]{:S(2)}) copy-start(bf16[1,256,512]{2,1,0:T(8,128)(2,1)} %param.11) | copy-start | bytes 786436
  8.0 259.1 %all-reduce.2.cloned.1.call-start = ((), (), s32[]{:S(2)}) async-start(), calls=%async_computation.3 | async-start | bytes 524288 | tf_op jit(solution)/shard_map/psum | solution.py:90
  12.1 256.0 %all-gather.4.cloned.1.call-start = ((), (), s32[]{:S(2)}) async-start(), calls=%async_computation.1 | async-start | bytes 8912896 | tf_op jit(solution)/shard_map/all_gather | solution.py:67
  14.3 335.3 %reduce-scatter.2.cloned.1.call-start = ((), (), s32[]{:S(2)}) async-start(), calls=%async_computation.2 | async-start | bytes 17825792 | tf_op jit(solution)/shard_map/reduce_scatter | solution.py:73
  27.9 240.3 %copy-start.7 = (f32[8192]{0:T(1024)S(1)}, f32[8192]{0:T(1024)}, u32[]{:S(2)}) copy-start(f32[8192]{0:T(1024)} %param.12) | copy-start | bytes 98308
  268.1 8.4 %copy-start.6 = (f32[1,1,32,512]{3,2,1,0:T(8,128)}, f32[1,1,32,512]{3,2,1,0:T(8,128)S(1)}, u32[]{:S(2)}) copy-start(f32[1,1,32,512]{3,2,1,0:T(8,128)S(1)} %bitcast_dynamic-update-slice_fusion.1) | copy-start | bytes 196612
  268.1 81.5 %copy-start.1 = (f32[1,512,512]{2,1,0:T(8,128)S(1)}, f32[1,512,512]{2,1,0:T(8,128)}, u32[]{:S(2)}) copy-start(f32[1,512,512]{2,1,0:T(8,128)} %param.13) | copy-start | bytes 3145732
  268.1 81.5 %copy-start.3 = (f32[1,512,512]{2,1,0:T(8,128)S(1)}, f32[1,512,512]{2,1,0:T(8,128)}, u32[]{:S(2)}) copy-start(f32[1,512,512]{2,1,0:T(8,128)} %param.15) | copy-start | bytes 3145732
  276.5 76.8 %copy-start.4 = (f32[512,128]{1,0:T(8,128)S(1)}, f32[512,128]{1,0:T(8,128)}, u32[]{:S(2)}) copy-start(f32[512,128]{1,0:T(8,128)} %all-reduce.2.cloned.1.call-done) | copy-start | bytes 786436
  353.4 1.0 copy-start.2
  353.5 0.9 copy-start.5
Sparse Core Ops, SparseCore 0:
  12.3 254.7 all-reduce.1
Sparse Core Ops, SparseCore 1:
  15.6 124.5 all-gather.3
  143.7 205.8 reduce-scatter.1
where the time goes:
time: 363 us; the launch traced here: 362 us
  waiting for transfers between devices  271 us (75%)
  blocking collectives  40.5 us (11%)
  matrix products  18.8 us (5%)
  between operations  17.1 us (5%)
  other arithmetic  9.98 us (3%)
  local copies, waits for them, and re-layouts  4.48 us (1%)
    psum x1, waiting for transfers between devices, local(): params_total = lax.psum(own_frag, 'rep')  198 us
    reduce_scatter x1, waiting for transfers between devices, local(): lax.psum_scatter(contract_tokens(feature_block, cot_local), 'shard', scat...  73.1 us
    all_gather x1, blocking collectives, local(): lax.all_gather(moment_frag, 'rep', axis=0, tiled=True)  22.4 us
    all_gather x1, blocking collectives, local(): lax.all_gather(anchor_frag, 'rep', axis=0, tiled=True)  18.1 us
    dot_general x1, matrix products, contract_tokens(): lax.dot_general(left, right, (((0,), (0,)), ((), ())), preferred_element_...  10.4 us
    dot_general x1, matrix products, local(): jnp.dot(feature_block, lax.all_gather(weights_half, 'shard', axis=0, tile...  8.33 us
  transfers between devices with their start and end apart: 3, of which 2 were waited for; matrix products, arithmetic and copies ran while one was open for 7% of the time, Pallas kernels for 0%

commit v1 on v0

v1 whole, which is shorter than its diff:
```python
import functools
import math

import jax
import jax.numpy as jnp
from jax import lax
from jax.experimental import pallas as pl
from jax.experimental.pallas import tpu as pltpu
from jax.sharding import PartitionSpec as P

FRAG = 4
RING = 4
CHUNKS = 2

FIRST_DECAY = 0.9
SECOND_DECAY = 0.95
ADAM_EPSILON = 1e-08
PEAK_RATE = 0.125
WEIGHT_DECAY = 0.1
HORIZON_STEPS = 4096.0
OUTER_RATE = 0.7
OUTER_MOMENTUM = 0.9
NORM_EPSILON = 1e-05

VMEM_LIMIT = 50 * 1024 * 1024
F32 = jnp.float32
BF16 = jnp.bfloat16


def shift_y(array, k):
    pairs = [(y * RING + z, (y + k) % RING * RING + z) for y in range(RING) for z in range(RING)]
    return lax.ppermute(array, "shard", pairs)


def shift_z(array, k):
    pairs = [(y * RING + z, y * RING + (z + k) % RING) for y in range(RING) for z in range(RING)]
    return lax.ppermute(array, "shard", pairs)


def swap_rep(array, bit):
    return lax.ppermute(array, "rep", [(r, r ^ bit) for r in range(16)])


def shift_x(array, k):
    return lax.ppermute(array, "rep", [(r, (r + 4 * k) % 16) for r in range(16)])


def whole(n):
    return [pl.BlockSpec(memory_space=pltpu.VMEM)] * n


def scalars():
    return pl.BlockSpec(memory_space=pltpu.SMEM)


def params_of():
    return pltpu.CompilerParams(vmem_limit_bytes=VMEM_LIMIT)


def pack_kernel(place, hidden_ref, gain_ref, *outs):
    y, z = place[0], place[1]
    features = hidden_ref.shape[1]
    group = features // RING
    width = group // RING // CHUNKS
    widened = hidden_ref[...].astype(F32)
    scale = lax.rsqrt(jnp.mean(widened * widened, axis=-1, keepdims=True) + NORM_EPSILON)
    for chunk in range(CHUNKS):
        for ky in range(RING):
            for kz in range(RING):
                start = lax.rem(y + ky, RING) * group + lax.rem(z + RING - kz, RING) * (group // RING) + chunk * width
                columns = pl.ds(pl.multiple_of(start, width), width)
                block = hidden_ref[:, columns].astype(F32) * scale * gain_ref[:, columns]
                outs[chunk * RING + ky][:, kz * width : (kz + 1) * width] = block.astype(BF16)


def pack(place, hidden, gain):
    tokens, features = hidden.shape
    rows = 32
    width = features // RING // CHUNKS
    outs = CHUNKS * RING
    flat = pl.pallas_call(
        pack_kernel,
        out_shape=[jax.ShapeDtypeStruct((tokens, width), BF16)] * outs,
        grid_spec=pltpu.PrefetchScalarGridSpec(
            num_scalar_prefetch=1,
            grid=(tokens // rows,),
            in_specs=[
                pl.BlockSpec((rows, features), lambda i, place: (i, 0)),
                pl.BlockSpec((1, features), lambda i, place: (0, 0)),
            ],
            out_specs=[pl.BlockSpec((rows, width), lambda i, place: (i, 0))] * outs,
        ),
        compiler_params=params_of(),
        cost_estimate=pl.CostEstimate(flops=0, bytes_accessed=4 * tokens * features, transcendentals=0),
        name="pack",
    )(place, hidden, gain)
    return [flat[c * RING : (c + 1) * RING] for c in range(CHUNKS)]


def gradient_kernel(*refs):
    normed, cot = refs[:RING], refs[RING : 2 * RING]
    own, left, right, keep_left, keep_right = refs[2 * RING :]
    height = own.shape[0]
    half = height // 2
    cot_all = jnp.concatenate([c[...] for c in cot], axis=0)

    def block(kz):
        rows = jnp.concatenate([n[:, kz * height : (kz + 1) * height] for n in normed], axis=0)
        return lax.dot_general(rows, cot_all, (((0,), (0,)), ((), ())), preferred_element_type=F32)

    far = block(2).astype(BF16)
    left[:half] = far[:half]
    right[half:] = far[half:]
    near = block(1)
    keep_left[...] = near[:half]
    left[half:] = near[half:].astype(BF16)
    near = block(3)
    keep_right[...] = near[half:]
    right[:half] = near[:half].astype(BF16)
    own[...] = block(0)


def gradient_chunk(normed, cot):
    tokens, width = normed[0].shape
    columns = cot[0].shape[1]
    height = width // RING
    full, part = (height, columns), (height // 2, columns)
    return pl.pallas_call(
        gradient_kernel,
        out_shape=[
            jax.ShapeDtypeStruct(full, F32),
            jax.ShapeDtypeStruct(full, BF16),
            jax.ShapeDtypeStruct(full, BF16),
            jax.ShapeDtypeStruct(part, F32),
            jax.ShapeDtypeStruct(part, F32),
        ],
        in_specs=whole(2 * RING),
        out_specs=whole(5),
        compiler_params=params_of(),
        cost_estimate=pl.CostEstimate(
            flops=2 * RING * tokens * width * columns, bytes_accessed=2 * RING * tokens * (width + columns) + 8 * width * columns // 4, transcendentals=0
        ),
        name="gradient_chunk",
    )(*normed, *cot)


def values_kernel(*refs):
    n = CHUNKS * RING
    normed = refs[:n]
    own, before, far_top, far_bottom, after = refs[n : n + 5]
    outs = refs[n + 5 :]
    height = own.shape[0]
    step = height // CHUNKS
    half = height // 2
    totals = [None] * RING
    for chunk in range(CHUNKS):
        rows = slice(chunk * step, (chunk + 1) * step)
        if chunk * step < half:
            assert (chunk + 1) * step <= half or CHUNKS == 1
            far = far_top[chunk * step : (chunk + 1) * step]
        else:
            far = far_bottom[chunk * step - half : (chunk + 1) * step - half]
        weights = jnp.concatenate([own[rows], before[rows], far, after[rows]], axis=0)
        for ky in range(RING):
            product = jnp.dot(normed[chunk * RING + ky][...], weights, preferred_element_type=F32)
            totals[ky] = product if chunk == 0 else totals[ky] + product
    for ky in range(RING):
        outs[ky][...] = totals[ky].astype(outs[ky].dtype)


def values_partial(normed, weights):
    tokens, width = normed[0].shape
    columns = weights[0].shape[1]
    return pl.pallas_call(
        values_kernel,
        out_shape=[jax.ShapeDtypeStruct((tokens, columns), F32 if k == 0 else BF16) for k in range(RING)],
        in_specs=whole(len(normed) + 5),
        out_specs=whole(RING),
        compiler_params=params_of(),
        cost_estimate=pl.CostEstimate(
            flops=2 * tokens * width * columns * len(normed), bytes_accessed=2 * tokens * width * len(normed) + 8 * tokens * columns + 8 * 512 * columns, transcendentals=0
        ),
        name="values_partial",
    )(*normed, *weights)


def adam_kernel(place, rates, weights, first, second, *refs):
    pieces = refs[: 5 * CHUNKS]
    anchor_near, anchor_far, out_weights, out_first, out_second = refs[5 * CHUNKS :]
    fragment, rep = place[2], place[3]
    x, zl, core = rep // 4, lax.rem(rep // 2, 2), lax.rem(rep, 2)
    rate, first_scale, second_scale, factor = rates[0], rates[1], rates[2], rates[3]
    step = weights.shape[0] // CHUNKS
    width = weights.shape[1] // FRAG
    for chunk in range(CHUNKS):
        own, from_left, from_right, last_left, last_right = pieces[5 * chunk : 5 * chunk + 5]
        half = step // 2
        for part in range(2):
            if part == 0:
                total = own[:half] + from_right[:half].astype(F32) + last_left[...].astype(F32)
            else:
                total = own[half:] + from_left[half:].astype(F32) + last_right[...].astype(F32)
            rows = slice(chunk * step + part * half, chunk * step + (part + 1) * half)
            gradient = total * factor
            first_new = FIRST_DECAY * first[rows] + (1.0 - FIRST_DECAY) * gradient
            second_new = SECOND_DECAY * second[rows] + (1.0 - SECOND_DECAY) * gradient * gradient
            out_first[rows] = first_new
            out_second[rows] = second_new
            update = (first_new * first_scale) / (jnp.sqrt(second_new * second_scale) + ADAM_EPSILON)
            out_weights[rows] = weights[rows] - rate * (update + WEIGHT_DECAY * weights[rows])
    for q in range(FRAG):

        @pl.when(fragment == q)
        def _():
            columns = slice(q * width, (q + 1) * width)
            for r in range(16):
                rows = slice(r * 32, (r + 1) * 32)
                where = lax.rem(x + 4 - r // 4, 4)
                other = lax.rem(zl + r // 2, 2)
                base = jnp.where(core == r % 2, anchor_near[other * 4 + where], anchor_far[other * 4 + where])
                out_weights[rows, columns] = base + (out_weights[rows, columns] - weights[rows, columns])


def adam(place, rates, weights, first, second, pieces, anchor_near, anchor_far):
    shape = jax.ShapeDtypeStruct(weights.shape, F32)
    return pl.pallas_call(
        adam_kernel,
        out_shape=[shape] * 3,
        in_specs=[scalars(), scalars()] + whole(3 + len(pieces) + 2),
        out_specs=whole(3),
        compiler_params=params_of(),
        cost_estimate=pl.CostEstimate(flops=20 * weights.size, bytes_accessed=32 * weights.size, transcendentals=0),
        name="adam",
    )(place, rates, weights, first, second, *pieces, anchor_near, anchor_far)


def pick(array, index, axis):
    return lax.dynamic_index_in_dim(array, index, axis, keepdims=False)


def local(
    hidden,
    cotangent,
    norm_gain,
    params,
    adam_first,
    adam_second,
    outer_anchor,
    outer_momentum,
    fragment,
    inner_step,
):
    tokens = hidden[0]
    cot_local = cotangent[0]
    weights = params[0]
    factor = tokens.shape[1] ** (-0.5)
    shard = lax.axis_index("shard")
    rep = lax.axis_index("rep")
    place = jnp.stack([shard // RING, shard % RING, fragment, rep]).astype(jnp.int32)

    weights_half = weights.astype(BF16)
    half = weights.shape[0] // 2
    before = shift_z(weights_half, 1)
    after = shift_z(weights_half, -1)
    cot = [cot_local] + [shift_y(cot_local, k) for k in (1, 3, 2)]

    packed = pack(place, tokens, norm_gain.reshape(1, -1))
    normed = []
    for chunk in range(CHUNKS):
        mine = packed[chunk]
        normed.append([mine[0]] + [shift_y(mine[k], k) for k in (1, 3, 2)])
    far_top = shift_z(before[:half], 1)
    far_bottom = shift_z(after[half:], -1)

    frag_width = weights.shape[1] // FRAG
    frag_start = fragment * frag_width
    x, zl, core = rep // 4, rep // 2 % 2, rep % 2
    total = lax.dynamic_slice_in_dim(weights, frag_start, frag_width, 1).reshape(4, 2, 2, -1, frag_width)
    total = pick(total, core, 2) + swap_rep(pick(total, 1 - core, 2), 1)
    total = pick(total, zl, 1) + swap_rep(pick(total, 1 - zl, 1), 2)
    arrived = [shift_x(pick(total, (x + k) % 4, 0), k) for k in (1, 2, 3)]
    total = pick(total, x, 0) + arrived[0] + arrived[1] + arrived[2]
    anchor_local = outer_anchor[0, 0]
    moment_local = outer_momentum[0, 0]
    anchor_frag = lax.dynamic_slice_in_dim(anchor_local, frag_start, frag_width, 1)
    moment_frag = lax.dynamic_slice_in_dim(moment_local, frag_start, frag_width, 1)
    delta = anchor_frag - total / lax.axis_size("rep")
    moment_new = OUTER_MOMENTUM * moment_frag + delta
    anchor_new = anchor_frag - OUTER_RATE * (delta + OUTER_MOMENTUM * moment_new)
    anchor_out = lax.dynamic_update_slice_in_dim(anchor_local, anchor_new, frag_start, 1)
    moment_out = lax.dynamic_update_slice_in_dim(moment_local, moment_new, frag_start, 1)
    near = jnp.stack([anchor_new] + [shift_x(anchor_new, k) for k in (1, 2, 3)])
    near = jnp.concatenate([near, swap_rep(near, 2)])
    far = swap_rep(near, 1)

    pieces = []
    for chunk in range(CHUNKS):
        own, left, right, keep_left, keep_right = gradient_chunk(normed[chunk], cot)
        from_left, from_right = shift_z(left, -1), shift_z(right, 1)
        quarter = from_left.shape[0] // 2
        last_left = (keep_left + from_left[:quarter].astype(F32)).astype(BF16)
        last_right = (keep_right + from_right[quarter:].astype(F32)).astype(BF16)
        pieces += [own, from_left, from_right, shift_z(last_left, -1), shift_z(last_right, 1)]

    partial = values_partial(sum(normed, []), [weights_half, before, far_top, far_bottom, after])
    summed = partial[0]
    for k, source in zip((1, 3, 2), partial[1:]):
        summed = summed + shift_y(source, -k).astype(F32)
    value_rows = (summed * factor).astype(BF16)

    clock = inner_step.astype(F32)
    rate = PEAK_RATE * 0.5 * (1.0 + jnp.cos(math.pi * clock / HORIZON_STEPS))
    first_scale = 1.0 / (1.0 - jnp.power(FIRST_DECAY, clock))
    second_scale = 1.0 / (1.0 - jnp.power(SECOND_DECAY, clock))
    rates = jnp.stack([rate, first_scale, second_scale, jnp.full((), factor, F32)])
    params_out, first_new, second_new = adam(
        place, rates, weights, adam_first[0], adam_second[0], pieces, near, far
    )
    return (
        value_rows[None],
        params_out[None],
        first_new[None],
        second_new[None],
        anchor_out[None, None],
        moment_out[None, None],
    )


def solution(mesh):
    in_specs = (
        P("rep", "shard", None),
        P("rep", "shard", None),
        P(),
        P("rep", "shard", None),
        P("rep", "shard", None),
        P("rep", "shard", None),
        P("shard", "rep", None, None),
        P("shard", "rep", None, None),
        P(),
        P(),
    )
    out_specs = (
        P("rep", "shard", None),
        P("rep", "shard", None),
        P("rep", "shard", None),
        P("rep", "shard", None),
        P("shard", "rep", None, None),
        P("shard", "rep", None, None),
    )
    return jax.shard_map(local, mesh=mesh, in_specs=in_specs, out_specs=out_specs, check_vma=False)
```

time: 363 us -> 147 us (0.40)
  waiting for transfers between devices: 271 us -> 41.8 us
  starting transfers between devices: 0.13 us -> 63.7 us
  blocking collectives: 40.5 us -> 0 us
  Pallas kernels: 0 us -> 21.4 us
  matrix products: 18.8 us -> 0 us
  between operations: 17.1 us -> 2.54 us
  local copies, waits for them, and re-layouts: 4.48 us -> 12.9 us
  other arithmetic: 9.98 us -> 3.42 us
    psum x1 -> x0, waiting for transfers between devices: 198 us -> none  [local(): params_total = lax.psum(own_frag, 'rep')]
    reduce_scatter x1 -> x0, waiting for transfers between devices: 73.1 us -> none  [local(): lax.psum_scatter(contract_tokens(feature_block, cot_local), 'shard', scat...]
    ppermute x0 -> x34, starting transfers between devices: none -> 63.7 us  [the longest x12 27.4 us: shift_y(): return lax.ppermute(array, 'shard', pairs)]
    ppermute x0 -> x34, waiting for transfers between devices: none -> 41.8 us  [the longest x12 13.6 us: shift_y(): return lax.ppermute(array, 'shard', pairs)]
    all_gather x2 -> x0, blocking collectives: 40.5 us -> none  [the longest x1 22.4 us: local(): lax.all_gather(moment_frag, 'rep', axis=0, tiled=True)]
    pallas_call x0 -> x5, Pallas kernels: none -> 21.4 us  [the longest x1 7.33 us: pack(): pl.pallas_call(pack_kernel, out_shape=[jax.ShapeDtypeStruct((tokens, widt...]
    dot_general x2 -> x0, matrix products: 18.8 us -> none  [the longest x1 10.4 us: contract_tokens(): lax.dot_general(left, right, (((0,), (0,)), ((), ())), preferred_element_...]
    unnamed x19 -> x49, local copies, waits for them, and re-layouts: 2.76 us -> 9.25 us
  transfers between devices with their start and end apart: 3 -> 34, of which waited for: 2 -> 11; matrix products, arithmetic and copies ran while one was open for 7% -> 5% of each run, Pallas kernels for 0% -> 15%
where the time goes in v1:
time: 147 us; the launch traced here: 146 us
  starting transfers between devices  63.7 us (43%)
  waiting for transfers between devices  41.8 us (28%)
  Pallas kernels  21.4 us (15%)
  local copies, waits for them, and re-layouts  12.9 us (9%)
  other arithmetic  3.42 us (2%)
  between operations  2.54 us (2%)
    ppermute x12, starting transfers between devices, shift_y(): return lax.ppermute(array, 'shard', pairs)  27.4 us
    ppermute x12, starting transfers between devices, shift_z(): return lax.ppermute(array, 'shard', pairs)  24.1 us
    ppermute x12, waiting for transfers between devices, shift_y(): return lax.ppermute(array, 'shard', pairs)  13.6 us
    ppermute x4, waiting for transfers between devices, swap_rep(): return lax.ppermute(array, 'rep', [(r, r ^ bit) for r in range(16)])  13.3 us
    ppermute x12, waiting for transfers between devices, shift_z(): return lax.ppermute(array, 'shard', pairs)  13 us
    unnamed x49, local copies, waits for them, and re-layouts  9.25 us
    ppermute x6, starting transfers between devices, shift_x(): lax.ppermute(array, 'rep', [(r, (r + 4 * k) % 16) for r in range(16)])  9.08 us
    pallas_call x1, Pallas kernels, pack(): pl.pallas_call(pack_kernel, out_shape=[jax.ShapeDtypeStruct((tokens, widt...  7.33 us
  transfers between devices with their start and end apart: 34, of which 11 were waited for; matrix products, arithmetic and copies ran while one was open for 5% of the time, Pallas kernels for 15%

profile of v1, /device:TPU:2, one launch (start us, length us, event | category | flops | bytes accessed | tf_op | source)
XLA Modules:
  0.0 145.8 jit_solution(7098880244991264904)
XLA Ops:
  21.3 7.3 %pack.1 = (bf16[256,1024]{1,0:T(8,128)(2,1)S(1)}, bf16[256,1024]{1,0:T(8,128)(2,1)}, bf16[256,1024]{1,0:T(8,128)(2,1)S(1)}, bf16[256,1024]{1,0:T(8,128)(2,1)S(1)...) custom-call(s32[4]{0:T(128)S(1)} %pad_add_fusion.place, ...), custom_call_target="tpu_custom_call" | custom-call | bytes 8388608 | tf_op jit(solution)/shard_map/pack/pallas_call | solution.py:81
  31.5 2.6 %collective-permute-start.30 = (f32[32,128]{1,0:T(8,128)S(1)}, f32[32,128]{1,0:T(8,128)S(1)}, u32[]{:S(2)}, u32[]{:S(2)}) collective-permute-start(f32[32,128]{1,0:T(8,128)S(1)} %get-tuple-element.59), channel_id=1, source_target_pairs={{0,128},{16,144},{32,160},{48,176},{64,192},{80,208},{96,224},{112... | collective-permute-start | bytes 49160 | tf_op jit(solution)/shard_map/ppermute | solution.py:45
  36.8 3.3 %collective-permute-start.6 = (bf16[512,512]{1,0:T(8,128)(2,1)}, bf16[512,512]{1,0:T(8,128)(2,1)}, u32[]{:S(2)}, u32[]{:S(2)}) collective-permute-start(bf16[512,512]{1,0:T(8,128)(2,1)} %bitcast_convert_fusion.refs_8_), channel_id=1, source_target_pairs={{0,1},{1,2},{2,3},{3,0},{4,5},{5,6},{6,7},{7,4},{8,9},{9,10},{10,1... | collective-permute-start | bytes 1572872 | tf_op jit(solution)/shard_map/ppermute | solution.py:37
  40.1 4.1 %collective-permute-start.8 = (bf16[512,512]{1,0:T(8,128)(2,1)}, bf16[512,512]{1,0:T(8,128)(2,1)}, u32[]{:S(2)}, u32[]{:S(2)}) collective-permute-start(bf16[512,512]{1,0:T(8,128)(2,1)} %bitcast_convert_fusion.refs_8_), channel_id=1, source_target_pairs={{0,3},{1,0},{2,1},{3,2},{4,7},{5,4},{6,5},{7,6},{8,11},{9,8},{10,9... | collective-permute-start | bytes 1572872 | tf_op jit(solution)/shard_map/ppermute | solution.py:37
  44.2 3.0 %collective-permute-start.15 = (bf16[256,512]{1,0:T(8,128)(2,1)S(1)}, bf16[256,512]{1,0:T(8,128)(2,1)}, u32[]{:S(2)}, u32[]{:S(2)}) collective-permute-start(bf16[256,512]{1,0:T(8,128)(2,1)S(1)} %bitcast.73), channel_id=1, source_target_pairs={{0,8},{1,9},{2,10},{3,11},{4,12},{5,13},{6,14},{7,15},{8,0},{9,1},... | collective-permute-start | bytes 786440 | tf_op jit(solution)/shard_map/ppermute | solution.py:32
  52.3 2.9 %collective-permute-start.1 = (bf16[256,1024]{1,0:T(8,128)(2,1)}, bf16[256,1024]{1,0:T(8,128)(2,1)S(1)}, u32[]{:S(2)}, u32[]{:S(2)}) collective-permute-start(bf16[256,1024]{1,0:T(8,128)(2,1)} %copy-done.5), channel_id=1, source_target_pairs={{0,12},{1,13},{2,14},{3,15},{4,0},{5,1},{6,2},{7,3},{8,4},{9,5},{1... | collective-permute-start | bytes 1572872 | tf_op jit(solution)/shard_map/ppermute | solution.py:32
  55.2 9.6 %collective-permute-done.32 = f32[4,32,128]{2,1,0:T(8,128)S(1)} collective-permute-done((f32[4,32,128]{2,1,0:T(8,128)S(1)}, f32[4,32,128]{2,1,0:T(8,128)S(1)}, u32[]{:S(2)}, u32[]{:S(2)}) %collective-permute-start.32) | collective-permute-done | bytes 65568 | tf_op jit(solution)/shard_map/ppermute | solution.py:41
  64.8 2.9 %collective-permute-start.2 = (bf16[256,1024]{1,0:T(8,128)(2,1)}, bf16[256,1024]{1,0:T(8,128)(2,1)S(1)}, u32[]{:S(2)}, u32[]{:S(2)}) collective-permute-start(bf16[256,1024]{1,0:T(8,128)(2,1)} %copy-done.4), channel_id=1, source_target_pairs={{0,8},{1,9},{2,10},{3,11},{4,12},{5,13},{6,14},{7,15},{8,0},{9,1},... | collective-permute-start | bytes 1572872 | tf_op jit(solution)/shard_map/ppermute | solution.py:32
  68.4 3.2 %collective-permute-start.4 = (bf16[256,1024]{1,0:T(8,128)(2,1)}, bf16[256,1024]{1,0:T(8,128)(2,1)S(1)}, u32[]{:S(2)}, u32[]{:S(2)}) collective-permute-start(bf16[256,1024]{1,0:T(8,128)(2,1)} %get-tuple-element.37), channel_id=1, source_target_pairs={{0,12},{1,13},{2,14},{3,15},{4,0},{5,1},{6,2},{7,3},{8,4},{9,5},{1... | collective-permute-start | bytes 1572872 | tf_op jit(solution)/shard_map/ppermute | solution.py:32
  76.3 4.4 %collective-permute-done.2.refs_3_ = bf16[256,1024]{1,0:T(8,128)(2,1)S(1)} collective-permute-done((bf16[256,1024]{1,0:T(8,128)(2,1)}, bf16[256,1024]{1,0:T(8,128)(2,1)S(1)}, u32[]{:S(2)}, u32[]{:S(2)}) %collective-permute-start.2) | collective-permute-done | bytes 524320 | tf_op jit(solution)/shard_map/ppermute | solution.py:32
  81.4 2.7 %gradient_chunk.2 = (f32[256,512]{1,0:T(8,128)S(1)}, bf16[256,512]{1,0:T(8,128)(2,1)S(1)}, bf16[256,512]{1,0:T(8,128)(2,1)S(1)}, f32[128,512]{1,0:T(8,128)S(1)}, f32[128,512]{1,0:T(8,128)S(1)}) custom-call(bf16[256,1024]{1,0:T(8,128)(2,1)S(1)} %get-tuple-element.31.refs_0_, bf16[256,1024]{1,0:T(8,128)(2,1)S(1)} %collective-permute-done.refs_1_, ...), custom_call_target="tpu_custom_call" | custom-call | flops 1073741824 | bytes 4194304 | tf_op jit(solution)/shard_map/gradient_chunk/pallas_call | solution.py:128
  86.2 5.0 %collective-permute-done.4.refs_6_.refs_2_ = bf16[256,1024]{1,0:T(8,128)(2,1)S(1)} collective-permute-done((bf16[256,1024]{1,0:T(8,128)(2,1)}, bf16[256,1024]{1,0:T(8,128)(2,1)S(1)}, u32[]{:S(2)}, u32[]{:S(2)}) %collective-permute-start.4) | collective-permute-done | bytes 524320 | tf_op jit(solution)/shard_map/ppermute | solution.py:32
  91.2 2.5 %collective-permute-start.16 = (bf16[256,512]{1,0:T(8,128)(2,1)S(1)}, bf16[256,512]{1,0:T(8,128)(2,1)S(1)}, u32[]{:S(2)}, u32[]{:S(2)}) collective-permute-start(bf16[256,512]{1,0:T(8,128)(2,1)S(1)} %get-tuple-element.44), channel_id=1, source_target_pairs={{0,3},{1,0},{2,1},{3,2},{4,7},{5,4},{6,5},{7,6},{8,11},{9,8},{10,9... | collective-permute-start | bytes 786440 | tf_op jit(solution)/shard_map/ppermute | solution.py:37
  95.3 2.7 %gradient_chunk.3 = (f32[256,512]{1,0:T(8,128)S(1)}, bf16[256,512]{1,0:T(8,128)(2,1)S(1)}, bf16[256,512]{1,0:T(8,128)(2,1)S(1)}, f32[128,512]{1,0:T(8,128)S(1)}, f32[128,512]{1,0:T(8,128)S(1)}) custom-call(bf16[256,1024]{1,0:T(8,128)(2,1)S(1)} %get-tuple-element.35.refs_4_.refs_0_, bf16[256,1024]{1,0:T(8,128)(2,1)S(1)} %collective-permute-done.3.refs_5_.refs_1_, ...), custom_call_target="tpu_custom_call" | custom-call | flops 1073741824 | bytes 4194304 | tf_op jit(solution)/shard_map/gradient_chunk/pallas_call | solution.py:128
  98.0 2.6 %collective-permute-start.20 = (bf16[256,512]{1,0:T(8,128)(2,1)S(1)}, bf16[256,512]{1,0:T(8,128)(2,1)S(1)}, u32[]{:S(2)}, u32[]{:S(2)}) collective-permute-start(bf16[256,512]{1,0:T(8,128)(2,1)S(1)} %get-tuple-element.49), channel_id=1, source_target_pairs={{0,3},{1,0},{2,1},{3,2},{4,7},{5,4},{6,5},{7,6},{8,11},{9,8},{10,9... | collective-permute-start | bytes 786440 | tf_op jit(solution)/shard_map/ppermute | solution.py:37
  103.2 4.4 %values_partial.1 = (f32[256,512]{1,0:T(8,128)S(1)}, bf16[256,512]{1,0:T(8,128)(2,1)S(1)}, bf16[256,512]{1,0:T(8,128)(2,1)S(1)}, bf16[256,512]{1,0:T(8,128)(2,1)S(1)}) custom-call(bf16[256,1024]{1,0:T(8,128)(2,1)S(1)} %get-tuple-element.31.refs_0_, bf16[256,1024]{1,0:T(8,128)(2,1)S(1)} %collective-permute-done.refs_1_, bf16[256,1024]{1,0:T(8,128)(2,1)S(1)} %copy-done.7, ...), custom_call_target="tpu_custom_call" | custom-call | flops 2147483648 | bytes 7340032 | tf_op jit(solution)/shard_map/values_partial/pallas_call | solution.py:174
  107.6 7.3 %collective-permute-start.12 = (bf16[256,512]{1,0:T(8,128)(2,1)S(1)}, bf16[256,512]{1,0:T(8,128)(2,1)S(1)}, u32[]{:S(2)}, u32[]{:S(2)}) collective-permute-start(bf16[256,512]{1,0:T(8,128)(2,1)S(1)} %get-tuple-element.42), channel_id=1, source_target_pairs={{0,8},{1,9},{2,10},{3,11},{4,12},{5,13},{6,14},{7,15},{8,0},{9,1},... | collective-permute-start | bytes 786440 | tf_op jit(solution)/shard_map/ppermute | solution.py:32
  116.5 2.8 %collective-permute-start.10 = (bf16[256,512]{1,0:T(8,128)(2,1)S(1)}, bf16[256,512]{1,0:T(8,128)(2,1)S(1)}, u32[]{:S(2)}, u32[]{:S(2)}) collective-permute-start(bf16[256,512]{1,0:T(8,128)(2,1)S(1)} %get-tuple-element.40), channel_id=1, source_target_pairs={{0,12},{1,13},{2,14},{3,15},{4,0},{5,1},{6,2},{7,3},{8,4},{9,5},{1... | collective-permute-start | bytes 786440 | tf_op jit(solution)/shard_map/ppermute | solution.py:32
  119.3 2.5 %collective-permute-start.18 = (bf16[128,512]{1,0:T(8,128)(2,1)S(1)}, bf16[128,512]{1,0:T(8,128)(2,1)S(1)}, u32[]{:S(2)}, u32[]{:S(2)}) collective-permute-start(bf16[128,512]{1,0:T(8,128)(2,1)S(1)} %add_convert_fusion.3), channel_id=1, source_target_pairs={{0,3},{1,0},{2,1},{3,2},{4,7},{5,4},{6,5},{7,6},{8,11},{9,8},{10,9... | collective-permute-start | bytes 393224 | tf_op jit(solution)/shard_map/ppermute | solution.py:37
  122.4 5.3 %collective-permute-done.18.refs_3_ = bf16[128,512]{1,0:T(8,128)(2,1)S(1)} collective-permute-done((bf16[128,512]{1,0:T(8,128)(2,1)S(1)}, bf16[128,512]{1,0:T(8,128)(2,1)S(1)}, u32[]{:S(2)}, u32[]{:S(2)}) %collective-permute-start.18) | collective-permute-done | bytes 131104 | tf_op jit(solution)/shard_map/ppermute | solution.py:37
  127.6 4.6 %collective-permute-start.22 = (bf16[128,512]{1,0:T(8,128)(2,1)S(1)}, bf16[128,512]{1,0:T(8,128)(2,1)S(1)}, u32[]{:S(2)}, u32[]{:S(2)}) collective-permute-start(bf16[128,512]{1,0:T(8,128)(2,1)S(1)} %add_convert_fusion.1), channel_id=1, source_target_pairs={{0,3},{1,0},{2,1},{3,2},{4,7},{5,4},{6,5},{7,6},{8,11},{9,8},{10,9... | collective-permute-start | bytes 393224 | tf_op jit(solution)/shard_map/ppermute | solution.py:37
  132.8 2.9 %collective-permute-done.22.refs_8_ = bf16[128,512]{1,0:T(8,128)(2,1)S(1)} collective-permute-done((bf16[128,512]{1,0:T(8,128)(2,1)S(1)}, bf16[128,512]{1,0:T(8,128)(2,1)S(1)}, u32[]{:S(2)}, u32[]{:S(2)}) %collective-permute-start.22) | collective-permute-done | bytes 131104 | tf_op jit(solution)/shard_map/ppermute | solution.py:37
  135.8 4.8 %collective-permute-done.23.refs_9_ = bf16[128,512]{1,0:T(8,128)(2,1)S(1)} collective-permute-done((bf16[128,512]{1,0:T(8,128)(2,1)S(1)}, bf16[128,512]{1,0:T(8,128)(2,1)S(1)}, u32[]{:S(2)}, u32[]{:S(2)}) %collective-permute-start.23) | collective-permute-done | bytes 131104 | tf_op jit(solution)/shard_map/ppermute | solution.py:37
  140.6 4.3 %adam.1 = (f32[512,512]{1,0:T(8,128)}, f32[512,512]{1,0:T(8,128)}, f32[512,512]{1,0:T(8,128)}) custom-call(s32[4]{0:T(128)S(1)} %pad_add_fusion.place, f32[4]{0:T(128)S(1)} %pad_maximum_fusion.1.rates, f32[512,512]{1,0:T(8,128)S(1)} %bitcast.69, f32[512,512]{1,0:T(8,128)} %bitcast.77, f32[512,512]{1,0:T(8,128)} %bitcast.78, ...), custom_call_target="tpu_custom_call" | custom-call | flops 5242880 | bytes 8388608 | tf_op jit(solution)/shard_map/adam/pallas_call | solution.py:226
  (120 shorter events, 45.6 us)
Async XLA Ops:
  15.0 29.2 %collective-permute-start.13 = (bf16[256,512]{1,0:T(8,128)(2,1)}, bf16[256,512]{1,0:T(8,128)(2,1)}, u32[]{:S(2)}, u32[]{:S(2)}) collective-permute-start(bf16[256,512]{1,0:T(8,128)(2,1)} %bitcast.71), channel_id=1, source_target_pairs={{0,4},{1,5},{2,6},{3,7},{4,8},{5,9},{6,10},{7,11},{8,12},{9,13},{1... | collective-permute-start | bytes 786440 | tf_op jit(solution)/shard_map/ppermute | solution.py:32
  16.5 32.3 %collective-permute-start.14 = (bf16[256,512]{1,0:T(8,128)(2,1)}, bf16[256,512]{1,0:T(8,128)(2,1)}, u32[]{:S(2)}, u32[]{:S(2)}) collective-permute-start(bf16[256,512]{1,0:T(8,128)(2,1)} %bitcast.72), channel_id=1, source_target_pairs={{0,12},{1,13},{2,14},{3,15},{4,0},{5,1},{6,2},{7,3},{8,4},{9,5},{1... | collective-permute-start | bytes 786440 | tf_op jit(solution)/shard_map/ppermute | solution.py:32
  18.9 15.3 %collective-permute-start.29 = (f32[32,128]{1,0:T(8,128)S(1)}, f32[32,128]{1,0:T(8,128)S(1)}, u32[]{:S(2)}, u32[]{:S(2)}) collective-permute-start(f32[32,128]{1,0:T(8,128)S(1)} %get-tuple-element.59), channel_id=1, source_target_pairs={{0,64},{16,80},{32,96},{48,112},{64,128},{80,144},{96,160},{112,17... | collective-permute-start | bytes 49160 | tf_op jit(solution)/shard_map/ppermute | solution.py:45
  31.0 37.4 %collective-permute-start = (bf16[256,1024]{1,0:T(8,128)(2,1)}, bf16[256,1024]{1,0:T(8,128)(2,1)S(1)}, u32[]{:S(2)}, u32[]{:S(2)}) collective-permute-start(bf16[256,1024]{1,0:T(8,128)(2,1)} %get-tuple-element.32), channel_id=1, source_target_pairs={{0,4},{1,5},{2,6},{3,7},{4,8},{5,9},{6,10},{7,11},{8,12},{9,13},{1... | collective-permute-start | bytes 1572872 | tf_op jit(solution)/shard_map/ppermute | solution.py:32
  36.8 31.6 %collective-permute-start.6 = (bf16[512,512]{1,0:T(8,128)(2,1)}, bf16[512,512]{1,0:T(8,128)(2,1)}, u32[]{:S(2)}, u32[]{:S(2)}) collective-permute-start(bf16[512,512]{1,0:T(8,128)(2,1)} %bitcast_convert_fusion.refs_8_), channel_id=1, source_target_pairs={{0,1},{1,2},{2,3},{3,0},{4,5},{5,6},{6,7},{7,4},{8,9},{9,10},{10,1... | collective-permute-start | bytes 1572872 | tf_op jit(solution)/shard_map/ppermute | solution.py:37
  40.1 31.6 %collective-permute-start.8 = (bf16[512,512]{1,0:T(8,128)(2,1)}, bf16[512,512]{1,0:T(8,128)(2,1)}, u32[]{:S(2)}, u32[]{:S(2)}) collective-permute-start(bf16[512,512]{1,0:T(8,128)(2,1)} %bitcast_convert_fusion.refs_8_), channel_id=1, source_target_pairs={{0,3},{1,0},{2,1},{3,2},{4,7},{5,4},{6,5},{7,6},{8,11},{9,8},{10,9... | collective-permute-start | bytes 1572872 | tf_op jit(solution)/shard_map/ppermute | solution.py:37
  48.9 15.9 %collective-permute-start.32 = (f32[4,32,128]{2,1,0:T(8,128)S(1)}, f32[4,32,128]{2,1,0:T(8,128)S(1)}, u32[]{:S(2)}, u32[]{:S(2)}) collective-permute-start(f32[4,32,128]{2,1,0:T(8,128)S(1)} %pad_maximum_fusion), channel_id=1, source_target_pairs={{0,32},{16,48},{32,0},{48,16},{64,96},{80,112},{96,64},{112,80},{1... | collective-permute-start | bytes 196616 | tf_op jit(solution)/shard_map/ppermute | solution.py:41
  52.3 22.8 %collective-permute-start.1 = (bf16[256,1024]{1,0:T(8,128)(2,1)}, bf16[256,1024]{1,0:T(8,128)(2,1)S(1)}, u32[]{:S(2)}, u32[]{:S(2)}) collective-permute-start(bf16[256,1024]{1,0:T(8,128)(2,1)} %copy-done.5), channel_id=1, source_target_pairs={{0,12},{1,13},{2,14},{3,15},{4,0},{5,1},{6,2},{7,3},{8,4},{9,5},{1... | collective-permute-start | bytes 1572872 | tf_op jit(solution)/shard_map/ppermute | solution.py:32
  64.8 15.8 %collective-permute-start.2 = (bf16[256,1024]{1,0:T(8,128)(2,1)}, bf16[256,1024]{1,0:T(8,128)(2,1)S(1)}, u32[]{:S(2)}, u32[]{:S(2)}) collective-permute-start(bf16[256,1024]{1,0:T(8,128)(2,1)} %copy-done.4), channel_id=1, source_target_pairs={{0,8},{1,9},{2,10},{3,11},{4,12},{5,13},{6,14},{7,15},{8,0},{9,1},... | collective-permute-start | bytes 1572872 | tf_op jit(solution)/shard_map/ppermute | solution.py:32
  68.4 17.7 %collective-permute-start.3 = (bf16[256,1024]{1,0:T(8,128)(2,1)}, bf16[256,1024]{1,0:T(8,128)(2,1)S(1)}, u32[]{:S(2)}, u32[]{:S(2)}) collective-permute-start(bf16[256,1024]{1,0:T(8,128)(2,1)} %copy-done.3), channel_id=1, source_target_pairs={{0,4},{1,5},{2,6},{3,7},{4,8},{5,9},{6,10},{7,11},{8,12},{9,13},{1... | collective-permute-start | bytes 1572872 | tf_op jit(solution)/shard_map/ppermute | solution.py:32
  68.4 22.7 %collective-permute-start.4 = (bf16[256,1024]{1,0:T(8,128)(2,1)}, bf16[256,1024]{1,0:T(8,128)(2,1)S(1)}, u32[]{:S(2)}, u32[]{:S(2)}) collective-permute-start(bf16[256,1024]{1,0:T(8,128)(2,1)} %get-tuple-element.37), channel_id=1, source_target_pairs={{0,12},{1,13},{2,14},{3,15},{4,0},{5,1},{6,2},{7,3},{8,4},{9,5},{1... | collective-permute-start | bytes 1572872 | tf_op jit(solution)/shard_map/ppermute | solution.py:32
  71.7 22.0 %collective-permute-start.5 = (bf16[256,1024]{1,0:T(8,128)(2,1)S(1)}, bf16[256,1024]{1,0:T(8,128)(2,1)S(1)}, u32[]{:S(2)}, u32[]{:S(2)}) collective-permute-start(bf16[256,1024]{1,0:T(8,128)(2,1)S(1)} %get-tuple-element.38), channel_id=1, source_target_pairs={{0,8},{1,9},{2,10},{3,11},{4,12},{5,13},{6,14},{7,15},{8,0},{9,1},... | collective-permute-start | bytes 1572872 | tf_op jit(solution)/shard_map/ppermute | solution.py:32
  75.1 22.9 %collective-permute-start.7 = (bf16[256,512]{1,0:T(8,128)(2,1)S(1)}, bf16[256,512]{1,0:T(8,128)(2,1)S(1)}, u32[]{:S(2)}, u32[]{:S(2)}) collective-permute-start(bf16[256,512]{1,0:T(8,128)(2,1)S(1)} %slice.24), channel_id=1, source_target_pairs={{0,1},{1,2},{2,3},{3,0},{4,5},{5,6},{6,7},{7,4},{8,9},{9,10},{10,1... | collective-permute-start | bytes 786440 | tf_op jit(solution)/shard_map/ppermute | solution.py:37
  80.6 20.0 %collective-permute-start.9 = (bf16[256,512]{1,0:T(8,128)(2,1)S(1)}, bf16[256,512]{1,0:T(8,128)(2,1)S(1)}, u32[]{:S(2)}, u32[]{:S(2)}) collective-permute-start(bf16[256,512]{1,0:T(8,128)(2,1)S(1)} %slice.25), channel_id=1, source_target_pairs={{0,3},{1,0},{2,1},{3,2},{4,7},{5,4},{6,5},{7,6},{8,11},{9,8},{10,9... | collective-permute-start | bytes 786440 | tf_op jit(solution)/shard_map/ppermute | solution.py:37
  86.2 33.2 %collective-permute-start.33 = (f32[8,32,128]{2,1,0:T(8,128)S(1)}, f32[8,32,128]{2,1,0:T(8,128)S(1)}, u32[]{:S(2)}, u32[]{:S(2)}) collective-permute-start(f32[8,32,128]{2,1,0:T(8,128)S(1)} %constant_dynamic-update-slice_fusion.refs_10_), channel_id=1, source_target_pairs={{0,16},{16,0},{32,48},{48,32},{64,80},{80,64},{96,112},{112,96},{1... | collective-permute-start | bytes 393224 | tf_op jit(solution)/shard_map/ppermute | solution.py:41
  91.2 16.4 %collective-permute-start.16 = (bf16[256,512]{1,0:T(8,128)(2,1)S(1)}, bf16[256,512]{1,0:T(8,128)(2,1)S(1)}, u32[]{:S(2)}, u32[]{:S(2)}) collective-permute-start(bf16[256,512]{1,0:T(8,128)(2,1)S(1)} %get-tuple-element.44), channel_id=1, source_target_pairs={{0,3},{1,0},{2,1},{3,2},{4,7},{5,4},{6,5},{7,6},{8,11},{9,8},{10,9... | collective-permute-start | bytes 786440 | tf_op jit(solution)/shard_map/ppermute | solution.py:37
  93.6 21.3 %collective-permute-start.17 = (bf16[256,512]{1,0:T(8,128)(2,1)S(1)}, bf16[256,512]{1,0:T(8,128)(2,1)S(1)}, u32[]{:S(2)}, u32[]{:S(2)}) collective-permute-start(bf16[256,512]{1,0:T(8,128)(2,1)S(1)} %get-tuple-element.45), channel_id=1, source_target_pairs={{0,1},{1,2},{2,3},{3,0},{4,5},{5,6},{6,7},{7,4},{8,9},{9,10},{10,1... | collective-permute-start | bytes 786440 | tf_op jit(solution)/shard_map/ppermute | solution.py:37
  98.0 18.5 %collective-permute-start.20 = (bf16[256,512]{1,0:T(8,128)(2,1)S(1)}, bf16[256,512]{1,0:T(8,128)(2,1)S(1)}, u32[]{:S(2)}, u32[]{:S(2)}) collective-permute-start(bf16[256,512]{1,0:T(8,128)(2,1)S(1)} %get-tuple-element.49), channel_id=1, source_target_pairs={{0,3},{1,0},{2,1},{3,2},{4,7},{5,4},{6,5},{7,6},{8,11},{9,8},{10,9... | collective-permute-start | bytes 786440 | tf_op jit(solution)/shard_map/ppermute | solution.py:37
  100.6 21.2 %collective-permute-start.21 = (bf16[256,512]{1,0:T(8,128)(2,1)S(1)}, bf16[256,512]{1,0:T(8,128)(2,1)S(1)}, u32[]{:S(2)}, u32[]{:S(2)}) collective-permute-start(bf16[256,512]{1,0:T(8,128)(2,1)S(1)} %get-tuple-element.50), channel_id=1, source_target_pairs={{0,1},{1,2},{2,3},{3,0},{4,5},{5,6},{6,7},{7,4},{8,9},{9,10},{10,1... | collective-permute-start | bytes 786440 | tf_op jit(solution)/shard_map/ppermute | solution.py:37
  107.6 37.3 %collective-permute-start.12 = (bf16[256,512]{1,0:T(8,128)(2,1)S(1)}, bf16[256,512]{1,0:T(8,128)(2,1)S(1)}, u32[]{:S(2)}, u32[]{:S(2)}) collective-permute-start(bf16[256,512]{1,0:T(8,128)(2,1)S(1)} %get-tuple-element.42), channel_id=1, source_target_pairs={{0,8},{1,9},{2,10},{3,11},{4,12},{5,13},{6,14},{7,15},{8,0},{9,1},... | collective-permute-start | bytes 786440 | tf_op jit(solution)/shard_map/ppermute | solution.py:32
  115.0 29.9 %collective-permute-start.11 = (bf16[256,512]{1,0:T(8,128)(2,1)S(1)}, bf16[256,512]{1,0:T(8,128)(2,1)S(1)}, u32[]{:S(2)}, u32[]{:S(2)}) collective-permute-start(bf16[256,512]{1,0:T(8,128)(2,1)S(1)} %get-tuple-element.41), channel_id=1, source_target_pairs={{0,4},{1,5},{2,6},{3,7},{4,8},{5,9},{6,10},{7,11},{8,12},{9,13},{1... | collective-permute-start | bytes 786440 | tf_op jit(solution)/shard_map/ppermute | solution.py:32
  116.5 28.4 %collective-permute-start.10 = (bf16[256,512]{1,0:T(8,128)(2,1)S(1)}, bf16[256,512]{1,0:T(8,128)(2,1)S(1)}, u32[]{:S(2)}, u32[]{:S(2)}) collective-permute-start(bf16[256,512]{1,0:T(8,128)(2,1)S(1)} %get-tuple-element.40), channel_id=1, source_target_pairs={{0,12},{1,13},{2,14},{3,15},{4,0},{5,1},{6,2},{7,3},{8,4},{9,5},{1... | collective-permute-start | bytes 786440 | tf_op jit(solution)/shard_map/ppermute | solution.py:32
  121.8 10.4 %collective-permute-start.19 = (bf16[128,512]{1,0:T(8,128)(2,1)S(1)}, bf16[128,512]{1,0:T(8,128)(2,1)S(1)}, u32[]{:S(2)}, u32[]{:S(2)}) collective-permute-start(bf16[128,512]{1,0:T(8,128)(2,1)S(1)} %add_convert_fusion.2), channel_id=1, source_target_pairs={{0,1},{1,2},{2,3},{3,0},{4,5},{5,6},{6,7},{7,4},{8,9},{9,10},{10,1... | collective-permute-start | bytes 393224 | tf_op jit(solution)/shard_map/ppermute | solution.py:37
  132.2 8.4 %collective-permute-start.23 = (bf16[128,512]{1,0:T(8,128)(2,1)S(1)}, bf16[128,512]{1,0:T(8,128)(2,1)S(1)}, u32[]{:S(2)}, u32[]{:S(2)}) collective-permute-start(bf16[128,512]{1,0:T(8,128)(2,1)S(1)} %add_convert_fusion), channel_id=1, source_target_pairs={{0,1},{1,2},{2,3},{3,0},{4,5},{5,6},{6,7},{7,4},{8,9},{9,10},{10,1... | collective-permute-start | bytes 393224 | tf_op jit(solution)/shard_map/ppermute | solution.py:37
  (32 other events, 376.9 us)

commit v2 on v0

v2 whole, which is shorter than its diff:
```python
import functools
import math

import jax
import jax.numpy as jnp
from jax import lax
from jax.experimental import pallas as pl
from jax.experimental.pallas import tpu as pltpu
from jax.sharding import PartitionSpec as P

FRAG = 4
RING = 4
N_REP = 16
CHUNKS = ((0, 256), (256, 256))

FIRST_DECAY = 0.9
SECOND_DECAY = 0.95
ADAM_EPSILON = 1e-08
PEAK_RATE = 0.125
WEIGHT_DECAY = 0.1
HORIZON_STEPS = 4096.0
OUTER_RATE = 0.7
OUTER_MOMENTUM = 0.9
NORM_EPSILON = 1e-05

COST = pl.CostEstimate(flops=1, bytes_accessed=1, transcendentals=0)
VMEM_LIMIT = 62 * 1024 * 1024
F32 = jnp.float32
BF16 = jnp.bfloat16


def exchange_y(array):
    groups = [[y * RING + z for y in range(RING)] for z in range(RING)]
    return lax.all_to_all(array, "shard", 0, 0, axis_index_groups=groups, tiled=True)


def shift_z(array, k):
    pairs = [(y * RING + z, y * RING + (z + k) % RING) for y in range(RING) for z in range(RING)]
    return lax.ppermute(array, "shard", pairs)


def swap_rep(array, bit):
    return lax.ppermute(array, "rep", [(r, r ^ bit) for r in range(16)])


def shift_y(array, k):
    pairs = [(y * RING + z, (y + k) % RING * RING + z) for y in range(RING) for z in range(RING)]
    return lax.ppermute(array, "shard", pairs)


def whole(n):
    return [pl.BlockSpec(memory_space=pltpu.VMEM)] * n


def scalars():
    return pl.BlockSpec(memory_space=pltpu.SMEM)


def params_of():
    return pltpu.CompilerParams(vmem_limit_bytes=VMEM_LIMIT)


def first_pack_kernel(place, hidden_ref, gain_ref, cot_ref, out, scale_ref):
    z = place[1]
    group = hidden_ref.shape[1] // RING
    block = group // RING
    first, width = CHUNKS[0]
    widened = hidden_ref[...].astype(F32)
    scale = lax.rsqrt(jnp.mean(widened * widened, axis=-1, keepdims=True) + NORM_EPSILON)
    scale_ref[...] = scale
    for y in range(RING):
        for kz in range(RING):
            start = y * group + lax.rem(z + RING - kz, RING) * block + first
            columns = pl.ds(pl.multiple_of(start, 128), width)
            normed = hidden_ref[:, columns].astype(F32) * scale * gain_ref[:, columns]
            out[y, :, kz * width : (kz + 1) * width] = normed.astype(BF16)
        out[y, :, RING * width :] = cot_ref[...]


def first_pack(place, hidden, gain, cot):
    tokens, features = hidden.shape
    columns = cot.shape[1]
    rows = 64
    total = RING * CHUNKS[0][1] + columns
    return pl.pallas_call(
        first_pack_kernel,
        out_shape=[pltpu.HBM((RING, tokens, total), BF16), pltpu.HBM((tokens, 1), F32)],
        grid_spec=pltpu.PrefetchScalarGridSpec(
            num_scalar_prefetch=1,
            grid=(tokens // rows,),
            in_specs=[
                pl.BlockSpec((rows, features), lambda i, place: (i, 0)),
                pl.BlockSpec((1, features), lambda i, place: (0, 0)),
                pl.BlockSpec((rows, columns), lambda i, place: (i, 0)),
            ],
            out_specs=[
                pl.BlockSpec((RING, rows, total), lambda i, place: (0, i, 0)),
                pl.BlockSpec((rows, 1), lambda i, place: (i, 0)),
            ],
        ),
        compiler_params=params_of(),
        cost_estimate=COST,
        name="first_pack",
    )(place, hidden, gain, cot)


def later_pack_kernel(place, *refs):
    hidden, gain, scale = refs[:RING], refs[RING : 2 * RING], refs[2 * RING]
    outs = refs[-RING:]
    for ky in range(RING):
        outs[ky][...] = (hidden[ky][...].astype(F32) * scale[...] * gain[ky][...]).astype(BF16)


def later_pack(place, hidden, gain, scale, after):
    tokens, features = hidden.shape
    first, width = CHUNKS[1]
    per_place = features // RING // RING // width

    def column(ky):
        def at(kz, place):
            whose = lax.rem(place[0] + ky, RING) * RING + lax.rem(place[1] + RING - kz, RING)
            return (0, whose * per_place + first // width)

        return at

    return pl.pallas_call(
        later_pack_kernel,
        out_shape=[pltpu.HBM((tokens, RING * width), BF16)] * RING,
        grid_spec=pltpu.PrefetchScalarGridSpec(
            num_scalar_prefetch=1,
            grid=(RING,),
            in_specs=[pl.BlockSpec((tokens, width), column(ky)) for ky in range(RING)]
            + [pl.BlockSpec((1, width), column(ky)) for ky in range(RING)]
            + [pl.BlockSpec((tokens, 1), lambda kz, place: (0, 0))]
            + [pl.BlockSpec(memory_space=pl.ANY)] * len(after),
            out_specs=[pl.BlockSpec((tokens, width), lambda kz, place: (0, kz))] * RING,
        ),
        compiler_params=params_of(),
        cost_estimate=COST,
        name="later_pack",
    )(place, *[hidden] * RING, *[gain] * RING, scale, *after)


def gradient_block(normed, cot, kz, height):
    rows = jnp.concatenate([n[:, kz * height : (kz + 1) * height] for n in normed], axis=0)
    return lax.dot_general(rows, cot, (((0,), (0,)), ((), ())), preferred_element_type=F32)


def gradient_blocks(normed, cot, own, left, right, keep_left, keep_right):
    height = own.shape[0]
    half = height // 2
    far = gradient_block(normed, cot, 2, height).astype(BF16)
    left[:half] = far[:half]
    right[half:] = far[half:]
    near = gradient_block(normed, cot, 1, height)
    keep_left[...] = near[:half]
    left[half:] = near[half:].astype(BF16)
    near = gradient_block(normed, cot, 3, height)
    keep_right[...] = near[half:]
    right[:half] = near[:half].astype(BF16)
    own[...] = gradient_block(normed, cot, 0, height)


def first_gradient_kernel(normed, cot, *refs):
    rows = [normed.at[y] for y in range(RING)]
    gradient_blocks(rows, jnp.concatenate([cot[y] for y in range(RING)], axis=0), *refs[-5:])


def first_gradient(arrived, after):
    tokens = arrived.shape[1]
    height = CHUNKS[0][1]
    columns = arrived.shape[2] - RING * height
    full, part = (height, columns), (height // 2, columns)
    shapes = [(full, F32), (full, BF16), (full, BF16), (part, F32), (part, F32)]
    cot_at = RING * height // columns
    return pl.pallas_call(
        first_gradient_kernel,
        grid=(1,),
        out_shape=[pltpu.HBM(*s) for s in shapes],
        in_specs=[
            pl.BlockSpec((RING, tokens, RING * height), lambda i: (0, 0, 0)),
            pl.BlockSpec((RING, tokens, columns), lambda i: (0, 0, cot_at)),
        ]
        + [pl.BlockSpec(memory_space=pl.ANY)] * len(after),
        out_specs=[pl.BlockSpec(s[0], lambda i: (0, 0)) for s in shapes],
        compiler_params=params_of(),
        cost_estimate=COST,
        name="first_gradient",
    )(arrived, arrived, *after)


def later_gradient_kernel(place, *refs):
    normed, cot = refs[:RING], refs[RING]
    keep_left, keep_right, from_left, from_right = refs[RING + 1 : RING + 5]
    own, left, right, next_left, next_right = refs[-5:]
    half = keep_left.shape[0]
    left[:half] = (keep_left[...] + from_left[:half].astype(F32)).astype(BF16)
    right[:half] = (keep_right[...] + from_right[half:].astype(F32)).astype(BF16)
    cot_all = jnp.concatenate([cot[lax.rem(place[0] + RING - k, RING)] for k in range(RING)], axis=0)
    gradient_blocks(normed, cot_all, own, left.at[half:], right.at[half:], next_left, next_right)


def later_gradient(place, normed, arrived, kept, after):
    tokens = arrived.shape[1]
    height = CHUNKS[1][1]
    columns = kept[0].shape[1]
    full, part = (height, columns), (height // 2, columns)
    sent = (height + kept[0].shape[0], columns)
    shapes = [(full, F32), (sent, BF16), (sent, BF16), (part, F32), (part, F32)]
    cot_at = RING * CHUNKS[0][1] // columns
    return pl.pallas_call(
        later_gradient_kernel,
        grid=(1,),
        out_shape=[pltpu.HBM(*s) for s in shapes],
        in_specs=[scalars()]
        + [pl.BlockSpec((tokens, RING * height), lambda i: (0, 0))] * RING
        + [pl.BlockSpec((RING, tokens, columns), lambda i: (0, 0, cot_at))]
        + [pl.BlockSpec(k.shape, lambda i: (0, 0)) for k in kept]
        + [pl.BlockSpec(memory_space=pl.ANY)] * len(after),
        out_specs=[pl.BlockSpec(s[0], lambda i: (0, 0)) for s in shapes],
        compiler_params=params_of(),
        cost_estimate=COST,
        name="later_gradient",
    )(place, *normed, arrived, *kept, *after)


def chunk_weights(chunk, own, before, far_top, far_bottom, after):
    first, width = CHUNKS[chunk]
    rows = slice(first, first + width)
    half = far_top.shape[0]
    far = []
    if first < half:
        far.append(far_top[first : min(first + width, half)])
    if first + width > half:
        far.append(far_bottom[max(first - half, 0) : first + width - half])
    return jnp.concatenate([own[rows], before[rows]] + far + [after[rows]], axis=0)


def values_kernel(place, arrived, *refs):
    later, weights = refs[:RING], refs[RING : RING + 5]
    outs = refs[-RING:]
    first_weights, later_weights = chunk_weights(0, *weights), chunk_weights(1, *weights)
    for k in (2, 1, 3, 0):
        y = lax.rem(place[0] + RING - k, RING)
        total = jnp.dot(arrived[y], first_weights, preferred_element_type=F32)
        total += jnp.dot(later[k][...], later_weights, preferred_element_type=F32)
        outs[k][...] = total.astype(outs[k].dtype)


def values_partial(place, arrived, later, weights, needed):
    tokens = arrived.shape[1]
    columns = weights[0].shape[1]
    shape = (tokens, columns)
    return pl.pallas_call(
        values_kernel,
        grid=(1,),
        out_shape=[pltpu.HBM(shape, F32 if k == 0 else BF16) for k in range(RING)],
        in_specs=[scalars(), pl.BlockSpec((RING, tokens, RING * CHUNKS[0][1]), lambda i: (0, 0, 0))]
        + [pl.BlockSpec(w.shape, lambda i: (0, 0)) for w in (*later, *weights)]
        + [pl.BlockSpec(memory_space=pl.ANY)] * len(needed),
        out_specs=[pl.BlockSpec(shape, lambda i: (0, 0))] * RING,
        compiler_params=params_of(),
        cost_estimate=COST,
        name="values_partial",
    )(place, arrived, *later, *weights, *needed)


def fragment_kernel(place, weights, anchor, moment, after, keep, send, state):
    del after
    height, width = keep.shape[1:]
    columns = pl.ds(pl.multiple_of(place[2] * width, width), width)
    core = lax.rem(place[3], 2)
    for pair in range(8):
        low = weights[2 * pair * height : (2 * pair + 1) * height, columns]
        high = weights[(2 * pair + 1) * height : (2 * pair + 2) * height, columns]
        keep[pair] = jnp.where(core == 0, low, high)
        send[pair] = jnp.where(core == 0, high, low)
    state[0] = anchor[:, columns]
    state[1] = moment[:, columns]


def fragment_columns(place, weights, anchor, moment, after):
    height, width = anchor.shape[0], weights.shape[1] // FRAG
    blocks = jax.ShapeDtypeStruct((8, height, width), F32)
    return pl.pallas_call(
        fragment_kernel,
        out_shape=[blocks, blocks, jax.ShapeDtypeStruct((2, height, width), F32)],
        in_specs=[scalars()] + whole(3) + [pl.BlockSpec(memory_space=pl.ANY)],
        out_specs=whole(3),
        compiler_params=params_of(),
        cost_estimate=COST,
        name="fragment_columns",
    )(place, weights, anchor, moment, after)


def forward_kernel(keep_left, keep_right, from_left, from_right, last_left, last_right):
    half = keep_left.shape[0]
    skip = from_left.shape[0] - 2 * half
    last_left[...] = (keep_left[...] + from_left[skip : skip + half].astype(F32)).astype(BF16)
    last_right[...] = (keep_right[...] + from_right[skip + half :].astype(F32)).astype(BF16)


def forward(keep_left, keep_right, from_left, from_right):
    return pl.pallas_call(
        forward_kernel,
        out_shape=[pltpu.HBM(keep_left.shape, BF16)] * 2,
        grid=(1,),
        in_specs=[pl.BlockSpec(a.shape, lambda i: (0, 0)) for a in (keep_left, keep_right, from_left, from_right)],
        out_specs=[pl.BlockSpec(keep_left.shape, lambda i: (0, 0))] * 2,
        compiler_params=params_of(),
        cost_estimate=COST,
        name="forward",
    )(keep_left, keep_right, from_left, from_right)


def outer_kernel(place, mine, other, theirs, anchor, moment, both, anchor_out, moment_out):
    height, width = anchor.shape[0], both.shape[2]
    zl = lax.rem(place[3] // 2, 2)
    columns = pl.ds(pl.multiple_of(place[2] * width, width), width)

    def update(index, old, old_moment):
        delta = old - (mine[index] + other[index]) / N_REP
        moment_new = OUTER_MOMENTUM * old_moment + delta
        new = old - OUTER_RATE * (delta + OUTER_MOMENTUM * moment_new)
        both[index] = new
        return new, moment_new

    new, moment_new = update(zl, anchor[:, columns], moment[:, columns])
    update(1 - zl, theirs[0], theirs[1])
    anchor_out[...] = anchor[...]
    moment_out[...] = moment[...]
    anchor_out[:, columns] = new
    moment_out[:, columns] = moment_new


def outer(place, mine, other, theirs, anchor, moment):
    shape = jax.ShapeDtypeStruct(anchor.shape, F32)
    return pl.pallas_call(
        outer_kernel,
        out_shape=[jax.ShapeDtypeStruct(mine.shape, F32), shape, shape],
        in_specs=[scalars()] + whole(5),
        out_specs=whole(3),
        compiler_params=params_of(),
        cost_estimate=COST,
        name="outer",
    )(place, mine, other, theirs, anchor, moment)


def values_sum_kernel(factor, own, one, two, three, out):
    total = own[...] + one[...].astype(F32) + two[...].astype(F32) + three[...].astype(F32)
    out[...] = (total * factor).astype(BF16)


def values_sum(factor, parts):
    shape = parts[0].shape
    return pl.pallas_call(
        functools.partial(values_sum_kernel, factor),
        grid=(1,),
        out_shape=jax.ShapeDtypeStruct(shape, BF16),
        in_specs=[pl.BlockSpec(shape, lambda i: (0, 0))] * RING,
        out_specs=pl.BlockSpec(shape, lambda i: (0, 0)),
        compiler_params=params_of(),
        cost_estimate=COST,
        name="values_sum",
    )(*parts)


def adam_kernel(place, rates, weights, first, second, *refs):
    own_0, left_0, right_0, own_1, left_1, right_1, last_left, last_right, near, far = refs[:10]
    out_weights, out_first, out_second = refs[10:]
    fragment, rep = place[2], place[3]
    x, core = rep // 4, lax.rem(rep, 2)
    rate, first_scale, second_scale, factor = rates[0], rates[1], rates[2], rates[3]
    part = pl.program_id(0)
    rows = weights.shape[0]
    skip = CHUNKS[0][1] // 2

    def step(total):
        gradient = total * factor
        first_new = FIRST_DECAY * first[...] + (1.0 - FIRST_DECAY) * gradient
        second_new = SECOND_DECAY * second[...] + (1.0 - SECOND_DECAY) * gradient * gradient
        out_first[...] = first_new
        out_second[...] = second_new
        update = (first_new * first_scale) / (jnp.sqrt(second_new * second_scale) + ADAM_EPSILON)
        out_weights[...] = weights[...] - rate * (update + WEIGHT_DECAY * weights[...])

    @pl.when(part == 0)
    def _():
        step(own_0[:rows] + right_0[:rows].astype(F32) + left_1[:rows].astype(F32))

    @pl.when(part == 1)
    def _():
        step(own_0[rows:] + left_0[rows:].astype(F32) + right_1[:rows].astype(F32))

    @pl.when(part == 2)
    def _():
        step(own_1[:rows] + right_1[skip : skip + rows].astype(F32) + last_left[...].astype(F32))

    @pl.when(part == 3)
    def _():
        step(own_1[rows:] + left_1[skip + rows :].astype(F32) + last_right[...].astype(F32))

    width = weights.shape[1] // FRAG
    height = near.shape[1]
    columns = pl.ds(pl.multiple_of(fragment * width, width), width)
    at = 2 * lax.rem(part // 2 + x // 2, 2) + 4 * lax.rem(part + x, 2)
    for block in range(4):
        index = at + block // 2
        base = jnp.where(core == block % 2, near[index], far[index])
        here = slice(block * height, (block + 1) * height)
        out_weights[here, columns] = base + (out_weights[here, columns] - weights[here, columns])


def adam(place, rates, weights, first, second, pieces, near, far):
    shape = jax.ShapeDtypeStruct(weights.shape, F32)
    rows = pl.BlockSpec((weights.shape[0] // 4, weights.shape[1]), lambda i: (i, 0))
    return pl.pallas_call(
        adam_kernel,
        grid=(4,),
        out_shape=[shape] * 3,
        in_specs=[scalars(), scalars(), rows, rows, rows]
        + [pl.BlockSpec(p.shape, lambda i: (0, 0)) for p in pieces]
        + [pl.BlockSpec(near.shape, lambda i: (0, 0, 0))] * 2,
        out_specs=[rows] * 3,
        compiler_params=params_of(),
        cost_estimate=COST,
        name="adam",
    )(place, rates, weights, first, second, *pieces, near, far)


def pick(array, index, axis):
    return lax.dynamic_index_in_dim(array, index, axis, keepdims=False)


def local(
    hidden,
    cotangent,
    norm_gain,
    params,
    adam_first,
    adam_second,
    outer_anchor,
    outer_momentum,
    fragment,
    inner_step,
):
    tokens = hidden[0]
    cot_local = cotangent[0]
    weights = params[0]
    factor = tokens.shape[1] ** (-0.5)
    shard = lax.axis_index("shard")
    rep = lax.axis_index("rep")
    place = jnp.stack([shard // RING, shard % RING, fragment, rep]).astype(jnp.int32)

    anchor_local, moment_local = outer_anchor[0, 0], outer_momentum[0, 0]
    gain = norm_gain.reshape(1, -1)

    packed, scale = first_pack(place, tokens, gain, cot_local)
    arrived = exchange_y(packed)

    weights_half = weights.astype(BF16)
    half = weights.shape[0] // 2
    before, after = shift_z(weights_half, 1), shift_z(weights_half, -1)
    far_top, far_bottom = shift_z(before[:half], 1), shift_z(after[half:], -1)
    ring_weights = [weights_half, before, far_top, far_bottom, after]

    keep, send, state = fragment_columns(place, weights, anchor_local, moment_local, scale)
    mine = jnp.concatenate([keep + swap_rep(send, 1), state])
    theirs = swap_rep(mine, 2)
    total = (mine[:8] + theirs[:8]).reshape(2, 2, 2, *keep.shape[1:])
    x_high, x_low = rep // 8, rep // 4 % 2
    total = pick(total, x_low, 1) + swap_rep(pick(total, 1 - x_low, 1), 4)
    other = swap_rep(pick(total, 1 - x_high, 0), 8)
    near, anchor_out, moment_out = outer(place, pick(total, x_high, 0), other, theirs[8:], anchor_local, moment_local)

    packed = later_pack(place, tokens, gain, scale, (near,))
    later = [packed[0]] + [shift_y(packed[k], k) for k in (1, 2, 3)]

    own_0, left, right, keep_left, keep_right = first_gradient(arrived, (before, after))
    left_0, right_0 = shift_z(left, -1), shift_z(right, 1)
    kept = (keep_left, keep_right, left_0, right_0)
    own_1, left, right, keep_left, keep_right = later_gradient(place, later, arrived, kept, ())
    near = jnp.concatenate([near, swap_rep(near, 8)])
    near = jnp.concatenate([near, swap_rep(near, 4)])
    far = swap_rep(near, 1)
    left_1, right_1 = shift_z(left, -1), shift_z(right, 1)
    last_left, last_right = forward(keep_left, keep_right, left_1, right_1)
    last_left, last_right = shift_z(last_left, -1), shift_z(last_right, 1)
    pieces = [own_0, left_0, right_0, own_1, left_1, right_1, last_left, last_right]

    partial = values_partial(place, arrived, later, ring_weights, (own_1,))
    value_rows = values_sum(factor, [partial[0]] + [shift_y(partial[k], -k) for k in (1, 2, 3)])

    clock = inner_step.astype(F32)
    rate = PEAK_RATE * 0.5 * (1.0 + jnp.cos(math.pi * clock / HORIZON_STEPS))
    first_scale = 1.0 / (1.0 - jnp.power(FIRST_DECAY, clock))
    second_scale = 1.0 / (1.0 - jnp.power(SECOND_DECAY, clock))
    rates = jnp.stack([rate, first_scale, second_scale, jnp.full((), factor, F32)])
    params_out, first_new, second_new = adam(
        place, rates, weights, adam_first[0], adam_second[0], pieces, near, far
    )
    return (
        value_rows[None],
        params_out[None],
        first_new[None],
        second_new[None],
        anchor_out[None, None],
        moment_out[None, None],
    )


def solution(mesh):
    in_specs = (
        P("rep", "shard", None),
        P("rep", "shard", None),
        P(),
        P("rep", "shard", None),
        P("rep", "shard", None),
        P("rep", "shard", None),
        P("shard", "rep", None, None),
        P("shard", "rep", None, None),
        P(),
        P(),
    )
    out_specs = (
        P("rep", "shard", None),
        P("rep", "shard", None),
        P("rep", "shard", None),
        P("rep", "shard", None),
        P("shard", "rep", None, None),
        P("shard", "rep", None, None),
    )
    return jax.shard_map(local, mesh=mesh, in_specs=in_specs, out_specs=out_specs, check_vma=False)
```

time: 363 us -> 131 us (0.36)
  waiting for transfers between devices: 271 us -> 23.4 us
  starting transfers between devices: 0.13 us -> 52.6 us
  blocking collectives: 40.5 us -> 0 us
  Pallas kernels: 0 us -> 38.6 us
  matrix products: 18.8 us -> 0 us
  between operations: 17.1 us -> 2.51 us
  other arithmetic: 9.98 us -> 3.01 us
  local copies, waits for them, and re-layouts: 4.48 us -> 9.79 us
    psum x1 -> x0, waiting for transfers between devices: 198 us -> none  [local(): params_total = lax.psum(own_frag, 'rep')]
    reduce_scatter x1 -> x0, waiting for transfers between devices: 73.1 us -> none  [local(): lax.psum_scatter(contract_tokens(feature_block, cot_local), 'shard', scat...]
    ppermute x0 -> x23, starting transfers between devices: none -> 47.8 us  [the longest x10 25.5 us: shift_z(): return lax.ppermute(array, 'shard', pairs)]
    all_gather x2 -> x0, blocking collectives: 40.5 us -> none  [the longest x1 22.4 us: local(): lax.all_gather(moment_frag, 'rep', axis=0, tiled=True)]
    pallas_call x0 -> x10, Pallas kernels: none -> 38.6 us  [the longest x1 5.91 us: values_partial(): pl.pallas_call(values_kernel, grid=(1,), out_shape=[pltpu.HBM(shape, F32...]
    ppermute x0 -> x23, waiting for transfers between devices: none -> 23.4 us  [the longest x10 12.7 us: shift_z(): return lax.ppermute(array, 'shard', pairs)]
    dot_general x2 -> x0, matrix products: 18.8 us -> none  [the longest x1 10.4 us: contract_tokens(): lax.dot_general(left, right, (((0,), (0,)), ((), ())), preferred_element_...]
    all_to_all x0 -> x1, starting transfers between devices: none -> 4.79 us  [exchange_y(): lax.all_to_all(array, 'shard', 0, 0, axis_index_groups=groups, tiled=True)]
  transfers between devices with their start and end apart: 3 -> 24, of which waited for: 2 -> 9; matrix products, arithmetic and copies ran while one was open for 7% -> 5% of each run, Pallas kernels for 0% -> 21%
where the time goes in v2:
time: 131 us; the launch traced here: 130 us
  starting transfers between devices  52.6 us (40%)
  Pallas kernels  38.6 us (29%)
  waiting for transfers between devices  23.4 us (18%)
  local copies, waits for them, and re-layouts  9.79 us (7%)
  other arithmetic  3.01 us (2%)
  between operations  2.51 us (2%)
    ppermute x10, starting transfers between devices, shift_z(): return lax.ppermute(array, 'shard', pairs)  25.5 us
    ppermute x10, waiting for transfers between devices, shift_z(): return lax.ppermute(array, 'shard', pairs)  12.7 us
    ppermute x6, starting transfers between devices, shift_y(): return lax.ppermute(array, 'shard', pairs)  12 us
    ppermute x7, starting transfers between devices, swap_rep(): return lax.ppermute(array, 'rep', [(r, r ^ bit) for r in range(16)])  10.3 us
    ppermute x7, waiting for transfers between devices, swap_rep(): return lax.ppermute(array, 'rep', [(r, r ^ bit) for r in range(16)])  8.46 us
    pallas_call x1, Pallas kernels, values_partial(): pl.pallas_call(values_kernel, grid=(1,), out_shape=[pltpu.HBM(shape, F32...  5.91 us
    pallas_call x1, Pallas kernels, first_pack(): pl.pallas_call(first_pack_kernel, out_shape=[pltpu.HBM((RING, tokens, tot...  5.81 us
    pallas_call x1, Pallas kernels, adam(): pl.pallas_call(adam_kernel, grid=(4,), out_shape=[shape] * 3, in_specs=[s...  5.67 us
  transfers between devices with their start and end apart: 24, of which 9 were waited for; matrix products, arithmetic and copies ran while one was open for 5% of the time, Pallas kernels for 21%

profile of v2, /device:TPU:2, one launch (start us, length us, event | category | flops | bytes accessed | tf_op | source)
XLA Modules:
  0.0 129.8 jit_solution(869349883052462477)
XLA Ops:
  1.9 5.8 %first_pack.1 = (bf16[4,256,1536]{2,1,0:T(8,128)(2,1)}, f32[256,1]{1,0:T(8,128)}) custom-call(s32[4]{0:T(128)} %pad_add_fusion.place, bf16[256,8192]{1,0:T(8,128)(2,1)} %bitcast.32, f32[1,8192]{1,0:T(1,128)} %bitcast.41, bf16[256,512]{1,0:T(8,128)(2,1)} %bitcast.48), custom_call_target="tpu_custom_call" | custom-call | flops 1 | bytes 1 | tf_op jit(solution)/shard_map/first_pack/pallas_call | solution.py:85
  7.7 4.8 %all-to-all-start = ((bf16[4,256,1536]{2,1,0:T(8,128)(2,1)}), bf16[4,256,1536]{2,1,0:T(8,128)(2,1)}, u32[]{:S(2)}, u32[]{:S(2)}) async-start(bf16[4,256,1536]{2,1,0:T(8,128)(2,1)} %get-tuple-element.37), calls=%async_computation | async-start | bytes 6291456 | tf_op jit(solution)/shard_map/all_to_all | solution.py:34
  19.8 4.5 %collective-permute-done.1 = f32[10,32,128]{2,1,0:T(8,128)S(1)} collective-permute-done((f32[10,32,128]{2,1,0:T(8,128)S(1)}, f32[10,32,128]{2,1,0:T(8,128)S(1)}, u32[]{:S(2)}, u32[]{:S(2)}) %collective-permute-start.1) | collective-permute-done | bytes 163872 | tf_op jit(solution)/shard_map/ppermute | solution.py:43
  24.4 2.2 %collective-permute-start.2 = (f32[2,2,32,128]{3,2,1,0:T(8,128)S(1)}, f32[2,2,32,128]{3,2,1,0:T(8,128)S(1)}, u32[]{:S(2)}, u32[]{:S(2)}) collective-permute-start(f32[2,2,32,128]{3,2,1,0:T(8,128)S(1)} %dynamic-slice_bitcast_fusion), channel_id=1, source_target_pairs={{0,64},{16,80},{32,96},{48,112},{64,0},{80,16},{96,32},{112,48},{1... | collective-permute-start | bytes 196616 | tf_op jit(solution)/shard_map/ppermute | solution.py:43
  28.4 2.9 %collective-permute-start.9 = (bf16[512,512]{1,0:T(8,128)(2,1)S(1)}, bf16[512,512]{1,0:T(8,128)(2,1)S(1)}, u32[]{:S(2)}, u32[]{:S(2)}) collective-permute-start(bf16[512,512]{1,0:T(8,128)(2,1)S(1)} %bitcast_convert_fusion.refs_4_), channel_id=1, source_target_pairs={{0,3},{1,0},{2,1},{3,2},{4,7},{5,4},{6,5},{7,6},{8,11},{9,8},{10,9... | collective-permute-start | bytes 1572872 | tf_op jit(solution)/shard_map/ppermute | solution.py:39
  32.0 2.4 %collective-permute-start.3 = (f32[2,32,128]{2,1,0:T(8,128)S(1)}, f32[2,32,128]{2,1,0:T(8,128)S(1)}, u32[]{:S(2)}, u32[]{:S(2)}) collective-permute-start(f32[2,32,128]{2,1,0:T(8,128)S(1)} %get-tuple-element.68), channel_id=1, source_target_pairs={{0,128},{16,144},{32,160},{48,176},{64,192},{80,208},{96,224},{112... | collective-permute-start | bytes 98312 | tf_op jit(solution)/shard_map/ppermute | solution.py:43
  35.1 2.4 %collective-permute-done.3.other = f32[2,32,128]{2,1,0:T(8,128)S(1)} collective-permute-done((f32[2,32,128]{2,1,0:T(8,128)S(1)}, f32[2,32,128]{2,1,0:T(8,128)S(1)}, u32[]{:S(2)}, u32[]{:S(2)}) %collective-permute-start.3) | collective-permute-done | bytes 32800 | tf_op jit(solution)/shard_map/ppermute | solution.py:43
  39.7 5.0 %later_pack.1 = (bf16[256,1024]{1,0:T(8,128)(2,1)}, bf16[256,1024]{1,0:T(8,128)(2,1)}, bf16[256,1024]{1,0:T(8,128)(2,1)}, bf16[256,1024]{1,0:T(8,128)(2,1)}) custom-call(s32[4]{0:T(128)} %pad_add_fusion.place, bf16[256,8192]{1,0:T(8,128)(2,1)} %bitcast.33, bf16[256,8192]{1,0:T(8,128)(2,1)} %bitcast.34, bf16[256,8192]{1,0:T(8,128)(2,1)} %bitcast.35, ...), custom_call_target="tpu_custom_call" | custom-call | flops 1 | bytes 1 | tf_op jit(solution)/shard_map/later_pack/pallas_call | solution.py:126
  46.8 2.7 %collective-permute-start.5 = (bf16[256,1024]{1,0:T(8,128)(2,1)}, bf16[256,1024]{1,0:T(8,128)(2,1)}, u32[]{:S(2)}, u32[]{:S(2)}) collective-permute-start(bf16[256,1024]{1,0:T(8,128)(2,1)} %get-tuple-element.45), channel_id=1, source_target_pairs={{0,8},{1,9},{2,10},{3,11},{4,12},{5,13},{6,14},{7,15},{8,0},{9,1},... | collective-permute-start | bytes 1572872 | tf_op jit(solution)/shard_map/ppermute | solution.py:48
  50.9 4.0 %collective-permute-done.9.refs_1_.refs_8_ = bf16[512,512]{1,0:T(8,128)(2,1)S(1)} collective-permute-done((bf16[512,512]{1,0:T(8,128)(2,1)S(1)}, bf16[512,512]{1,0:T(8,128)(2,1)S(1)}, u32[]{:S(2)}, u32[]{:S(2)}) %collective-permute-start.9) | collective-permute-done | bytes 524320 | tf_op jit(solution)/shard_map/ppermute | solution.py:39
  55.7 3.9 %first_gradient.1 = (f32[256,512]{1,0:T(8,128)}, bf16[256,512]{1,0:T(8,128)(2,1)}, bf16[256,512]{1,0:T(8,128)(2,1)}, f32[128,512]{1,0:T(8,128)}, f32[128,512]{1,0:T(8,128)}) custom-call(bf16[4,256,1536]{2,1,0:T(8,128)(2,1)} %all-to-all-done.normed.cot.refs_4_.arrived, bf16[4,256,1536]{2,1,0:T(8,128)(2,1)} %all-to-all-done.normed.cot.refs_4_.arrived, ...), custom_call_target="tpu_custom_call" | custom-call | flops 1 | bytes 1 | tf_op jit(solution)/shard_map/first_gradient/pallas_call | solution.py:176
  59.7 2.8 %collective-permute-start.11 = (bf16[256,512]{1,0:T(8,128)(2,1)}, bf16[256,512]{1,0:T(8,128)(2,1)S(1)}, u32[]{:S(2)}, u32[]{:S(2)}) collective-permute-start(bf16[256,512]{1,0:T(8,128)(2,1)} %get-tuple-element.49), channel_id=1, source_target_pairs={{0,3},{1,0},{2,1},{3,2},{4,7},{5,4},{6,5},{7,6},{8,11},{9,8},{10,9... | collective-permute-start | bytes 786440 | tf_op jit(solution)/shard_map/ppermute | solution.py:39
  66.7 4.1 %collective-permute-start.8 = (bf16[256,512]{1,0:T(8,128)(2,1)}, bf16[256,512]{1,0:T(8,128)(2,1)S(1)}, u32[]{:S(2)}, u32[]{:S(2)}) collective-permute-start(bf16[256,512]{1,0:T(8,128)(2,1)} %slice.18), channel_id=1, source_target_pairs={{0,1},{1,2},{2,3},{3,0},{4,5},{5,6},{6,7},{7,4},{8,9},{9,10},{10,1... | collective-permute-start | bytes 786440 | tf_op jit(solution)/shard_map/ppermute | solution.py:39
  70.8 2.2 %collective-permute-done.5.refs_2_ = bf16[256,1024]{1,0:T(8,128)(2,1)} collective-permute-done((bf16[256,1024]{1,0:T(8,128)(2,1)}, bf16[256,1024]{1,0:T(8,128)(2,1)}, u32[]{:S(2)}, u32[]{:S(2)}) %collective-permute-start.5) | collective-permute-done | bytes 524320 | tf_op jit(solution)/shard_map/ppermute | solution.py:48
  72.9 6.3 %collective-permute-start.10 = (bf16[256,512]{1,0:T(8,128)(2,1)}, bf16[256,512]{1,0:T(8,128)(2,1)S(1)}, u32[]{:S(2)}, u32[]{:S(2)}) collective-permute-start(bf16[256,512]{1,0:T(8,128)(2,1)} %slice.19), channel_id=1, source_target_pairs={{0,3},{1,0},{2,1},{3,2},{4,7},{5,4},{6,5},{7,6},{8,11},{9,8},{10,9... | collective-permute-start | bytes 786440 | tf_op jit(solution)/shard_map/ppermute | solution.py:39
  79.2 2.1 %collective-permute-start.20 = (f32[2,32,128]{2,1,0:T(8,128)S(1)}, f32[2,32,128]{2,1,0:T(8,128)S(1)}, u32[]{:S(2)}, u32[]{:S(2)}) collective-permute-start(f32[2,32,128]{2,1,0:T(8,128)S(1)} %copy-done.8), channel_id=1, source_target_pairs={{0,128},{16,144},{32,160},{48,176},{64,192},{80,208},{96,224},{112... | collective-permute-start | bytes 98312 | tf_op jit(solution)/shard_map/ppermute | solution.py:43
  82.2 4.5 %later_gradient.1 = (f32[256,512]{1,0:T(8,128)}, bf16[384,512]{1,0:T(8,128)(2,1)}, bf16[384,512]{1,0:T(8,128)(2,1)}, f32[128,512]{1,0:T(8,128)}, f32[128,512]{1,0:T(8,128)}) custom-call(s32[4]{0:T(128)} %pad_add_fusion.place, bf16[256,1024]{1,0:T(8,128)(2,1)} %get-tuple-element.43.refs_0_, bf16[256,1024]{1,0:T(8,128)(2,1)} %collective-permute-done.4.refs_1_, ...), custom_call_target="tpu_custom_call" | custom-call | flops 1 | bytes 1 | tf_op jit(solution)/shard_map/later_gradient/pallas_call | solution.py:211
  91.9 5.9 %values_partial.1 = (f32[256,512]{1,0:T(8,128)}, bf16[256,512]{1,0:T(8,128)(2,1)}, bf16[256,512]{1,0:T(8,128)(2,1)}, bf16[256,512]{1,0:T(8,128)(2,1)}) custom-call(s32[4]{0:T(128)} %pad_add_fusion.place, bf16[4,256,1536]{2,1,0:T(8,128)(2,1)} %all-to-all-done.normed.cot.refs_4_.arrived, bf16[256,1024]{1,0:T(8,128)(2,1)} %get-tuple-element.43.refs_0_, ...), custom_call_target="tpu_custom_call" | custom-call | flops 1 | bytes 1 | tf_op jit(solution)/shard_map/values_partial/pallas_call | solution.py:254
  97.8 3.4 %collective-permute-start.13 = (bf16[256,512]{1,0:T(8,128)(2,1)}, bf16[256,512]{1,0:T(8,128)(2,1)S(1)}, u32[]{:S(2)}, u32[]{:S(2)}) collective-permute-start(bf16[256,512]{1,0:T(8,128)(2,1)} %get-tuple-element.53), channel_id=1, source_target_pairs={{0,12},{1,13},{2,14},{3,15},{4,0},{5,1},{6,2},{7,3},{8,4},{9,5},{1... | collective-permute-start | bytes 786440 | tf_op jit(solution)/shard_map/ppermute | solution.py:48
  103.7 3.1 %collective-permute-done.16.from_left.refs_4_ = bf16[384,512]{1,0:T(8,128)(2,1)S(1)} collective-permute-done((bf16[384,512]{1,0:T(8,128)(2,1)}, bf16[384,512]{1,0:T(8,128)(2,1)S(1)}, u32[]{:S(2)}, u32[]{:S(2)}) %collective-permute-start.16) | collective-permute-done | bytes 393248 | tf_op jit(solution)/shard_map/ppermute | solution.py:39
  110.3 3.8 %collective-permute-start.18 = (bf16[128,512]{1,0:T(8,128)(2,1)}, bf16[128,512]{1,0:T(8,128)(2,1)S(1)}, u32[]{:S(2)}, u32[]{:S(2)}) collective-permute-start(bf16[128,512]{1,0:T(8,128)(2,1)} %get-tuple-element.61), channel_id=1, source_target_pairs={{0,3},{1,0},{2,1},{3,2},{4,7},{5,4},{6,5},{7,6},{8,11},{9,8},{10,9... | collective-permute-start | bytes 393224 | tf_op jit(solution)/shard_map/ppermute | solution.py:39
  116.4 2.1 %values_sum.1 = bf16[256,512]{1,0:T(8,128)(2,1)} custom-call(f32[256,512]{1,0:T(8,128)} %get-tuple-element.52.own, bf16[256,512]{1,0:T(8,128)(2,1)} %copy-done.11, bf16[256,512]{1,0:T(8,128)(2,1)} %copy-done.12, bf16[256,512]{1,0:T(8,128)(2,1)} %copy-done.13), custom_call_target="tpu_custom_call" | custom-call | flops 1 | bytes 1 | tf_op jit(solution)/shard_map/values_sum/pallas_call | solution.py:356
  120.4 2.9 %collective-permute-done.19.refs_7_ = bf16[128,512]{1,0:T(8,128)(2,1)S(1)} collective-permute-done((bf16[128,512]{1,0:T(8,128)(2,1)}, bf16[128,512]{1,0:T(8,128)(2,1)S(1)}, u32[]{:S(2)}, u32[]{:S(2)}) %collective-permute-start.19) | collective-permute-done | bytes 131104 | tf_op jit(solution)/shard_map/ppermute | solution.py:39
  124.0 5.7 %adam.1 = (f32[512,512]{1,0:T(8,128)}, f32[512,512]{1,0:T(8,128)}, f32[512,512]{1,0:T(8,128)}) custom-call(s32[4]{0:T(128)} %pad_add_fusion.place, f32[4]{0:T(128)} %pad_maximum_fusion.2.rates, f32[512,512]{1,0:T(8,128)} %bitcast.38, f32[512,512]{1,0:T(8,128)} %bitcast.39, f32[512,512]{1,0:T(8,128)} %bitcast.40, f32[256,512]{1,0:T(8,128)} %get-tuple-element.56.refs_0_, ...), custom_call_target="tpu_custom_call" | custom-call | flops 1 | bytes 1 | tf_op jit(solution)/shard_map/adam/pallas_call | solution.py:417
  (88 shorter events, 37.8 us)
Async XLA Ops:
  7.7 47.2 %all-to-all-start = ((bf16[4,256,1536]{2,1,0:T(8,128)(2,1)}), bf16[4,256,1536]{2,1,0:T(8,128)(2,1)}, u32[]{:S(2)}, u32[]{:S(2)}) async-start(bf16[4,256,1536]{2,1,0:T(8,128)(2,1)} %get-tuple-element.37), calls=%async_computation | async-start | bytes 6291456 | tf_op jit(solution)/shard_map/all_to_all | solution.py:34
  14.6 1.6 %collective-permute-start = (f32[8,32,128]{2,1,0:T(8,128)}, f32[8,32,128]{2,1,0:T(8,128)S(1)}, u32[]{:S(2)}, u32[]{:S(2)}) collective-permute-start(f32[8,32,128]{2,1,0:T(8,128)} %get-tuple-element.40), channel_id=1, source_target_pairs={{0,16},{16,0},{32,48},{48,32},{64,80},{80,64},{96,112},{112,96},{1... | collective-permute-start | bytes 393224 | tf_op jit(solution)/shard_map/ppermute | solution.py:43
  17.8 6.5 %collective-permute-start.1 = (f32[10,32,128]{2,1,0:T(8,128)S(1)}, f32[10,32,128]{2,1,0:T(8,128)S(1)}, u32[]{:S(2)}, u32[]{:S(2)}) collective-permute-start(f32[10,32,128]{2,1,0:T(8,128)S(1)} %pad_maximum_fusion), channel_id=1, source_target_pairs={{0,32},{16,48},{32,0},{48,16},{64,96},{80,112},{96,64},{112,80},{1... | collective-permute-start | bytes 491528 | tf_op jit(solution)/shard_map/ppermute | solution.py:43
  24.4 7.0 %collective-permute-start.2 = (f32[2,2,32,128]{3,2,1,0:T(8,128)S(1)}, f32[2,2,32,128]{3,2,1,0:T(8,128)S(1)}, u32[]{:S(2)}, u32[]{:S(2)}) collective-permute-start(f32[2,2,32,128]{3,2,1,0:T(8,128)S(1)} %dynamic-slice_bitcast_fusion), channel_id=1, source_target_pairs={{0,64},{16,80},{32,96},{48,112},{64,0},{80,16},{96,32},{112,48},{1... | collective-permute-start | bytes 196616 | tf_op jit(solution)/shard_map/ppermute | solution.py:43
  26.6 24.3 %collective-permute-start.7 = (bf16[512,512]{1,0:T(8,128)(2,1)S(1)}, bf16[512,512]{1,0:T(8,128)(2,1)S(1)}, u32[]{:S(2)}, u32[]{:S(2)}) collective-permute-start(bf16[512,512]{1,0:T(8,128)(2,1)S(1)} %bitcast_convert_fusion.refs_4_), channel_id=1, source_target_pairs={{0,1},{1,2},{2,3},{3,0},{4,5},{5,6},{6,7},{7,4},{8,9},{9,10},{10,1... | collective-permute-start | bytes 1572872 | tf_op jit(solution)/shard_map/ppermute | solution.py:39
  28.4 26.5 %collective-permute-start.9 = (bf16[512,512]{1,0:T(8,128)(2,1)S(1)}, bf16[512,512]{1,0:T(8,128)(2,1)S(1)}, u32[]{:S(2)}, u32[]{:S(2)}) collective-permute-start(bf16[512,512]{1,0:T(8,128)(2,1)S(1)} %bitcast_convert_fusion.refs_4_), channel_id=1, source_target_pairs={{0,3},{1,0},{2,1},{3,2},{4,7},{5,4},{6,5},{7,6},{8,11},{9,8},{10,9... | collective-permute-start | bytes 1572872 | tf_op jit(solution)/shard_map/ppermute | solution.py:39
  32.0 5.4 %collective-permute-start.3 = (f32[2,32,128]{2,1,0:T(8,128)S(1)}, f32[2,32,128]{2,1,0:T(8,128)S(1)}, u32[]{:S(2)}, u32[]{:S(2)}) collective-permute-start(f32[2,32,128]{2,1,0:T(8,128)S(1)} %get-tuple-element.68), channel_id=1, source_target_pairs={{0,128},{16,144},{32,160},{48,176},{64,192},{80,208},{96,224},{112... | collective-permute-start | bytes 98312 | tf_op jit(solution)/shard_map/ppermute | solution.py:43
  44.7 21.9 %collective-permute-start.4 = (bf16[256,1024]{1,0:T(8,128)(2,1)}, bf16[256,1024]{1,0:T(8,128)(2,1)}, u32[]{:S(2)}, u32[]{:S(2)}) collective-permute-start(bf16[256,1024]{1,0:T(8,128)(2,1)} %get-tuple-element.44), channel_id=1, source_target_pairs={{0,4},{1,5},{2,6},{3,7},{4,8},{5,9},{6,10},{7,11},{8,12},{9,13},{1... | collective-permute-start | bytes 1572872 | tf_op jit(solution)/shard_map/ppermute | solution.py:48
  46.8 26.2 %collective-permute-start.5 = (bf16[256,1024]{1,0:T(8,128)(2,1)}, bf16[256,1024]{1,0:T(8,128)(2,1)}, u32[]{:S(2)}, u32[]{:S(2)}) collective-permute-start(bf16[256,1024]{1,0:T(8,128)(2,1)} %get-tuple-element.45), channel_id=1, source_target_pairs={{0,8},{1,9},{2,10},{3,11},{4,12},{5,13},{6,14},{7,15},{8,0},{9,1},... | collective-permute-start | bytes 1572872 | tf_op jit(solution)/shard_map/ppermute | solution.py:48
  49.4 29.8 %collective-permute-start.6 = (bf16[256,1024]{1,0:T(8,128)(2,1)}, bf16[256,1024]{1,0:T(8,128)(2,1)}, u32[]{:S(2)}, u32[]{:S(2)}) collective-permute-start(bf16[256,1024]{1,0:T(8,128)(2,1)} %get-tuple-element.46), channel_id=1, source_target_pairs={{0,12},{1,13},{2,14},{3,15},{4,0},{5,1},{6,2},{7,3},{8,4},{9,5},{1... | collective-permute-start | bytes 1572872 | tf_op jit(solution)/shard_map/ppermute | solution.py:48
  59.7 21.7 %collective-permute-start.11 = (bf16[256,512]{1,0:T(8,128)(2,1)}, bf16[256,512]{1,0:T(8,128)(2,1)S(1)}, u32[]{:S(2)}, u32[]{:S(2)}) collective-permute-start(bf16[256,512]{1,0:T(8,128)(2,1)} %get-tuple-element.49), channel_id=1, source_target_pairs={{0,3},{1,0},{2,1},{3,2},{4,7},{5,4},{6,5},{7,6},{8,11},{9,8},{10,9... | collective-permute-start | bytes 786440 | tf_op jit(solution)/shard_map/ppermute | solution.py:39
  62.4 19.0 %collective-permute-start.12 = (bf16[256,512]{1,0:T(8,128)(2,1)}, bf16[256,512]{1,0:T(8,128)(2,1)S(1)}, u32[]{:S(2)}, u32[]{:S(2)}) collective-permute-start(bf16[256,512]{1,0:T(8,128)(2,1)} %get-tuple-element.50), channel_id=1, source_target_pairs={{0,1},{1,2},{2,3},{3,0},{4,5},{5,6},{6,7},{7,4},{8,9},{9,10},{10,1... | collective-permute-start | bytes 786440 | tf_op jit(solution)/shard_map/ppermute | solution.py:39
  66.7 24.5 %collective-permute-start.8 = (bf16[256,512]{1,0:T(8,128)(2,1)}, bf16[256,512]{1,0:T(8,128)(2,1)S(1)}, u32[]{:S(2)}, u32[]{:S(2)}) collective-permute-start(bf16[256,512]{1,0:T(8,128)(2,1)} %slice.18), channel_id=1, source_target_pairs={{0,1},{1,2},{2,3},{3,0},{4,5},{5,6},{6,7},{7,4},{8,9},{9,10},{10,1... | collective-permute-start | bytes 786440 | tf_op jit(solution)/shard_map/ppermute | solution.py:39
  72.9 18.2 %collective-permute-start.10 = (bf16[256,512]{1,0:T(8,128)(2,1)}, bf16[256,512]{1,0:T(8,128)(2,1)S(1)}, u32[]{:S(2)}, u32[]{:S(2)}) collective-permute-start(bf16[256,512]{1,0:T(8,128)(2,1)} %slice.19), channel_id=1, source_target_pairs={{0,3},{1,0},{2,1},{3,2},{4,7},{5,4},{6,5},{7,6},{8,11},{9,8},{10,9... | collective-permute-start | bytes 786440 | tf_op jit(solution)/shard_map/ppermute | solution.py:39
  79.2 10.4 %collective-permute-start.20 = (f32[2,32,128]{2,1,0:T(8,128)S(1)}, f32[2,32,128]{2,1,0:T(8,128)S(1)}, u32[]{:S(2)}, u32[]{:S(2)}) collective-permute-start(f32[2,32,128]{2,1,0:T(8,128)S(1)} %copy-done.8), channel_id=1, source_target_pairs={{0,128},{16,144},{32,160},{48,176},{64,192},{80,208},{96,224},{112... | collective-permute-start | bytes 98312 | tf_op jit(solution)/shard_map/ppermute | solution.py:43
  86.7 20.1 %collective-permute-start.16 = (bf16[384,512]{1,0:T(8,128)(2,1)}, bf16[384,512]{1,0:T(8,128)(2,1)S(1)}, u32[]{:S(2)}, u32[]{:S(2)}) collective-permute-start(bf16[384,512]{1,0:T(8,128)(2,1)} %get-tuple-element.57), channel_id=1, source_target_pairs={{0,3},{1,0},{2,1},{3,2},{4,7},{5,4},{6,5},{7,6},{8,11},{9,8},{10,9... | collective-permute-start | bytes 1179656 | tf_op jit(solution)/shard_map/ppermute | solution.py:39
  88.1 19.4 %collective-permute-start.17 = (bf16[384,512]{1,0:T(8,128)(2,1)}, bf16[384,512]{1,0:T(8,128)(2,1)S(1)}, u32[]{:S(2)}, u32[]{:S(2)}) collective-permute-start(bf16[384,512]{1,0:T(8,128)(2,1)} %get-tuple-element.58), channel_id=1, source_target_pairs={{0,1},{1,2},{2,3},{3,0},{4,5},{5,6},{6,7},{7,4},{8,9},{9,10},{10,1... | collective-permute-start | bytes 1179656 | tf_op jit(solution)/shard_map/ppermute | solution.py:39
  89.6 12.7 %collective-permute-start.21 = (f32[4,32,128]{2,1,0:T(8,128)S(1)}, f32[4,32,128]{2,1,0:T(8,128)S(1)}, u32[]{:S(2)}, u32[]{:S(2)}) collective-permute-start(f32[4,32,128]{2,1,0:T(8,128)S(1)} %pad_maximum_fusion.1), channel_id=1, source_target_pairs={{0,64},{16,80},{32,96},{48,112},{64,0},{80,16},{96,32},{112,48},{1... | collective-permute-start | bytes 196616 | tf_op jit(solution)/shard_map/ppermute | solution.py:43
  97.8 16.3 %collective-permute-start.13 = (bf16[256,512]{1,0:T(8,128)(2,1)}, bf16[256,512]{1,0:T(8,128)(2,1)S(1)}, u32[]{:S(2)}, u32[]{:S(2)}) collective-permute-start(bf16[256,512]{1,0:T(8,128)(2,1)} %get-tuple-element.53), channel_id=1, source_target_pairs={{0,12},{1,13},{2,14},{3,15},{4,0},{5,1},{6,2},{7,3},{8,4},{9,5},{1... | collective-permute-start | bytes 786440 | tf_op jit(solution)/shard_map/ppermute | solution.py:48
  101.2 14.4 %collective-permute-start.14 = (bf16[256,512]{1,0:T(8,128)(2,1)}, bf16[256,512]{1,0:T(8,128)(2,1)S(1)}, u32[]{:S(2)}, u32[]{:S(2)}) collective-permute-start(bf16[256,512]{1,0:T(8,128)(2,1)} %get-tuple-element.54), channel_id=1, source_target_pairs={{0,8},{1,9},{2,10},{3,11},{4,12},{5,13},{6,14},{7,15},{8,0},{9,1},... | collective-permute-start | bytes 786440 | tf_op jit(solution)/shard_map/ppermute | solution.py:48
  102.3 13.3 %collective-permute-start.15 = (bf16[256,512]{1,0:T(8,128)(2,1)}, bf16[256,512]{1,0:T(8,128)(2,1)S(1)}, u32[]{:S(2)}, u32[]{:S(2)}) collective-permute-start(bf16[256,512]{1,0:T(8,128)(2,1)} %get-tuple-element.55), channel_id=1, source_target_pairs={{0,4},{1,5},{2,6},{3,7},{4,8},{5,9},{6,10},{7,11},{8,12},{9,13},{1... | collective-permute-start | bytes 786440 | tf_op jit(solution)/shard_map/ppermute | solution.py:48
  106.8 11.8 %collective-permute-start.22 = (f32[8,32,128]{2,1,0:T(8,128)S(1)}, f32[8,32,128]{2,1,0:T(8,128)S(1)}, u32[]{:S(2)}, u32[]{:S(2)}) collective-permute-start(f32[8,32,128]{2,1,0:T(8,128)S(1)} %constant_dynamic-update-slice_fusion.refs_8_), channel_id=1, source_target_pairs={{0,16},{16,0},{32,48},{48,32},{64,80},{80,64},{96,112},{112,96},{1... | collective-permute-start | bytes 393224 | tf_op jit(solution)/shard_map/ppermute | solution.py:43
  110.3 10.1 %collective-permute-start.18 = (bf16[128,512]{1,0:T(8,128)(2,1)}, bf16[128,512]{1,0:T(8,128)(2,1)S(1)}, u32[]{:S(2)}, u32[]{:S(2)}) collective-permute-start(bf16[128,512]{1,0:T(8,128)(2,1)} %get-tuple-element.61), channel_id=1, source_target_pairs={{0,3},{1,0},{2,1},{3,2},{4,7},{5,4},{6,5},{7,6},{8,11},{9,8},{10,9... | collective-permute-start | bytes 393224 | tf_op jit(solution)/shard_map/ppermute | solution.py:39
  114.1 9.2 %collective-permute-start.19 = (bf16[128,512]{1,0:T(8,128)(2,1)}, bf16[128,512]{1,0:T(8,128)(2,1)S(1)}, u32[]{:S(2)}, u32[]{:S(2)}) collective-permute-start(bf16[128,512]{1,0:T(8,128)(2,1)} %get-tuple-element.62), channel_id=1, source_target_pairs={{0,1},{1,2},{2,3},{3,0},{4,5},{5,6},{6,7},{7,4},{8,9},{9,10},{10,1... | collective-permute-start | bytes 393224 | tf_op jit(solution)/shard_map/ppermute | solution.py:39
  (19 other events, 107.8 us)

commit v3 on v2

--- a/solution.py
+++ b/solution.py
@@ -141,6 +141,29 @@
     )(place, *[hidden] * RING, *[gain] * RING, scale, *after)
 
 
+def halves_kernel(before, after, *refs):
+    top, bottom = refs[-2:]
+    half = top.shape[0]
+    top[...] = before[:half]
+    bottom[...] = after[half:]
+
+
+def halves(before, after, needed):
+    rows, columns = before.shape
+    whole_block = pl.BlockSpec((rows, columns), lambda i: (0, 0))
+    half_block = pl.BlockSpec((rows // 2, columns), lambda i: (0, 0))
+    return pl.pallas_call(
+        halves_kernel,
+        grid=(1,),
+        out_shape=[pltpu.HBM((rows // 2, columns), BF16)] * 2,
+        in_specs=[whole_block] * 2 + [pl.BlockSpec(memory_space=pl.ANY)] * len(needed),
+        out_specs=[half_block] * 2,
+        compiler_params=params_of(),
+        cost_estimate=COST,
+        name="halves",
+    )(before, after, *needed)
+
+
 def gradient_block(normed, cot, kz, height):
     rows = jnp.concatenate([n[:, kz * height : (kz + 1) * height] for n in normed], axis=0)
     return lax.dot_general(rows, cot, (((0,), (0,)), ((), ())), preferred_element_type=F32)
@@ -191,21 +214,20 @@
 
 def later_gradient_kernel(place, *refs):
     normed, cot = refs[:RING], refs[RING]
-    keep_left, keep_right, from_left, from_right = refs[RING + 1 : RING + 5]
     own, left, right, next_left, next_right = refs[-5:]
-    half = keep_left.shape[0]
-    left[:half] = (keep_left[...] + from_left[:half].astype(F32)).astype(BF16)
-    right[:half] = (keep_right[...] + from_right[half:].astype(F32)).astype(BF16)
+    first = CHUNKS[0][1] // 2
     cot_all = jnp.concatenate([cot[lax.rem(place[0] + RING - k, RING)] for k in range(RING)], axis=0)
-    gradient_blocks(normed, cot_all, own, left.at[half:], right.at[half:], next_left, next_right)
-
-
-def later_gradient(place, normed, arrived, kept, after):
+    for out in (left, right):
+        out[:first] = jnp.zeros_like(out[:first])
+    gradient_blocks(normed, cot_all, own, left.at[first:], right.at[first:], next_left, next_right)
+
+
+def later_gradient(place, normed, arrived):
     tokens = arrived.shape[1]
     height = CHUNKS[1][1]
-    columns = kept[0].shape[1]
+    columns = arrived.shape[2] - RING * CHUNKS[0][1]
     full, part = (height, columns), (height // 2, columns)
-    sent = (height + kept[0].shape[0], columns)
+    sent = (height + CHUNKS[0][1] // 2, columns)
     shapes = [(full, F32), (sent, BF16), (sent, BF16), (part, F32), (part, F32)]
     cot_at = RING * CHUNKS[0][1] // columns
     return pl.pallas_call(
@@ -214,14 +236,36 @@
         out_shape=[pltpu.HBM(*s) for s in shapes],
         in_specs=[scalars()]
         + [pl.BlockSpec((tokens, RING * height), lambda i: (0, 0))] * RING
-        + [pl.BlockSpec((RING, tokens, columns), lambda i: (0, 0, cot_at))]
-        + [pl.BlockSpec(k.shape, lambda i: (0, 0)) for k in kept]
-        + [pl.BlockSpec(memory_space=pl.ANY)] * len(after),
+        + [pl.BlockSpec((RING, tokens, columns), lambda i: (0, 0, cot_at))],
         out_specs=[pl.BlockSpec(s[0], lambda i: (0, 0)) for s in shapes],
         compiler_params=params_of(),
         cost_estimate=COST,
         name="later_gradient",
-    )(place, *normed, arrived, *kept, *after)
+    )(place, *normed, arrived)
+
+
+def join_kernel(keep_left, keep_right, from_left, from_right, *refs):
+    left, right = refs[-2:]
+    left[...] = (keep_left[...] + from_left[...].astype(F32)).astype(BF16)
+    right[...] = (keep_right[...] + from_right[...].astype(F32)).astype(BF16)
+
+
+def join(keep_left, keep_right, from_left, from_right, left, right):
+    rows, columns = keep_left.shape
+    top = pl.BlockSpec((rows, columns), lambda i: (0, 0))
+    bottom = pl.BlockSpec((rows, columns), lambda i: (1, 0))
+    anywhere = pl.BlockSpec(memory_space=pl.ANY)
+    return pl.pallas_call(
+        join_kernel,
+        grid=(1,),
+        out_shape=[pltpu.HBM(left.shape, BF16)] * 2,
+        in_specs=[top, top, top, bottom, anywhere, anywhere],
+        out_specs=[top, top],
+        input_output_aliases={4: 0, 5: 1},
+        compiler_params=params_of(),
+        cost_estimate=COST,
+        name="join",
+    )(keep_left, keep_right, from_left, from_right, left, right)
 
 
 def chunk_weights(chunk, own, before, far_top, far_bottom, after):
@@ -294,19 +338,25 @@
 
 
 def forward_kernel(keep_left, keep_right, from_left, from_right, last_left, last_right):
-    half = keep_left.shape[0]
-    skip = from_left.shape[0] - 2 * half
-    last_left[...] = (keep_left[...] + from_left[skip : skip + half].astype(F32)).astype(BF16)
-    last_right[...] = (keep_right[...] + from_right[skip + half :].astype(F32)).astype(BF16)
+    last_left[...] = (keep_left[...] + from_left[...].astype(F32)).astype(BF16)
+    last_right[...] = (keep_right[...] + from_right[...].astype(F32)).astype(BF16)
 
 
 def forward(keep_left, keep_right, from_left, from_right):
+    rows, columns = keep_left.shape
+    skip = CHUNKS[0][1] // 2 // rows
+    first = pl.BlockSpec((rows, columns), lambda i: (0, 0))
     return pl.pallas_call(
         forward_kernel,
+        grid=(1,),
         out_shape=[pltpu.HBM(keep_left.shape, BF16)] * 2,
-        grid=(1,),
-        in_specs=[pl.BlockSpec(a.shape, lambda i: (0, 0)) for a in (keep_left, keep_right, from_left, from_right)],
-        out_specs=[pl.BlockSpec(keep_left.shape, lambda i: (0, 0))] * 2,
+        in_specs=[
+            first,
+            first,
+            pl.BlockSpec((rows, columns), lambda i: (skip, 0)),
+            pl.BlockSpec((rows, columns), lambda i: (skip + 1, 0)),
+        ],
+        out_specs=[first] * 2,
         compiler_params=params_of(),
         cost_estimate=COST,
         name="forward",
@@ -365,15 +415,15 @@
     )(*parts)
 
 
-def adam_kernel(place, rates, weights, first, second, *refs):
-    own_0, left_0, right_0, own_1, left_1, right_1, last_left, last_right, near, far = refs[:10]
-    out_weights, out_first, out_second = refs[10:]
+def adam_kernel(chunk, place, rates, weights, first, second, own, left, right, last_left, last_right, near, far, *refs):
+    out_weights, out_first, out_second = refs[-3:]
     fragment, rep = place[2], place[3]
     x, core = rep // 4, lax.rem(rep, 2)
     rate, first_scale, second_scale, factor = rates[0], rates[1], rates[2], rates[3]
-    part = pl.program_id(0)
+    step_of = pl.program_id(0)
+    part = 2 * chunk + step_of
     rows = weights.shape[0]
-    skip = CHUNKS[0][1] // 2
+    skip = left.shape[0] - 2 * rows
 
     def step(total):
         gradient = total * factor
@@ -384,21 +434,13 @@
         update = (first_new * first_scale) / (jnp.sqrt(second_new * second_scale) + ADAM_EPSILON)
         out_weights[...] = weights[...] - rate * (update + WEIGHT_DECAY * weights[...])
 
-    @pl.when(part == 0)
+    @pl.when(step_of == 0)
     def _():
-        step(own_0[:rows] + right_0[:rows].astype(F32) + left_1[:rows].astype(F32))
-
-    @pl.when(part == 1)
+        step(own[:rows] + right[skip : skip + rows].astype(F32) + last_left[:rows].astype(F32))
+
+    @pl.when(step_of == 1)
     def _():
-        step(own_0[rows:] + left_0[rows:].astype(F32) + right_1[:rows].astype(F32))
-
-    @pl.when(part == 2)
-    def _():
-        step(own_1[:rows] + right_1[skip : skip + rows].astype(F32) + last_left[...].astype(F32))
-
-    @pl.when(part == 3)
-    def _():
-        step(own_1[rows:] + left_1[skip + rows :].astype(F32) + last_right[...].astype(F32))
+        step(own[rows:] + left[skip + rows :].astype(F32) + last_right[:rows].astype(F32))
 
     width = weights.shape[1] // FRAG
     height = near.shape[1]
@@ -411,21 +453,24 @@
         out_weights[here, columns] = base + (out_weights[here, columns] - weights[here, columns])
 
 
-def adam(place, rates, weights, first, second, pieces, near, far):
+def adam(chunk, place, rates, weights, first, second, pieces, near, far, begun):
     shape = jax.ShapeDtypeStruct(weights.shape, F32)
-    rows = pl.BlockSpec((weights.shape[0] // 4, weights.shape[1]), lambda i: (i, 0))
-    return pl.pallas_call(
-        adam_kernel,
-        grid=(4,),
+    rows = pl.BlockSpec((weights.shape[0] // 4, weights.shape[1]), lambda i: (2 * chunk + i, 0))
+    operands = (place, rates, weights, first, second, *pieces, near, far)
+    return pl.pallas_call(
+        functools.partial(adam_kernel, chunk),
+        grid=(2,),
         out_shape=[shape] * 3,
         in_specs=[scalars(), scalars(), rows, rows, rows]
         + [pl.BlockSpec(p.shape, lambda i: (0, 0)) for p in pieces]
-        + [pl.BlockSpec(near.shape, lambda i: (0, 0, 0))] * 2,
+        + [pl.BlockSpec(near.shape, lambda i: (0, 0, 0))] * 2
+        + [pl.BlockSpec(memory_space=pl.ANY)] * len(begun),
         out_specs=[rows] * 3,
+        input_output_aliases={len(operands) + i: i for i in range(len(begun))},
         compiler_params=params_of(),
         cost_estimate=COST,
         name="adam",
-    )(place, rates, weights, first, second, *pieces, near, far)
+    )(*operands, *begun)
 
 
 def pick(array, index, axis):
@@ -459,9 +504,9 @@
     arrived = exchange_y(packed)
 
     weights_half = weights.astype(BF16)
-    half = weights.shape[0] // 2
     before, after = shift_z(weights_half, 1), shift_z(weights_half, -1)
-    far_top, far_bottom = shift_z(before[:half], 1), shift_z(after[half:], -1)
+    top, bottom = halves(before, after, ())
+    far_top, far_bottom = shift_z(top, 1), shift_z(bottom, -1)
     ring_weights = [weights_half, before, far_top, far_bottom, after]
 
     keep, send, state = fragment_columns(place, weights, anchor_local, moment_local, scale)
@@ -478,15 +523,15 @@
 
     own_0, left, right, keep_left, keep_right = first_gradient(arrived, (before, after))
     left_0, right_0 = shift_z(left, -1), shift_z(right, 1)
-    kept = (keep_left, keep_right, left_0, right_0)
-    own_1, left, right, keep_left, keep_right = later_gradient(place, later, arrived, kept, ())
+    own_1, left, right, next_left, next_right = later_gradient(place, later, arrived)
+    left, right = join(keep_left, keep_right, left_0, right_0, left, right)
     near = jnp.concatenate([near, swap_rep(near, 8)])
     near = jnp.concatenate([near, swap_rep(near, 4)])
     far = swap_rep(near, 1)
     left_1, right_1 = shift_z(left, -1), shift_z(right, 1)
-    last_left, last_right = forward(keep_left, keep_right, left_1, right_1)
+    last_left, last_right = forward(next_left, next_right, left_1, right_1)
     last_left, last_right = shift_z(last_left, -1), shift_z(last_right, 1)
-    pieces = [own_0, left_0, right_0, own_1, left_1, right_1, last_left, last_right]
+    pieces = ([own_0, left_0, right_0, left_1, right_1], [own_1, left_1, right_1, last_left, last_right])
 
     partial = values_partial(place, arrived, later, ring_weights, (own_1,))
     value_rows = values_sum(factor, [partial[0]] + [shift_y(partial[k], -k) for k in (1, 2, 3)])
@@ -496,9 +541,12 @@
     first_scale = 1.0 / (1.0 - jnp.power(FIRST_DECAY, clock))
     second_scale = 1.0 / (1.0 - jnp.power(SECOND_DECAY, clock))
     rates = jnp.stack([rate, first_scale, second_scale, jnp.full((), factor, F32)])
-    params_out, first_new, second_new = adam(
-        place, rates, weights, adam_first[0], adam_second[0], pieces, near, far
-    )
+    begun = ()
+    for chunk in range(len(CHUNKS)):
+        begun = adam(
+            chunk, place, rates, weights, adam_first[0], adam_second[0], pieces[chunk], near, far, begun
+        )
+    params_out, first_new, second_new = begun
     return (
         value_rows[None],
         params_out[None],

time: 131 us -> 129 us (0.985)
  Pallas kernels: 38.6 us -> 42.7 us
  starting transfers between devices: 52.6 us -> 49.7 us
  local copies, waits for them, and re-layouts: 9.79 us -> 7.12 us
  waiting for transfers between devices: 23.4 us -> 21.9 us
    pallas_call x2 -> x5, Pallas kernels: 7.66 us -> 12.3 us  [the longest x2 6.66 us: adam(): pl.pallas_call(functools.partial(adam_kernel, chunk), grid=(2,), out_shap...]
    slice x2 -> x0, local copies, waits for them, and re-layouts: 3.33 us -> none  [local(): far_top, far_bottom = (shift_z(before[:half], 1), shift_z(after[half:], -1))]
    ppermute x10, waiting for transfers between devices: 12.7 us -> 9.9 us  [shift_z(): return lax.ppermute(array, 'shard', pairs)]
    ppermute x6, starting transfers between devices: 12 us -> 10 us  [shift_y(): return lax.ppermute(array, 'shard', pairs)]
    ppermute x6, waiting for transfers between devices: 2.16 us -> 3.48 us  [shift_y(): return lax.ppermute(array, 'shard', pairs)]
  transfers between devices with their start and end apart: 24 -> 24, of which waited for: 9 -> 7; matrix products, arithmetic and copies ran while one was open for 5% -> 3% of each run, Pallas kernels for 21% -> 26%
where the time goes in v3:
time: 129 us; the launch traced here: 127 us
  starting transfers between devices  49.7 us (39%)
  Pallas kernels  42.7 us (33%)
  waiting for transfers between devices  21.9 us (17%)
  local copies, waits for them, and re-layouts  7.12 us (6%)
  other arithmetic  3.03 us (2%)
  between operations  2.57 us (2%)
    ppermute x10, starting transfers between devices, shift_z(): return lax.ppermute(array, 'shard', pairs)  24.7 us
    ppermute x7, starting transfers between devices, swap_rep(): return lax.ppermute(array, 'rep', [(r, r ^ bit) for r in range(16)])  10.2 us
    ppermute x6, starting transfers between devices, shift_y(): return lax.ppermute(array, 'shard', pairs)  10 us
    ppermute x10, waiting for transfers between devices, shift_z(): return lax.ppermute(array, 'shard', pairs)  9.9 us
    ppermute x7, waiting for transfers between devices, swap_rep(): return lax.ppermute(array, 'rep', [(r, r ^ bit) for r in range(16)])  8.46 us
    pallas_call x2, Pallas kernels, adam(): pl.pallas_call(functools.partial(adam_kernel, chunk), grid=(2,), out_shap...  6.66 us
    pallas_call x1, Pallas kernels, values_partial(): pl.pallas_call(values_kernel, grid=(1,), out_shape=[pltpu.HBM(shape, F32...  5.91 us
    unnamed x40, local copies, waits for them, and re-layouts  5.86 us
  transfers between devices with their start and end apart: 24, of which 7 were waited for; matrix products, arithmetic and copies ran while one was open for 3% of the time, Pallas kernels for 26%

profile of v3, /device:TPU:2, one launch (start us, length us, event | category | flops | bytes accessed | tf_op | source)
XLA Modules:
  0.0 127.1 jit_solution(4486754803227798342)
XLA Ops:
  1.9 5.8 %first_pack.1 = (bf16[4,256,1536]{2,1,0:T(8,128)(2,1)}, f32[256,1]{1,0:T(8,128)}) custom-call(s32[4]{0:T(128)} %pad_add_fusion.place, bf16[256,8192]{1,0:T(8,128)(2,1)} %bitcast.32, f32[1,8192]{1,0:T(1,128)} %bitcast.47, bf16[256,512]{1,0:T(8,128)(2,1)} %bitcast.54), custom_call_target="tpu_custom_call" | custom-call | flops 1 | bytes 1 | tf_op jit(solution)/shard_map/first_pack/pallas_call | solution.py:85
  7.7 4.8 %all-to-all-start = ((bf16[4,256,1536]{2,1,0:T(8,128)(2,1)}), bf16[4,256,1536]{2,1,0:T(8,128)(2,1)}, u32[]{:S(2)}, u32[]{:S(2)}) async-start(bf16[4,256,1536]{2,1,0:T(8,128)(2,1)} %get-tuple-element.44), calls=%async_computation | async-start | bytes 6291456 | tf_op jit(solution)/shard_map/all_to_all | solution.py:34
  19.8 4.5 %collective-permute-done.1 = f32[10,32,128]{2,1,0:T(8,128)S(1)} collective-permute-done((f32[10,32,128]{2,1,0:T(8,128)S(1)}, f32[10,32,128]{2,1,0:T(8,128)S(1)}, u32[]{:S(2)}, u32[]{:S(2)}) %collective-permute-start.1) | collective-permute-done | bytes 163872 | tf_op jit(solution)/shard_map/ppermute | solution.py:43
  24.4 2.2 %collective-permute-start.2 = (f32[2,2,32,128]{3,2,1,0:T(8,128)S(1)}, f32[2,2,32,128]{3,2,1,0:T(8,128)S(1)}, u32[]{:S(2)}, u32[]{:S(2)}) collective-permute-start(f32[2,2,32,128]{3,2,1,0:T(8,128)S(1)} %dynamic-slice_bitcast_fusion), channel_id=1, source_target_pairs={{0,64},{16,80},{32,96},{48,112},{64,0},{80,16},{96,32},{112,48},{1... | collective-permute-start | bytes 196616 | tf_op jit(solution)/shard_map/ppermute | solution.py:43
  28.4 2.9 %collective-permute-start.8 = (bf16[512,512]{1,0:T(8,128)(2,1)S(1)}, bf16[512,512]{1,0:T(8,128)(2,1)S(1)}, u32[]{:S(2)}, u32[]{:S(2)}) collective-permute-start(bf16[512,512]{1,0:T(8,128)(2,1)S(1)} %bitcast_convert_fusion.refs_4_), channel_id=1, source_target_pairs={{0,3},{1,0},{2,1},{3,2},{4,7},{5,4},{6,5},{7,6},{8,11},{9,8},{10,9... | collective-permute-start | bytes 1572872 | tf_op jit(solution)/shard_map/ppermute | solution.py:39
  32.0 2.4 %collective-permute-start.3 = (f32[2,32,128]{2,1,0:T(8,128)S(1)}, f32[2,32,128]{2,1,0:T(8,128)S(1)}, u32[]{:S(2)}, u32[]{:S(2)}) collective-permute-start(f32[2,32,128]{2,1,0:T(8,128)S(1)} %get-tuple-element.82), channel_id=1, source_target_pairs={{0,128},{16,144},{32,160},{48,176},{64,192},{80,208},{96,224},{112... | collective-permute-start | bytes 98312 | tf_op jit(solution)/shard_map/ppermute | solution.py:43
  35.0 2.4 %collective-permute-done.3.other = f32[2,32,128]{2,1,0:T(8,128)S(1)} collective-permute-done((f32[2,32,128]{2,1,0:T(8,128)S(1)}, f32[2,32,128]{2,1,0:T(8,128)S(1)}, u32[]{:S(2)}, u32[]{:S(2)}) %collective-permute-start.3) | collective-permute-done | bytes 32800 | tf_op jit(solution)/shard_map/ppermute | solution.py:43
  39.7 5.0 %later_pack.1 = (bf16[256,1024]{1,0:T(8,128)(2,1)}, bf16[256,1024]{1,0:T(8,128)(2,1)}, bf16[256,1024]{1,0:T(8,128)(2,1)}, bf16[256,1024]{1,0:T(8,128)(2,1)}) custom-call(s32[4]{0:T(128)} %pad_add_fusion.place, bf16[256,8192]{1,0:T(8,128)(2,1)} %bitcast.33, bf16[256,8192]{1,0:T(8,128)(2,1)} %bitcast.34, bf16[256,8192]{1,0:T(8,128)(2,1)} %bitcast.35, ...), custom_call_target="tpu_custom_call" | custom-call | flops 1 | bytes 1 | tf_op jit(solution)/shard_map/later_pack/pallas_call | solution.py:126
  46.7 2.7 %collective-permute-start.5 = (bf16[256,1024]{1,0:T(8,128)(2,1)}, bf16[256,1024]{1,0:T(8,128)(2,1)}, u32[]{:S(2)}, u32[]{:S(2)}) collective-permute-start(bf16[256,1024]{1,0:T(8,128)(2,1)} %get-tuple-element.52), channel_id=1, source_target_pairs={{0,8},{1,9},{2,10},{3,11},{4,12},{5,13},{6,14},{7,15},{8,0},{9,1},... | collective-permute-start | bytes 1572872 | tf_op jit(solution)/shard_map/ppermute | solution.py:48
  50.9 4.1 %collective-permute-done.8.after.refs_8_.refs_1_ = bf16[512,512]{1,0:T(8,128)(2,1)S(1)} collective-permute-done((bf16[512,512]{1,0:T(8,128)(2,1)S(1)}, bf16[512,512]{1,0:T(8,128)(2,1)S(1)}, u32[]{:S(2)}, u32[]{:S(2)}) %collective-permute-start.8) | collective-permute-done | bytes 524320 | tf_op jit(solution)/shard_map/ppermute | solution.py:39
  55.7 3.9 %first_gradient.1 = (f32[256,512]{1,0:T(8,128)}, bf16[256,512]{1,0:T(8,128)(2,1)}, bf16[256,512]{1,0:T(8,128)(2,1)}, f32[128,512]{1,0:T(8,128)}, f32[128,512]{1,0:T(8,128)}) custom-call(bf16[4,256,1536]{2,1,0:T(8,128)(2,1)} %all-to-all-done.refs_4_.arrived.normed.cot, bf16[4,256,1536]{2,1,0:T(8,128)(2,1)} %all-to-all-done.refs_4_.arrived.normed.cot, ...), custom_call_target="tpu_custom_call" | custom-call | flops 1 | bytes 1 | tf_op jit(solution)/shard_map/first_gradient/pallas_call | solution.py:199
  59.7 2.8 %collective-permute-start.14 = (bf16[256,512]{1,0:T(8,128)(2,1)}, bf16[256,512]{1,0:T(8,128)(2,1)S(1)}, u32[]{:S(2)}, u32[]{:S(2)}) collective-permute-start(bf16[256,512]{1,0:T(8,128)(2,1)} %get-tuple-element.63), channel_id=1, source_target_pairs={{0,3},{1,0},{2,1},{3,2},{4,7},{5,4},{6,5},{7,6},{8,11},{9,8},{10,9... | collective-permute-start | bytes 786440 | tf_op jit(solution)/shard_map/ppermute | solution.py:39
  65.3 4.1 %collective-permute-start.9 = (bf16[256,512]{1,0:T(8,128)(2,1)}, bf16[256,512]{1,0:T(8,128)(2,1)S(1)}, u32[]{:S(2)}, u32[]{:S(2)}) collective-permute-start(bf16[256,512]{1,0:T(8,128)(2,1)} %get-tuple-element.54), channel_id=1, source_target_pairs={{0,1},{1,2},{2,3},{3,0},{4,5},{5,6},{6,7},{7,4},{8,9},{9,10},{10,1... | collective-permute-start | bytes 786440 | tf_op jit(solution)/shard_map/ppermute | solution.py:39
  69.5 3.5 %collective-permute-done.5.refs_2_ = bf16[256,1024]{1,0:T(8,128)(2,1)} collective-permute-done((bf16[256,1024]{1,0:T(8,128)(2,1)}, bf16[256,1024]{1,0:T(8,128)(2,1)}, u32[]{:S(2)}, u32[]{:S(2)}) %collective-permute-start.5) | collective-permute-done | bytes 524320 | tf_op jit(solution)/shard_map/ppermute | solution.py:48
  72.9 6.3 %collective-permute-start.10 = (bf16[256,512]{1,0:T(8,128)(2,1)}, bf16[256,512]{1,0:T(8,128)(2,1)S(1)}, u32[]{:S(2)}, u32[]{:S(2)}) collective-permute-start(bf16[256,512]{1,0:T(8,128)(2,1)} %get-tuple-element.55), channel_id=1, source_target_pairs={{0,3},{1,0},{2,1},{3,2},{4,7},{5,4},{6,5},{7,6},{8,11},{9,8},{10,9... | collective-permute-start | bytes 786440 | tf_op jit(solution)/shard_map/ppermute | solution.py:39
  79.2 2.1 %collective-permute-start.20 = (f32[2,32,128]{2,1,0:T(8,128)S(1)}, f32[2,32,128]{2,1,0:T(8,128)S(1)}, u32[]{:S(2)}, u32[]{:S(2)}) collective-permute-start(f32[2,32,128]{2,1,0:T(8,128)S(1)} %copy-done.10), channel_id=1, source_target_pairs={{0,128},{16,144},{32,160},{48,176},{64,192},{80,208},{96,224},{112... | collective-permute-start | bytes 98312 | tf_op jit(solution)/shard_map/ppermute | solution.py:43
  81.4 4.0 %later_gradient.1 = (f32[256,512]{1,0:T(8,128)}, bf16[384,512]{1,0:T(8,128)(2,1)}, bf16[384,512]{1,0:T(8,128)(2,1)}, f32[128,512]{1,0:T(8,128)}, f32[128,512]{1,0:T(8,128)}) custom-call(s32[4]{0:T(128)} %pad_add_fusion.place, bf16[256,1024]{1,0:T(8,128)(2,1)} %get-tuple-element.50.refs_0_, bf16[256,1024]{1,0:T(8,128)(2,1)} %collective-permute-done.4.refs_1_, ...), custom_call_target="tpu_custom_call" | custom-call | flops 1 | bytes 1 | tf_op jit(solution)/shard_map/later_gradient/pallas_call | solution.py:233
  93.3 5.9 %values_partial.1 = (f32[256,512]{1,0:T(8,128)}, bf16[256,512]{1,0:T(8,128)(2,1)}, bf16[256,512]{1,0:T(8,128)(2,1)}, bf16[256,512]{1,0:T(8,128)(2,1)}) custom-call(s32[4]{0:T(128)} %pad_add_fusion.place, bf16[4,256,1536]{2,1,0:T(8,128)(2,1)} %all-to-all-done.refs_4_.arrived.normed.cot, bf16[256,1024]{1,0:T(8,128)(2,1)} %get-tuple-element.50.refs_0_, ...), custom_call_target="tpu_custom_call" | custom-call | flops 1 | bytes 1 | tf_op jit(solution)/shard_map/values_partial/pallas_call | solution.py:298
  99.2 2.5 %collective-permute-start.12 = (bf16[256,512]{1,0:T(8,128)(2,1)}, bf16[256,512]{1,0:T(8,128)(2,1)S(1)}, u32[]{:S(2)}, u32[]{:S(2)}) collective-permute-start(bf16[256,512]{1,0:T(8,128)(2,1)} %get-tuple-element.59), channel_id=1, source_target_pairs={{0,8},{1,9},{2,10},{3,11},{4,12},{5,13},{6,14},{7,15},{8,0},{9,1},... | collective-permute-start | bytes 786440 | tf_op jit(solution)/shard_map/ppermute | solution.py:48
  103.1 3.9 %collective-permute-done.16.from_left.last_left.left = bf16[384,512]{1,0:T(8,128)(2,1)S(1)} collective-permute-done((bf16[384,512]{1,0:T(8,128)(2,1)}, bf16[384,512]{1,0:T(8,128)(2,1)S(1)}, u32[]{:S(2)}, u32[]{:S(2)}) %collective-permute-start.16) | collective-permute-done | bytes 393248 | tf_op jit(solution)/shard_map/ppermute | solution.py:39
  111.6 2.5 %collective-permute-start.18 = (bf16[128,512]{1,0:T(8,128)(2,1)}, bf16[128,512]{1,0:T(8,128)(2,1)S(1)}, u32[]{:S(2)}, u32[]{:S(2)}) collective-permute-start(bf16[128,512]{1,0:T(8,128)(2,1)} %get-tuple-element.71), channel_id=1, source_target_pairs={{0,3},{1,0},{2,1},{3,2},{4,7},{5,4},{6,5},{7,6},{8,11},{9,8},{10,9... | collective-permute-start | bytes 393224 | tf_op jit(solution)/shard_map/ppermute | solution.py:39
  116.8 2.1 %values_sum.1 = bf16[256,512]{1,0:T(8,128)(2,1)} custom-call(f32[256,512]{1,0:T(8,128)} %get-tuple-element.57.own, bf16[256,512]{1,0:T(8,128)(2,1)} %copy-done.13, bf16[256,512]{1,0:T(8,128)(2,1)} %copy-done.14, bf16[256,512]{1,0:T(8,128)(2,1)} %copy-done.15), custom_call_target="tpu_custom_call" | custom-call | flops 1 | bytes 1 | tf_op jit(solution)/shard_map/values_sum/pallas_call | solution.py:406
  119.5 3.4 %adam.2 = (f32[512,512]{1,0:T(8,128)}, f32[512,512]{1,0:T(8,128)}, f32[512,512]{1,0:T(8,128)}) custom-call(s32[4]{0:T(128)} %pad_add_fusion.place, f32[4]{0:T(128)} %pad_maximum_fusion.2.rates, f32[512,512]{1,0:T(8,128)} %bitcast.38, f32[512,512]{1,0:T(8,128)} %bitcast.40, f32[512,512]{1,0:T(8,128)} %bitcast.42, f32[256,512]{1,0:T(8,128)} %get-tuple-element.73.own, ...), custom_call_target="tpu_custom_call" | custom-call | flops 1 | bytes 1 | tf_op jit(solution)/shard_map/adam/pallas_call | solution.py:460
  123.6 3.3 %adam.3 = (f32[512,512]{1,0:T(8,128)}, f32[512,512]{1,0:T(8,128)}, f32[512,512]{1,0:T(8,128)}) custom-call(s32[4]{0:T(128)} %pad_add_fusion.place, f32[4]{0:T(128)} %pad_maximum_fusion.2.rates, f32[512,512]{1,0:T(8,128)} %bitcast.39, f32[512,512]{1,0:T(8,128)} %bitcast.41, ...), custom_call_target="tpu_custom_call", output_to_operand_aliasing={{0}: (12, {}), {1}: (13, {}), {2}: (14, {})} | custom-call | flops 1 | bytes 1 | tf_op jit(solution)/shard_map/adam/pallas_call | solution.py:460
  (89 shorter events, 37.4 us)
Async XLA Ops:
  7.7 47.2 %all-to-all-start = ((bf16[4,256,1536]{2,1,0:T(8,128)(2,1)}), bf16[4,256,1536]{2,1,0:T(8,128)(2,1)}, u32[]{:S(2)}, u32[]{:S(2)}) async-start(bf16[4,256,1536]{2,1,0:T(8,128)(2,1)} %get-tuple-element.44), calls=%async_computation | async-start | bytes 6291456 | tf_op jit(solution)/shard_map/all_to_all | solution.py:34
  14.5 1.6 %collective-permute-start = (f32[8,32,128]{2,1,0:T(8,128)}, f32[8,32,128]{2,1,0:T(8,128)S(1)}, u32[]{:S(2)}, u32[]{:S(2)}) collective-permute-start(f32[8,32,128]{2,1,0:T(8,128)} %get-tuple-element.47), channel_id=1, source_target_pairs={{0,16},{16,0},{32,48},{48,32},{64,80},{80,64},{96,112},{112,96},{1... | collective-permute-start | bytes 393224 | tf_op jit(solution)/shard_map/ppermute | solution.py:43
  17.8 6.5 %collective-permute-start.1 = (f32[10,32,128]{2,1,0:T(8,128)S(1)}, f32[10,32,128]{2,1,0:T(8,128)S(1)}, u32[]{:S(2)}, u32[]{:S(2)}) collective-permute-start(f32[10,32,128]{2,1,0:T(8,128)S(1)} %pad_maximum_fusion), channel_id=1, source_target_pairs={{0,32},{16,48},{32,0},{48,16},{64,96},{80,112},{96,64},{112,80},{1... | collective-permute-start | bytes 491528 | tf_op jit(solution)/shard_map/ppermute | solution.py:43
  24.4 7.0 %collective-permute-start.2 = (f32[2,2,32,128]{3,2,1,0:T(8,128)S(1)}, f32[2,2,32,128]{3,2,1,0:T(8,128)S(1)}, u32[]{:S(2)}, u32[]{:S(2)}) collective-permute-start(f32[2,2,32,128]{3,2,1,0:T(8,128)S(1)} %dynamic-slice_bitcast_fusion), channel_id=1, source_target_pairs={{0,64},{16,80},{32,96},{48,112},{64,0},{80,16},{96,32},{112,48},{1... | collective-permute-start | bytes 196616 | tf_op jit(solution)/shard_map/ppermute | solution.py:43
  26.6 24.2 %collective-permute-start.7 = (bf16[512,512]{1,0:T(8,128)(2,1)S(1)}, bf16[512,512]{1,0:T(8,128)(2,1)S(1)}, u32[]{:S(2)}, u32[]{:S(2)}) collective-permute-start(bf16[512,512]{1,0:T(8,128)(2,1)S(1)} %bitcast_convert_fusion.refs_4_), channel_id=1, source_target_pairs={{0,1},{1,2},{2,3},{3,0},{4,5},{5,6},{6,7},{7,4},{8,9},{9,10},{10,1... | collective-permute-start | bytes 1572872 | tf_op jit(solution)/shard_map/ppermute | solution.py:39
  28.4 26.5 %collective-permute-start.8 = (bf16[512,512]{1,0:T(8,128)(2,1)S(1)}, bf16[512,512]{1,0:T(8,128)(2,1)S(1)}, u32[]{:S(2)}, u32[]{:S(2)}) collective-permute-start(bf16[512,512]{1,0:T(8,128)(2,1)S(1)} %bitcast_convert_fusion.refs_4_), channel_id=1, source_target_pairs={{0,3},{1,0},{2,1},{3,2},{4,7},{5,4},{6,5},{7,6},{8,11},{9,8},{10,9... | collective-permute-start | bytes 1572872 | tf_op jit(solution)/shard_map/ppermute | solution.py:39
  32.0 5.4 %collective-permute-start.3 = (f32[2,32,128]{2,1,0:T(8,128)S(1)}, f32[2,32,128]{2,1,0:T(8,128)S(1)}, u32[]{:S(2)}, u32[]{:S(2)}) collective-permute-start(f32[2,32,128]{2,1,0:T(8,128)S(1)} %get-tuple-element.82), channel_id=1, source_target_pairs={{0,128},{16,144},{32,160},{48,176},{64,192},{80,208},{96,224},{112... | collective-permute-start | bytes 98312 | tf_op jit(solution)/shard_map/ppermute | solution.py:43
  44.7 20.7 %collective-permute-start.4 = (bf16[256,1024]{1,0:T(8,128)(2,1)}, bf16[256,1024]{1,0:T(8,128)(2,1)}, u32[]{:S(2)}, u32[]{:S(2)}) collective-permute-start(bf16[256,1024]{1,0:T(8,128)(2,1)} %get-tuple-element.51), channel_id=1, source_target_pairs={{0,4},{1,5},{2,6},{3,7},{4,8},{5,9},{6,10},{7,11},{8,12},{9,13},{1... | collective-permute-start | bytes 1572872 | tf_op jit(solution)/shard_map/ppermute | solution.py:48
  46.7 26.2 %collective-permute-start.5 = (bf16[256,1024]{1,0:T(8,128)(2,1)}, bf16[256,1024]{1,0:T(8,128)(2,1)}, u32[]{:S(2)}, u32[]{:S(2)}) collective-permute-start(bf16[256,1024]{1,0:T(8,128)(2,1)} %get-tuple-element.52), channel_id=1, source_target_pairs={{0,8},{1,9},{2,10},{3,11},{4,12},{5,13},{6,14},{7,15},{8,0},{9,1},... | collective-permute-start | bytes 1572872 | tf_op jit(solution)/shard_map/ppermute | solution.py:48
  49.4 29.8 %collective-permute-start.6 = (bf16[256,1024]{1,0:T(8,128)(2,1)}, bf16[256,1024]{1,0:T(8,128)(2,1)}, u32[]{:S(2)}, u32[]{:S(2)}) collective-permute-start(bf16[256,1024]{1,0:T(8,128)(2,1)} %get-tuple-element.53), channel_id=1, source_target_pairs={{0,12},{1,13},{2,14},{3,15},{4,0},{5,1},{6,2},{7,3},{8,4},{9,5},{1... | collective-permute-start | bytes 1572872 | tf_op jit(solution)/shard_map/ppermute | solution.py:48
  59.7 25.7 %collective-permute-start.14 = (bf16[256,512]{1,0:T(8,128)(2,1)}, bf16[256,512]{1,0:T(8,128)(2,1)S(1)}, u32[]{:S(2)}, u32[]{:S(2)}) collective-permute-start(bf16[256,512]{1,0:T(8,128)(2,1)} %get-tuple-element.63), channel_id=1, source_target_pairs={{0,3},{1,0},{2,1},{3,2},{4,7},{5,4},{6,5},{7,6},{8,11},{9,8},{10,9... | collective-permute-start | bytes 786440 | tf_op jit(solution)/shard_map/ppermute | solution.py:39
  62.4 23.0 %collective-permute-start.15 = (bf16[256,512]{1,0:T(8,128)(2,1)}, bf16[256,512]{1,0:T(8,128)(2,1)S(1)}, u32[]{:S(2)}, u32[]{:S(2)}) collective-permute-start(bf16[256,512]{1,0:T(8,128)(2,1)} %get-tuple-element.64), channel_id=1, source_target_pairs={{0,1},{1,2},{2,3},{3,0},{4,5},{5,6},{6,7},{7,4},{8,9},{9,10},{10,1... | collective-permute-start | bytes 786440 | tf_op jit(solution)/shard_map/ppermute | solution.py:39
  65.3 27.2 %collective-permute-start.9 = (bf16[256,512]{1,0:T(8,128)(2,1)}, bf16[256,512]{1,0:T(8,128)(2,1)S(1)}, u32[]{:S(2)}, u32[]{:S(2)}) collective-permute-start(bf16[256,512]{1,0:T(8,128)(2,1)} %get-tuple-element.54), channel_id=1, source_target_pairs={{0,1},{1,2},{2,3},{3,0},{4,5},{5,6},{6,7},{7,4},{8,9},{9,10},{10,1... | collective-permute-start | bytes 786440 | tf_op jit(solution)/shard_map/ppermute | solution.py:39
  72.9 19.6 %collective-permute-start.10 = (bf16[256,512]{1,0:T(8,128)(2,1)}, bf16[256,512]{1,0:T(8,128)(2,1)S(1)}, u32[]{:S(2)}, u32[]{:S(2)}) collective-permute-start(bf16[256,512]{1,0:T(8,128)(2,1)} %get-tuple-element.55), channel_id=1, source_target_pairs={{0,3},{1,0},{2,1},{3,2},{4,7},{5,4},{6,5},{7,6},{8,11},{9,8},{10,9... | collective-permute-start | bytes 786440 | tf_op jit(solution)/shard_map/ppermute | solution.py:39
  79.2 11.7 %collective-permute-start.20 = (f32[2,32,128]{2,1,0:T(8,128)S(1)}, f32[2,32,128]{2,1,0:T(8,128)S(1)}, u32[]{:S(2)}, u32[]{:S(2)}) collective-permute-start(f32[2,32,128]{2,1,0:T(8,128)S(1)} %copy-done.10), channel_id=1, source_target_pairs={{0,128},{16,144},{32,160},{48,176},{64,192},{80,208},{96,224},{112... | collective-permute-start | bytes 98312 | tf_op jit(solution)/shard_map/ppermute | solution.py:43
  88.0 18.9 %collective-permute-start.16 = (bf16[384,512]{1,0:T(8,128)(2,1)}, bf16[384,512]{1,0:T(8,128)(2,1)S(1)}, u32[]{:S(2)}, u32[]{:S(2)}) collective-permute-start(bf16[384,512]{1,0:T(8,128)(2,1)} %get-tuple-element.67), channel_id=1, source_target_pairs={{0,3},{1,0},{2,1},{3,2},{4,7},{5,4},{6,5},{7,6},{8,11},{9,8},{10,9... | collective-permute-start | bytes 1179656 | tf_op jit(solution)/shard_map/ppermute | solution.py:39
  89.5 19.4 %collective-permute-start.17 = (bf16[384,512]{1,0:T(8,128)(2,1)}, bf16[384,512]{1,0:T(8,128)(2,1)S(1)}, u32[]{:S(2)}, u32[]{:S(2)}) collective-permute-start(bf16[384,512]{1,0:T(8,128)(2,1)} %get-tuple-element.68), channel_id=1, source_target_pairs={{0,1},{1,2},{2,3},{3,0},{4,5},{5,6},{6,7},{7,4},{8,9},{9,10},{10,1... | collective-permute-start | bytes 1179656 | tf_op jit(solution)/shard_map/ppermute | solution.py:39
  91.0 10.8 %collective-permute-start.21 = (f32[4,32,128]{2,1,0:T(8,128)S(1)}, f32[4,32,128]{2,1,0:T(8,128)S(1)}, u32[]{:S(2)}, u32[]{:S(2)}) collective-permute-start(f32[4,32,128]{2,1,0:T(8,128)S(1)} %pad_maximum_fusion.1), channel_id=1, source_target_pairs={{0,64},{16,80},{32,96},{48,112},{64,0},{80,16},{96,32},{112,48},{1... | collective-permute-start | bytes 196616 | tf_op jit(solution)/shard_map/ppermute | solution.py:43
  99.2 14.8 %collective-permute-start.11 = (bf16[256,512]{1,0:T(8,128)(2,1)}, bf16[256,512]{1,0:T(8,128)(2,1)S(1)}, u32[]{:S(2)}, u32[]{:S(2)}) collective-permute-start(bf16[256,512]{1,0:T(8,128)(2,1)} %get-tuple-element.58), channel_id=1, source_target_pairs={{0,12},{1,13},{2,14},{3,15},{4,0},{5,1},{6,2},{7,3},{8,4},{9,5},{1... | collective-permute-start | bytes 786440 | tf_op jit(solution)/shard_map/ppermute | solution.py:48
  99.2 16.8 %collective-permute-start.12 = (bf16[256,512]{1,0:T(8,128)(2,1)}, bf16[256,512]{1,0:T(8,128)(2,1)S(1)}, u32[]{:S(2)}, u32[]{:S(2)}) collective-permute-start(bf16[256,512]{1,0:T(8,128)(2,1)} %get-tuple-element.59), channel_id=1, source_target_pairs={{0,8},{1,9},{2,10},{3,11},{4,12},{5,13},{6,14},{7,15},{8,0},{9,1},... | collective-permute-start | bytes 786440 | tf_op jit(solution)/shard_map/ppermute | solution.py:48
  101.8 14.2 %collective-permute-start.13 = (bf16[256,512]{1,0:T(8,128)(2,1)}, bf16[256,512]{1,0:T(8,128)(2,1)S(1)}, u32[]{:S(2)}, u32[]{:S(2)}) collective-permute-start(bf16[256,512]{1,0:T(8,128)(2,1)} %get-tuple-element.60), channel_id=1, source_target_pairs={{0,4},{1,5},{2,6},{3,7},{4,8},{5,9},{6,10},{7,11},{8,12},{9,13},{1... | collective-permute-start | bytes 786440 | tf_op jit(solution)/shard_map/ppermute | solution.py:48
  107.0 11.9 %collective-permute-start.22 = (f32[8,32,128]{2,1,0:T(8,128)S(1)}, f32[8,32,128]{2,1,0:T(8,128)S(1)}, u32[]{:S(2)}, u32[]{:S(2)}) collective-permute-start(f32[8,32,128]{2,1,0:T(8,128)S(1)} %constant_dynamic-update-slice_fusion.near), channel_id=1, source_target_pairs={{0,16},{16,0},{32,48},{48,32},{64,80},{80,64},{96,112},{112,96},{1... | collective-permute-start | bytes 393224 | tf_op jit(solution)/shard_map/ppermute | solution.py:43
  111.6 11.4 %collective-permute-start.18 = (bf16[128,512]{1,0:T(8,128)(2,1)}, bf16[128,512]{1,0:T(8,128)(2,1)S(1)}, u32[]{:S(2)}, u32[]{:S(2)}) collective-permute-start(bf16[128,512]{1,0:T(8,128)(2,1)} %get-tuple-element.71), channel_id=1, source_target_pairs={{0,3},{1,0},{2,1},{3,2},{4,7},{5,4},{6,5},{7,6},{8,11},{9,8},{10,9... | collective-permute-start | bytes 393224 | tf_op jit(solution)/shard_map/ppermute | solution.py:39
  114.1 8.9 %collective-permute-start.19 = (bf16[128,512]{1,0:T(8,128)(2,1)}, bf16[128,512]{1,0:T(8,128)(2,1)S(1)}, u32[]{:S(2)}, u32[]{:S(2)}) collective-permute-start(bf16[128,512]{1,0:T(8,128)(2,1)} %get-tuple-element.72), channel_id=1, source_target_pairs={{0,1},{1,2},{2,3},{3,0},{4,5},{5,6},{6,7},{7,4},{8,9},{9,10},{10,1... | collective-permute-start | bytes 393224 | tf_op jit(solution)/shard_map/ppermute | solution.py:39
  (19 other events, 99.2 us)

commit v4 on v3

--- a/solution.py
+++ b/solution.py
@@ -80,7 +80,7 @@
 def first_pack(place, hidden, gain, cot):
     tokens, features = hidden.shape
     columns = cot.shape[1]
-    rows = 64
+    rows = 128
     total = RING * CHUNKS[0][1] + columns
     return pl.pallas_call(
         first_pack_kernel,
@@ -141,29 +141,6 @@
     )(place, *[hidden] * RING, *[gain] * RING, scale, *after)
 
 
-def halves_kernel(before, after, *refs):
-    top, bottom = refs[-2:]
-    half = top.shape[0]
-    top[...] = before[:half]
-    bottom[...] = after[half:]
-
-
-def halves(before, after, needed):
-    rows, columns = before.shape
-    whole_block = pl.BlockSpec((rows, columns), lambda i: (0, 0))
-    half_block = pl.BlockSpec((rows // 2, columns), lambda i: (0, 0))
-    return pl.pallas_call(
-        halves_kernel,
-        grid=(1,),
-        out_shape=[pltpu.HBM((rows // 2, columns), BF16)] * 2,
-        in_specs=[whole_block] * 2 + [pl.BlockSpec(memory_space=pl.ANY)] * len(needed),
-        out_specs=[half_block] * 2,
-        compiler_params=params_of(),
-        cost_estimate=COST,
-        name="halves",
-    )(before, after, *needed)
-
-
 def gradient_block(normed, cot, kz, height):
     rows = jnp.concatenate([n[:, kz * height : (kz + 1) * height] for n in normed], axis=0)
     return lax.dot_general(rows, cot, (((0,), (0,)), ((), ())), preferred_element_type=F32)
@@ -184,17 +161,23 @@
     own[...] = gradient_block(normed, cot, 0, height)
 
 
-def first_gradient_kernel(normed, cot, *refs):
+def first_gradient_kernel(normed, cot, before, after, own, left, right, keep_left, keep_right):
     rows = [normed.at[y] for y in range(RING)]
-    gradient_blocks(rows, jnp.concatenate([cot[y] for y in range(RING)], axis=0), *refs[-5:])
-
-
-def first_gradient(arrived, after):
+    height = own.shape[0]
+    cot_all = jnp.concatenate([cot[y] for y in range(RING)], axis=0)
+    gradient_blocks(rows, cot_all, own, left.at[:height], right.at[:height], keep_left, keep_right)
+    left[height:] = after[...]
+    right[height:] = before[...]
+
+
+def first_gradient(arrived, before, after):
     tokens = arrived.shape[1]
     height = CHUNKS[0][1]
     columns = arrived.shape[2] - RING * height
     full, part = (height, columns), (height // 2, columns)
-    shapes = [(full, F32), (full, BF16), (full, BF16), (part, F32), (part, F32)]
+    rows = before.shape[0] // 2
+    sent = (height + rows, columns)
+    shapes = [(full, F32), (sent, BF16), (sent, BF16), (part, F32), (part, F32)]
     cot_at = RING * height // columns
     return pl.pallas_call(
         first_gradient_kernel,
@@ -203,13 +186,14 @@
         in_specs=[
             pl.BlockSpec((RING, tokens, RING * height), lambda i: (0, 0, 0)),
             pl.BlockSpec((RING, tokens, columns), lambda i: (0, 0, cot_at)),
-        ]
-        + [pl.BlockSpec(memory_space=pl.ANY)] * len(after),
+            pl.BlockSpec((rows, columns), lambda i: (0, 0)),
+            pl.BlockSpec((rows, columns), lambda i: (1, 0)),
+        ],
         out_specs=[pl.BlockSpec(s[0], lambda i: (0, 0)) for s in shapes],
         compiler_params=params_of(),
         cost_estimate=COST,
         name="first_gradient",
-    )(arrived, arrived, *after)
+    )(arrived, arrived, before, after)
 
 
 def later_gradient_kernel(place, *refs):
@@ -300,7 +284,9 @@
         grid=(1,),
         out_shape=[pltpu.HBM(shape, F32 if k == 0 else BF16) for k in range(RING)],
         in_specs=[scalars(), pl.BlockSpec((RING, tokens, RING * CHUNKS[0][1]), lambda i: (0, 0, 0))]
-        + [pl.BlockSpec(w.shape, lambda i: (0, 0)) for w in (*later, *weights)]
+        + [pl.BlockSpec(w.shape, lambda i: (0, 0)) for w in (*later, *weights[:2])]
+        + [pl.BlockSpec((weights[0].shape[0] // 2, columns), lambda i: (1, 0))] * 2
+        + [pl.BlockSpec(weights[4].shape, lambda i: (0, 0))]
         + [pl.BlockSpec(memory_space=pl.ANY)] * len(needed),
         out_specs=[pl.BlockSpec(shape, lambda i: (0, 0))] * RING,
         compiler_params=params_of(),
@@ -420,49 +406,46 @@
     fragment, rep = place[2], place[3]
     x, core = rep // 4, lax.rem(rep, 2)
     rate, first_scale, second_scale, factor = rates[0], rates[1], rates[2], rates[3]
-    step_of = pl.program_id(0)
-    part = 2 * chunk + step_of
-    rows = weights.shape[0]
-    skip = left.shape[0] - 2 * rows
-
-    def step(total):
+    rows = last_left.shape[0]
+    skip = CHUNKS[0][1] // 2 if chunk else 0
+
+    def step(half, total):
+        here = slice(half * rows, (half + 1) * rows)
         gradient = total * factor
-        first_new = FIRST_DECAY * first[...] + (1.0 - FIRST_DECAY) * gradient
-        second_new = SECOND_DECAY * second[...] + (1.0 - SECOND_DECAY) * gradient * gradient
-        out_first[...] = first_new
-        out_second[...] = second_new
+        first_new = FIRST_DECAY * first[here] + (1.0 - FIRST_DECAY) * gradient
+        second_new = SECOND_DECAY * second[here] + (1.0 - SECOND_DECAY) * gradient * gradient
+        out_first[here] = first_new
+        out_second[here] = second_new
         update = (first_new * first_scale) / (jnp.sqrt(second_new * second_scale) + ADAM_EPSILON)
-        out_weights[...] = weights[...] - rate * (update + WEIGHT_DECAY * weights[...])
-
-    @pl.when(step_of == 0)
-    def _():
-        step(own[:rows] + right[skip : skip + rows].astype(F32) + last_left[:rows].astype(F32))
-
-    @pl.when(step_of == 1)
-    def _():
-        step(own[rows:] + left[skip + rows :].astype(F32) + last_right[:rows].astype(F32))
+        out_weights[here] = weights[here] - rate * (update + WEIGHT_DECAY * weights[here])
+
+    step(0, own[:rows] + right[skip : skip + rows].astype(F32) + last_left[...].astype(F32))
+    step(1, own[rows:] + left[skip + rows :].astype(F32) + last_right[...].astype(F32))
 
     width = weights.shape[1] // FRAG
     height = near.shape[1]
     columns = pl.ds(pl.multiple_of(fragment * width, width), width)
-    at = 2 * lax.rem(part // 2 + x // 2, 2) + 4 * lax.rem(part + x, 2)
-    for block in range(4):
-        index = at + block // 2
+    for block in range(weights.shape[0] // height):
+        part = 2 * chunk + block // 4
+        index = 2 * lax.rem(part // 2 + x // 2, 2) + 4 * lax.rem(part + x, 2) + block % 4 // 2
         base = jnp.where(core == block % 2, near[index], far[index])
-        here = slice(block * height, (block + 1) * height)
-        out_weights[here, columns] = base + (out_weights[here, columns] - weights[here, columns])
+        lines = slice(block * height, (block + 1) * height)
+        out_weights[lines, columns] = base + (out_weights[lines, columns] - weights[lines, columns])
 
 
 def adam(chunk, place, rates, weights, first, second, pieces, near, far, begun):
     shape = jax.ShapeDtypeStruct(weights.shape, F32)
-    rows = pl.BlockSpec((weights.shape[0] // 4, weights.shape[1]), lambda i: (2 * chunk + i, 0))
+    rows = pl.BlockSpec((CHUNKS[chunk][1], weights.shape[1]), lambda i: (chunk, 0))
+    half = CHUNKS[chunk][1] // 2
+    skip = CHUNKS[0][1] // 2 if chunk else 0
+    used = (2 * half, skip + 2 * half, skip + 2 * half, half, half)
     operands = (place, rates, weights, first, second, *pieces, near, far)
     return pl.pallas_call(
         functools.partial(adam_kernel, chunk),
-        grid=(2,),
+        grid=(1,),
         out_shape=[shape] * 3,
         in_specs=[scalars(), scalars(), rows, rows, rows]
-        + [pl.BlockSpec(p.shape, lambda i: (0, 0)) for p in pieces]
+        + [pl.BlockSpec((n, p.shape[1]), lambda i: (0, 0)) for n, p in zip(used, pieces)]
         + [pl.BlockSpec(near.shape, lambda i: (0, 0, 0))] * 2
         + [pl.BlockSpec(memory_space=pl.ANY)] * len(begun),
         out_specs=[rows] * 3,
@@ -505,9 +488,6 @@
 
     weights_half = weights.astype(BF16)
     before, after = shift_z(weights_half, 1), shift_z(weights_half, -1)
-    top, bottom = halves(before, after, ())
-    far_top, far_bottom = shift_z(top, 1), shift_z(bottom, -1)
-    ring_weights = [weights_half, before, far_top, far_bottom, after]
 
     keep, send, state = fragment_columns(place, weights, anchor_local, moment_local, scale)
     mine = jnp.concatenate([keep + swap_rep(send, 1), state])
@@ -521,8 +501,9 @@
     packed = later_pack(place, tokens, gain, scale, (near,))
     later = [packed[0]] + [shift_y(packed[k], k) for k in (1, 2, 3)]
 
-    own_0, left, right, keep_left, keep_right = first_gradient(arrived, (before, after))
+    own_0, left, right, keep_left, keep_right = first_gradient(arrived, before, after)
     left_0, right_0 = shift_z(left, -1), shift_z(right, 1)
+    ring_weights = [weights_half, before, right_0, left_0, after]
     own_1, left, right, next_left, next_right = later_gradient(place, later, arrived)
     left, right = join(keep_left, keep_right, left_0, right_0, left, right)
     near = jnp.concatenate([near, swap_rep(near, 8)])

time: 129 us -> 126 us (0.977)
  the two profiles are of different devices: /device:TPU:2 before, /device:TPU:32 now
where the time goes in v4:
time: 126 us; the launch traced here: 125 us
  starting transfers between devices  49.6 us (39%)
  Pallas kernels  40.4 us (32%)
  waiting for transfers between devices  23.6 us (19%)
  local copies, waits for them, and re-layouts  5.56 us (4%)
  other arithmetic  3.84 us (3%)
  between operations  2.37 us (2%)
    ppermute x8, starting transfers between devices, shift_z(): return lax.ppermute(array, 'shard', pairs)  25.1 us
    ppermute x8, waiting for transfers between devices, shift_z(): return lax.ppermute(array, 'shard', pairs)  12.5 us
    ppermute x7, starting transfers between devices, swap_rep(): return lax.ppermute(array, 'rep', [(r, r ^ bit) for r in range(16)])  11.2 us
    ppermute x6, starting transfers between devices, shift_y(): return lax.ppermute(array, 'shard', pairs)  8.49 us
    pallas_call x2, Pallas kernels, adam(): pl.pallas_call(functools.partial(adam_kernel, chunk), grid=(1,), out_shap...  6.82 us
    ppermute x7, waiting for transfers between devices, swap_rep(): return lax.ppermute(array, 'rep', [(r, r ^ bit) for r in range(16)])  6.12 us
    pallas_call x1, Pallas kernels, values_partial(): pl.pallas_call(values_kernel, grid=(1,), out_shape=[pltpu.HBM(shape, F32...  5.91 us
    pallas_call x1, Pallas kernels, later_pack(): pl.pallas_call(later_pack_kernel, out_shape=[pltpu.HBM((tokens, RING * wi...  5.01 us
  transfers between devices with their start and end apart: 22, of which 8 were waited for; matrix products, arithmetic and copies ran while one was open for 4% of the time, Pallas kernels for 26%

profile of v4, /device:TPU:32, one launch (start us, length us, event | category | flops | bytes accessed | tf_op | source)
XLA Modules:
  0.0 125.4 jit_solution(1690786157730019726)
XLA Ops:
  1.9 4.8 %first_pack.1 = (bf16[4,256,1536]{2,1,0:T(8,128)(2,1)}, f32[256,1]{1,0:T(8,128)}) custom-call(s32[4]{0:T(128)} %pad_add_fusion.place, bf16[256,8192]{1,0:T(8,128)(2,1)} %bitcast.32, f32[1,8192]{1,0:T(1,128)} %bitcast.47, bf16[256,512]{1,0:T(8,128)(2,1)} %bitcast.54), custom_call_target="tpu_custom_call" | custom-call | flops 1 | bytes 1 | tf_op jit(solution)/shard_map/first_pack/pallas_call | solution.py:85
  6.7 4.8 %all-to-all-start = ((bf16[4,256,1536]{2,1,0:T(8,128)(2,1)}), bf16[4,256,1536]{2,1,0:T(8,128)(2,1)}, u32[]{:S(2)}, u32[]{:S(2)}) async-start(bf16[4,256,1536]{2,1,0:T(8,128)(2,1)} %get-tuple-element.42), calls=%async_computation | async-start | bytes 6291456 | tf_op jit(solution)/shard_map/all_to_all | solution.py:34
  11.5 2.0 %fragment_columns.1 = (f32[8,32,128]{2,1,0:T(8,128)}, f32[8,32,128]{2,1,0:T(8,128)}, f32[2,32,128]{2,1,0:T(8,128)}) custom-call(s32[4]{0:T(128)} %pad_add_fusion.place, f32[512,512]{1,0:T(8,128)} %bitcast.37, f32[32,512]{1,0:T(8,128)} %bitcast.55, f32[32,512]{1,0:T(8,128)} %bitcast.57, f32[256,1]{1,0:T(8,128)} %get-tuple-element.43.after.refs_8_), custom_call_target="tpu_custom_call" | custom-call | flops 1 | bytes 1 | tf_op jit(solution)/shard_map/fragment_columns/pallas_call | solution.py:315
  16.8 1.9 %collective-permute-start.1 = (f32[10,32,128]{2,1,0:T(8,128)S(1)}, f32[10,32,128]{2,1,0:T(8,128)S(1)}, u32[]{:S(2)}, u32[]{:S(2)}) collective-permute-start(f32[10,32,128]{2,1,0:T(8,128)S(1)} %pad_maximum_fusion), channel_id=1, source_target_pairs={{0,32},{16,48},{32,0},{48,16},{64,96},{80,112},{96,64},{112,80},{1... | collective-permute-start | bytes 491528 | tf_op jit(solution)/shard_map/ppermute | solution.py:43
  21.2 3.0 %collective-permute-start.8 = (bf16[512,512]{1,0:T(8,128)(2,1)}, bf16[512,512]{1,0:T(8,128)(2,1)S(1)}, u32[]{:S(2)}, u32[]{:S(2)}) collective-permute-start(bf16[512,512]{1,0:T(8,128)(2,1)} %bitcast_convert_fusion.refs_4_), channel_id=1, source_target_pairs={{0,3},{1,0},{2,1},{3,2},{4,7},{5,4},{6,5},{7,6},{8,11},{9,8},{10,9... | collective-permute-start | bytes 1572872 | tf_op jit(solution)/shard_map/ppermute | solution.py:39
  25.8 2.8 %collective-permute-done.2 = f32[2,2,32,128]{3,2,1,0:T(8,128)S(1)} collective-permute-done((f32[2,2,32,128]{3,2,1,0:T(8,128)S(1)}, f32[2,2,32,128]{3,2,1,0:T(8,128)S(1)}, u32[]{:S(2)}, u32[]{:S(2)}) %collective-permute-start.2) | collective-permute-done | bytes 65568 | tf_op jit(solution)/shard_map/ppermute | solution.py:43
  29.2 3.0 %collective-permute-start.3 = (f32[2,32,128]{2,1,0:T(8,128)S(1)}, f32[2,32,128]{2,1,0:T(8,128)S(1)}, u32[]{:S(2)}, u32[]{:S(2)}) collective-permute-start(f32[2,32,128]{2,1,0:T(8,128)S(1)} %get-tuple-element.78), channel_id=1, source_target_pairs={{0,128},{16,144},{32,160},{48,176},{64,192},{80,208},{96,224},{112... | collective-permute-start | bytes 98312 | tf_op jit(solution)/shard_map/ppermute | solution.py:43
  36.9 5.0 %later_pack.1 = (bf16[256,1024]{1,0:T(8,128)(2,1)}, bf16[256,1024]{1,0:T(8,128)(2,1)}, bf16[256,1024]{1,0:T(8,128)(2,1)}, bf16[256,1024]{1,0:T(8,128)(2,1)}) custom-call(s32[4]{0:T(128)} %pad_add_fusion.place, bf16[256,8192]{1,0:T(8,128)(2,1)} %bitcast.33, bf16[256,8192]{1,0:T(8,128)(2,1)} %bitcast.34, bf16[256,8192]{1,0:T(8,128)(2,1)} %bitcast.35, ...), custom_call_target="tpu_custom_call" | custom-call | flops 1 | bytes 1 | tf_op jit(solution)/shard_map/later_pack/pallas_call | solution.py:126
  41.9 2.0 %collective-permute-start.4 = (bf16[256,1024]{1,0:T(8,128)(2,1)}, bf16[256,1024]{1,0:T(8,128)(2,1)}, u32[]{:S(2)}, u32[]{:S(2)}) collective-permute-start(bf16[256,1024]{1,0:T(8,128)(2,1)} %get-tuple-element.49), channel_id=1, source_target_pairs={{0,4},{1,5},{2,6},{3,7},{4,8},{5,9},{6,10},{7,11},{8,12},{9,13},{1... | collective-permute-start | bytes 1572872 | tf_op jit(solution)/shard_map/ppermute | solution.py:48
  44.0 2.7 %collective-permute-start.5 = (bf16[256,1024]{1,0:T(8,128)(2,1)}, bf16[256,1024]{1,0:T(8,128)(2,1)}, u32[]{:S(2)}, u32[]{:S(2)}) collective-permute-start(bf16[256,1024]{1,0:T(8,128)(2,1)} %get-tuple-element.50), channel_id=1, source_target_pairs={{0,8},{1,9},{2,10},{3,11},{4,12},{5,13},{6,14},{7,15},{8,0},{9,1},... | collective-permute-start | bytes 1572872 | tf_op jit(solution)/shard_map/ppermute | solution.py:48
  48.1 2.5 %all-to-all-done.normed.cot.refs_4_.arrived = bf16[4,256,1536]{2,1,0:T(8,128)(2,1)} async-done(((bf16[4,256,1536]{2,1,0:T(8,128)(2,1)}), bf16[4,256,1536]{2,1,0:T(8,128)(2,1)}, u32[]{:S(2)}, u32[]{:S(2)}) %all-to-all-start) | async-done | bytes 3145760 | tf_op jit(solution)/shard_map/all_to_all | solution.py:34
  50.6 4.3 %first_gradient.1 = (f32[256,512]{1,0:T(8,128)}, bf16[512,512]{1,0:T(8,128)(2,1)}, bf16[512,512]{1,0:T(8,128)(2,1)}, f32[128,512]{1,0:T(8,128)}, f32[128,512]{1,0:T(8,128)}) custom-call(bf16[4,256,1536]{2,1,0:T(8,128)(2,1)} %all-to-all-done.normed.cot.refs_4_.arrived, bf16[4,256,1536]{2,1,0:T(8,128)(2,1)} %all-to-all-done.normed.cot.refs_4_.arrived, ...), custom_call_target="tpu_custom_call" | custom-call | flops 1 | bytes 1 | tf_op jit(solution)/shard_map/first_gradient/pallas_call | solution.py:182
  55.0 12.2 %collective-permute-start.9 = (bf16[512,512]{1,0:T(8,128)(2,1)}, bf16[512,512]{1,0:T(8,128)(2,1)S(1)}, u32[]{:S(2)}, u32[]{:S(2)}) collective-permute-start(bf16[512,512]{1,0:T(8,128)(2,1)} %get-tuple-element.52), channel_id=1, source_target_pairs={{0,1},{1,2},{2,3},{3,0},{4,5},{5,6},{6,7},{7,4},{8,9},{9,10},{10,1... | collective-permute-start | bytes 1572872 | tf_op jit(solution)/shard_map/ppermute | solution.py:39
  67.2 2.7 %collective-permute-start.10 = (bf16[512,512]{1,0:T(8,128)(2,1)}, bf16[512,512]{1,0:T(8,128)(2,1)S(1)}, u32[]{:S(2)}, u32[]{:S(2)}) collective-permute-start(bf16[512,512]{1,0:T(8,128)(2,1)} %get-tuple-element.53), channel_id=1, source_target_pairs={{0,3},{1,0},{2,1},{3,2},{4,7},{5,4},{6,5},{7,6},{8,11},{9,8},{10,9... | collective-permute-start | bytes 1572872 | tf_op jit(solution)/shard_map/ppermute | solution.py:39
  69.9 3.0 %collective-permute-start.18 = (f32[2,32,128]{2,1,0:T(8,128)S(1)}, f32[2,32,128]{2,1,0:T(8,128)S(1)}, u32[]{:S(2)}, u32[]{:S(2)}) collective-permute-start(f32[2,32,128]{2,1,0:T(8,128)S(1)} %copy-done.9), channel_id=1, source_target_pairs={{0,128},{16,144},{32,160},{48,176},{64,192},{80,208},{96,224},{112... | collective-permute-start | bytes 98312 | tf_op jit(solution)/shard_map/ppermute | solution.py:43
  72.9 4.0 %later_gradient.1 = (f32[256,512]{1,0:T(8,128)}, bf16[384,512]{1,0:T(8,128)(2,1)}, bf16[384,512]{1,0:T(8,128)(2,1)}, f32[128,512]{1,0:T(8,128)}, f32[128,512]{1,0:T(8,128)}) custom-call(s32[4]{0:T(128)} %pad_add_fusion.place, bf16[256,1024]{1,0:T(8,128)(2,1)} %get-tuple-element.48.refs_0_, bf16[256,1024]{1,0:T(8,128)(2,1)} %collective-permute-done.4.refs_1_, ...), custom_call_target="tpu_custom_call" | custom-call | flops 1 | bytes 1 | tf_op jit(solution)/shard_map/later_gradient/pallas_call | solution.py:217
  76.9 5.5 %collective-permute-done.9.refs_6_.from_right.right = bf16[512,512]{1,0:T(8,128)(2,1)S(1)} collective-permute-done((bf16[512,512]{1,0:T(8,128)(2,1)}, bf16[512,512]{1,0:T(8,128)(2,1)S(1)}, u32[]{:S(2)}, u32[]{:S(2)}) %collective-permute-start.9) | collective-permute-done | bytes 524320 | tf_op jit(solution)/shard_map/ppermute | solution.py:39
  82.4 7.0 %collective-permute-done.10.refs_7_.from_left.left = bf16[512,512]{1,0:T(8,128)(2,1)S(1)} collective-permute-done((bf16[512,512]{1,0:T(8,128)(2,1)}, bf16[512,512]{1,0:T(8,128)(2,1)S(1)}, u32[]{:S(2)}, u32[]{:S(2)}) %collective-permute-start.10) | collective-permute-done | bytes 524320 | tf_op jit(solution)/shard_map/ppermute | solution.py:39
  92.1 2.9 %collective-permute-start.15 = (bf16[384,512]{1,0:T(8,128)(2,1)}, bf16[384,512]{1,0:T(8,128)(2,1)S(1)}, u32[]{:S(2)}, u32[]{:S(2)}) collective-permute-start(bf16[384,512]{1,0:T(8,128)(2,1)} %get-tuple-element.64), channel_id=1, source_target_pairs={{0,1},{1,2},{2,3},{3,0},{4,5},{5,6},{6,7},{7,4},{8,9},{9,10},{10,1... | collective-permute-start | bytes 1179656 | tf_op jit(solution)/shard_map/ppermute | solution.py:39
  96.6 5.9 %values_partial.1 = (f32[256,512]{1,0:T(8,128)}, bf16[256,512]{1,0:T(8,128)(2,1)}, bf16[256,512]{1,0:T(8,128)(2,1)}, bf16[256,512]{1,0:T(8,128)(2,1)}) custom-call(s32[4]{0:T(128)} %pad_add_fusion.place, bf16[4,256,1536]{2,1,0:T(8,128)(2,1)} %all-to-all-done.normed.cot.refs_4_.arrived, bf16[256,1024]{1,0:T(8,128)(2,1)} %get-tuple-element.48.refs_0_, ...), custom_call_target="tpu_custom_call" | custom-call | flops 1 | bytes 1 | tf_op jit(solution)/shard_map/values_partial/pallas_call | solution.py:282
  112.1 2.3 %collective-permute-done.13.three = bf16[256,512]{1,0:T(8,128)(2,1)S(1)} collective-permute-done((bf16[256,512]{1,0:T(8,128)(2,1)}, bf16[256,512]{1,0:T(8,128)(2,1)S(1)}, u32[]{:S(2)}, u32[]{:S(2)}) %collective-permute-start.13) | collective-permute-done | bytes 262176 | tf_op jit(solution)/shard_map/ppermute | solution.py:48
  115.1 2.1 %values_sum.1 = bf16[256,512]{1,0:T(8,128)(2,1)} custom-call(f32[256,512]{1,0:T(8,128)} %get-tuple-element.55.own, bf16[256,512]{1,0:T(8,128)(2,1)} %copy-done.10, bf16[256,512]{1,0:T(8,128)(2,1)} %copy-done.11, bf16[256,512]{1,0:T(8,128)(2,1)} %copy-done.12), custom_call_target="tpu_custom_call" | custom-call | flops 1 | bytes 1 | tf_op jit(solution)/shard_map/values_sum/pallas_call | solution.py:392
  117.8 3.4 %adam.2 = (f32[512,512]{1,0:T(8,128)}, f32[512,512]{1,0:T(8,128)}, f32[512,512]{1,0:T(8,128)}) custom-call(s32[4]{0:T(128)} %pad_add_fusion.place, f32[4]{0:T(128)} %pad_maximum_fusion.2.rates, f32[512,512]{1,0:T(8,128)} %bitcast.38, f32[512,512]{1,0:T(8,128)} %bitcast.40, f32[512,512]{1,0:T(8,128)} %bitcast.42, f32[256,512]{1,0:T(8,128)} %get-tuple-element.69.own, ...), custom_call_target="tpu_custom_call" | custom-call | flops 1 | bytes 1 | tf_op jit(solution)/shard_map/adam/pallas_call | solution.py:443
  121.9 3.4 %adam.3 = (f32[512,512]{1,0:T(8,128)}, f32[512,512]{1,0:T(8,128)}, f32[512,512]{1,0:T(8,128)}) custom-call(s32[4]{0:T(128)} %pad_add_fusion.place, f32[4]{0:T(128)} %pad_maximum_fusion.2.rates, f32[512,512]{1,0:T(8,128)} %bitcast.39, f32[512,512]{1,0:T(8,128)} %bitcast.41, ...), custom_call_target="tpu_custom_call", output_to_operand_aliasing={{0}: (12, {}), {1}: (13, {}), {2}: (14, {})} | custom-call | flops 1 | bytes 1 | tf_op jit(solution)/shard_map/adam/pallas_call | solution.py:443
  (78 shorter events, 29.6 us)
Async XLA Ops:
  6.7 43.9 %all-to-all-start = ((bf16[4,256,1536]{2,1,0:T(8,128)(2,1)}), bf16[4,256,1536]{2,1,0:T(8,128)(2,1)}, u32[]{:S(2)}, u32[]{:S(2)}) async-start(bf16[4,256,1536]{2,1,0:T(8,128)(2,1)} %get-tuple-element.42), calls=%async_computation | async-start | bytes 6291456 | tf_op jit(solution)/shard_map/all_to_all | solution.py:34
  13.6 1.6 %collective-permute-start = (f32[8,32,128]{2,1,0:T(8,128)}, f32[8,32,128]{2,1,0:T(8,128)S(1)}, u32[]{:S(2)}, u32[]{:S(2)}) collective-permute-start(f32[8,32,128]{2,1,0:T(8,128)} %get-tuple-element.45), channel_id=1, source_target_pairs={{0,16},{16,0},{32,48},{48,32},{64,80},{80,64},{96,112},{112,96},{1... | collective-permute-start | bytes 393224 | tf_op jit(solution)/shard_map/ppermute | solution.py:43
  16.8 7.4 %collective-permute-start.1 = (f32[10,32,128]{2,1,0:T(8,128)S(1)}, f32[10,32,128]{2,1,0:T(8,128)S(1)}, u32[]{:S(2)}, u32[]{:S(2)}) collective-permute-start(f32[10,32,128]{2,1,0:T(8,128)S(1)} %pad_maximum_fusion), channel_id=1, source_target_pairs={{0,32},{16,48},{32,0},{48,16},{64,96},{80,112},{96,64},{112,80},{1... | collective-permute-start | bytes 491528 | tf_op jit(solution)/shard_map/ppermute | solution.py:43
  19.6 28.5 %collective-permute-start.7 = (bf16[512,512]{1,0:T(8,128)(2,1)}, bf16[512,512]{1,0:T(8,128)(2,1)S(1)}, u32[]{:S(2)}, u32[]{:S(2)}) collective-permute-start(bf16[512,512]{1,0:T(8,128)(2,1)} %bitcast_convert_fusion.refs_4_), channel_id=1, source_target_pairs={{0,1},{1,2},{2,3},{3,0},{4,5},{5,6},{6,7},{7,4},{8,9},{9,10},{10,1... | collective-permute-start | bytes 1572872 | tf_op jit(solution)/shard_map/ppermute | solution.py:39
  21.2 26.9 %collective-permute-start.8 = (bf16[512,512]{1,0:T(8,128)(2,1)}, bf16[512,512]{1,0:T(8,128)(2,1)S(1)}, u32[]{:S(2)}, u32[]{:S(2)}) collective-permute-start(bf16[512,512]{1,0:T(8,128)(2,1)} %bitcast_convert_fusion.refs_4_), channel_id=1, source_target_pairs={{0,3},{1,0},{2,1},{3,2},{4,7},{5,4},{6,5},{7,6},{8,11},{9,8},{10,9... | collective-permute-start | bytes 1572872 | tf_op jit(solution)/shard_map/ppermute | solution.py:39
  24.2 4.4 %collective-permute-start.2 = (f32[2,2,32,128]{3,2,1,0:T(8,128)S(1)}, f32[2,2,32,128]{3,2,1,0:T(8,128)S(1)}, u32[]{:S(2)}, u32[]{:S(2)}) collective-permute-start(f32[2,2,32,128]{3,2,1,0:T(8,128)S(1)} %dynamic-slice_bitcast_fusion), channel_id=1, source_target_pairs={{0,64},{16,80},{32,96},{48,112},{64,0},{80,16},{96,32},{112,48},{1... | collective-permute-start | bytes 196616 | tf_op jit(solution)/shard_map/ppermute | solution.py:43
  29.2 5.4 %collective-permute-start.3 = (f32[2,32,128]{2,1,0:T(8,128)S(1)}, f32[2,32,128]{2,1,0:T(8,128)S(1)}, u32[]{:S(2)}, u32[]{:S(2)}) collective-permute-start(f32[2,32,128]{2,1,0:T(8,128)S(1)} %get-tuple-element.78), channel_id=1, source_target_pairs={{0,128},{16,144},{32,160},{48,176},{64,192},{80,208},{96,224},{112... | collective-permute-start | bytes 98312 | tf_op jit(solution)/shard_map/ppermute | solution.py:43
  41.9 27.9 %collective-permute-start.4 = (bf16[256,1024]{1,0:T(8,128)(2,1)}, bf16[256,1024]{1,0:T(8,128)(2,1)}, u32[]{:S(2)}, u32[]{:S(2)}) collective-permute-start(bf16[256,1024]{1,0:T(8,128)(2,1)} %get-tuple-element.49), channel_id=1, source_target_pairs={{0,4},{1,5},{2,6},{3,7},{4,8},{5,9},{6,10},{7,11},{8,12},{9,13},{1... | collective-permute-start | bytes 1572872 | tf_op jit(solution)/shard_map/ppermute | solution.py:48
  44.0 28.9 %collective-permute-start.5 = (bf16[256,1024]{1,0:T(8,128)(2,1)}, bf16[256,1024]{1,0:T(8,128)(2,1)}, u32[]{:S(2)}, u32[]{:S(2)}) collective-permute-start(bf16[256,1024]{1,0:T(8,128)(2,1)} %get-tuple-element.50), channel_id=1, source_target_pairs={{0,8},{1,9},{2,10},{3,11},{4,12},{5,13},{6,14},{7,15},{8,0},{9,1},... | collective-permute-start | bytes 1572872 | tf_op jit(solution)/shard_map/ppermute | solution.py:48
  46.6 23.2 %copy-start.9 = (f32[2,32,128]{2,1,0:T(8,128)S(1)}, f32[2,32,128]{2,1,0:T(8,128)}, u32[]{:S(2)}) copy-start(f32[2,32,128]{2,1,0:T(8,128)} %get-tuple-element.47.refs_9_) | copy-start | bytes 98308
  46.6 26.3 %collective-permute-start.6 = (bf16[256,1024]{1,0:T(8,128)(2,1)}, bf16[256,1024]{1,0:T(8,128)(2,1)}, u32[]{:S(2)}, u32[]{:S(2)}) collective-permute-start(bf16[256,1024]{1,0:T(8,128)(2,1)} %get-tuple-element.51), channel_id=1, source_target_pairs={{0,12},{1,13},{2,14},{3,15},{4,0},{5,1},{6,2},{7,3},{8,4},{9,5},{1... | collective-permute-start | bytes 1572872 | tf_op jit(solution)/shard_map/ppermute | solution.py:48
  55.0 27.5 %collective-permute-start.9 = (bf16[512,512]{1,0:T(8,128)(2,1)}, bf16[512,512]{1,0:T(8,128)(2,1)S(1)}, u32[]{:S(2)}, u32[]{:S(2)}) collective-permute-start(bf16[512,512]{1,0:T(8,128)(2,1)} %get-tuple-element.52), channel_id=1, source_target_pairs={{0,1},{1,2},{2,3},{3,0},{4,5},{5,6},{6,7},{7,4},{8,9},{9,10},{10,1... | collective-permute-start | bytes 1572872 | tf_op jit(solution)/shard_map/ppermute | solution.py:39
  67.2 22.2 %collective-permute-start.10 = (bf16[512,512]{1,0:T(8,128)(2,1)}, bf16[512,512]{1,0:T(8,128)(2,1)S(1)}, u32[]{:S(2)}, u32[]{:S(2)}) collective-permute-start(bf16[512,512]{1,0:T(8,128)(2,1)} %get-tuple-element.53), channel_id=1, source_target_pairs={{0,3},{1,0},{2,1},{3,2},{4,7},{5,4},{6,5},{7,6},{8,11},{9,8},{10,9... | collective-permute-start | bytes 1572872 | tf_op jit(solution)/shard_map/ppermute | solution.py:39
  69.9 25.1 %collective-permute-start.18 = (f32[2,32,128]{2,1,0:T(8,128)S(1)}, f32[2,32,128]{2,1,0:T(8,128)S(1)}, u32[]{:S(2)}, u32[]{:S(2)}) collective-permute-start(f32[2,32,128]{2,1,0:T(8,128)S(1)} %copy-done.9), channel_id=1, source_target_pairs={{0,128},{16,144},{32,160},{48,176},{64,192},{80,208},{96,224},{112... | collective-permute-start | bytes 98312 | tf_op jit(solution)/shard_map/ppermute | solution.py:43
  92.1 12.8 %collective-permute-start.14 = (bf16[384,512]{1,0:T(8,128)(2,1)}, bf16[384,512]{1,0:T(8,128)(2,1)S(1)}, u32[]{:S(2)}, u32[]{:S(2)}) collective-permute-start(bf16[384,512]{1,0:T(8,128)(2,1)} %get-tuple-element.63), channel_id=1, source_target_pairs={{0,3},{1,0},{2,1},{3,2},{4,7},{5,4},{6,5},{7,6},{8,11},{9,8},{10,9... | collective-permute-start | bytes 1179656 | tf_op jit(solution)/shard_map/ppermute | solution.py:39
  92.1 12.9 %collective-permute-start.15 = (bf16[384,512]{1,0:T(8,128)(2,1)}, bf16[384,512]{1,0:T(8,128)(2,1)S(1)}, u32[]{:S(2)}, u32[]{:S(2)}) collective-permute-start(bf16[384,512]{1,0:T(8,128)(2,1)} %get-tuple-element.64), channel_id=1, source_target_pairs={{0,1},{1,2},{2,3},{3,0},{4,5},{5,6},{6,7},{7,4},{8,9},{9,10},{10,1... | collective-permute-start | bytes 1179656 | tf_op jit(solution)/shard_map/ppermute | solution.py:39
  95.0 9.8 %collective-permute-start.19 = (f32[4,32,128]{2,1,0:T(8,128)S(1)}, f32[4,32,128]{2,1,0:T(8,128)S(1)}, u32[]{:S(2)}, u32[]{:S(2)}) collective-permute-start(f32[4,32,128]{2,1,0:T(8,128)S(1)} %pad_maximum_fusion.1), channel_id=1, source_target_pairs={{0,64},{16,80},{32,96},{48,112},{64,0},{80,16},{96,32},{112,48},{1... | collective-permute-start | bytes 196616 | tf_op jit(solution)/shard_map/ppermute | solution.py:43
  102.5 6.6 %collective-permute-start.11 = (bf16[256,512]{1,0:T(8,128)(2,1)}, bf16[256,512]{1,0:T(8,128)(2,1)S(1)}, u32[]{:S(2)}, u32[]{:S(2)}) collective-permute-start(bf16[256,512]{1,0:T(8,128)(2,1)} %get-tuple-element.56), channel_id=1, source_target_pairs={{0,12},{1,13},{2,14},{3,15},{4,0},{5,1},{6,2},{7,3},{8,4},{9,5},{1... | collective-permute-start | bytes 786440 | tf_op jit(solution)/shard_map/ppermute | solution.py:48
  103.5 8.6 %collective-permute-start.12 = (bf16[256,512]{1,0:T(8,128)(2,1)}, bf16[256,512]{1,0:T(8,128)(2,1)S(1)}, u32[]{:S(2)}, u32[]{:S(2)}) collective-permute-start(bf16[256,512]{1,0:T(8,128)(2,1)} %get-tuple-element.57), channel_id=1, source_target_pairs={{0,8},{1,9},{2,10},{3,11},{4,12},{5,13},{6,14},{7,15},{8,0},{9,1},... | collective-permute-start | bytes 786440 | tf_op jit(solution)/shard_map/ppermute | solution.py:48
  104.8 9.6 %collective-permute-start.13 = (bf16[256,512]{1,0:T(8,128)(2,1)}, bf16[256,512]{1,0:T(8,128)(2,1)S(1)}, u32[]{:S(2)}, u32[]{:S(2)}) collective-permute-start(bf16[256,512]{1,0:T(8,128)(2,1)} %get-tuple-element.58), channel_id=1, source_target_pairs={{0,4},{1,5},{2,6},{3,7},{4,8},{5,9},{6,10},{7,11},{8,12},{9,13},{1... | collective-permute-start | bytes 786440 | tf_op jit(solution)/shard_map/ppermute | solution.py:48
  104.8 12.3 %copy-start.7 = (f32[8,32,128]{2,1,0:T(8,128)}, f32[8,32,128]{2,1,0:T(8,128)S(1)}, u32[]{:S(2)}) copy-start(f32[8,32,128]{2,1,0:T(8,128)S(1)} %constant_dynamic-update-slice_fusion.near) | copy-start | bytes 393220
  104.9 12.3 %collective-permute-start.20 = (f32[8,32,128]{2,1,0:T(8,128)S(1)}, f32[8,32,128]{2,1,0:T(8,128)S(1)}, u32[]{:S(2)}, u32[]{:S(2)}) collective-permute-start(f32[8,32,128]{2,1,0:T(8,128)S(1)} %constant_dynamic-update-slice_fusion.near), channel_id=1, source_target_pairs={{0,16},{16,0},{32,48},{48,32},{64,80},{80,64},{96,112},{112,96},{1... | collective-permute-start | bytes 393224 | tf_op jit(solution)/shard_map/ppermute | solution.py:43
  107.6 13.6 %collective-permute-start.16 = (bf16[128,512]{1,0:T(8,128)(2,1)}, bf16[128,512]{1,0:T(8,128)(2,1)S(1)}, u32[]{:S(2)}, u32[]{:S(2)}) collective-permute-start(bf16[128,512]{1,0:T(8,128)(2,1)} %get-tuple-element.67), channel_id=1, source_target_pairs={{0,3},{1,0},{2,1},{3,2},{4,7},{5,4},{6,5},{7,6},{8,11},{9,8},{10,9... | collective-permute-start | bytes 393224 | tf_op jit(solution)/shard_map/ppermute | solution.py:39
  109.1 12.1 %collective-permute-start.17 = (bf16[128,512]{1,0:T(8,128)(2,1)}, bf16[128,512]{1,0:T(8,128)(2,1)S(1)}, u32[]{:S(2)}, u32[]{:S(2)}) collective-permute-start(bf16[128,512]{1,0:T(8,128)(2,1)} %get-tuple-element.68), channel_id=1, source_target_pairs={{0,1},{1,2},{2,3},{3,0},{4,5},{5,6},{6,7},{7,4},{8,9},{9,10},{10,1... | collective-permute-start | bytes 393224 | tf_op jit(solution)/shard_map/ppermute | solution.py:39
  (14 other events, 37.4 us)

commit v5 on v4

--- a/solution.py
+++ b/solution.py
@@ -252,47 +252,68 @@
     )(keep_left, keep_right, from_left, from_right, left, right)
 
 
-def chunk_weights(chunk, own, before, far_top, far_bottom, after):
-    first, width = CHUNKS[chunk]
-    rows = slice(first, first + width)
-    half = far_top.shape[0]
-    far = []
-    if first < half:
-        far.append(far_top[first : min(first + width, half)])
-    if first + width > half:
-        far.append(far_bottom[max(first - half, 0) : first + width - half])
-    return jnp.concatenate([own[rows], before[rows]] + far + [after[rows]], axis=0)
-
-
-def values_kernel(place, arrived, *refs):
-    later, weights = refs[:RING], refs[RING : RING + 5]
+def near_values_kernel(place, arrived, *refs):
+    later, (own, before, after) = refs[:RING], refs[RING : RING + 3]
+    out = refs[-1]
+    (_, early), (start, late) = CHUNKS
+    for k in range(RING):
+        y = lax.rem(place[0] + RING - k, RING)
+        total = jnp.zeros(out.shape[1:], F32)
+        for kz, weights in ((0, own), (1, before), (3, after)):
+            rows = arrived[y, :, kz * early : (kz + 1) * early]
+            total += jnp.dot(rows, weights[:start], preferred_element_type=F32)
+            rows = later[k][:, kz * late : (kz + 1) * late]
+            total += jnp.dot(rows, weights[start:], preferred_element_type=F32)
+        out[k] = total
+
+
+def near_values(place, arrived, later, weights, needed):
+    tokens, columns = arrived.shape[1], weights[0].shape[1]
+    shape = (RING, tokens, columns)
+    return pl.pallas_call(
+        near_values_kernel,
+        grid=(1,),
+        out_shape=pltpu.HBM(shape, F32),
+        in_specs=[scalars(), pl.BlockSpec((RING, tokens, RING * CHUNKS[0][1]), lambda i: (0, 0, 0))]
+        + [pl.BlockSpec(w.shape, lambda i: (0, 0)) for w in (*later, *weights)]
+        + [pl.BlockSpec(memory_space=pl.ANY)] * len(needed),
+        out_specs=pl.BlockSpec(shape, lambda i: (0, 0, 0)),
+        compiler_params=params_of(),
+        cost_estimate=COST,
+        name="near_values",
+    )(place, arrived, *later, *weights, *needed)
+
+
+def far_values_kernel(place, total, arrived, *refs):
+    later, (top, bottom) = refs[:RING], refs[RING : RING + 2]
     outs = refs[-RING:]
-    first_weights, later_weights = chunk_weights(0, *weights), chunk_weights(1, *weights)
     for k in (2, 1, 3, 0):
         y = lax.rem(place[0] + RING - k, RING)
-        total = jnp.dot(arrived[y], first_weights, preferred_element_type=F32)
-        total += jnp.dot(later[k][...], later_weights, preferred_element_type=F32)
-        outs[k][...] = total.astype(outs[k].dtype)
-
-
-def values_partial(place, arrived, later, weights, needed):
-    tokens = arrived.shape[1]
-    columns = weights[0].shape[1]
+        share = total[k] + jnp.dot(arrived[y], top[...], preferred_element_type=F32)
+        share += jnp.dot(later[k][...], bottom[...], preferred_element_type=F32)
+        outs[k][...] = share.astype(outs[k].dtype)
+
+
+def far_values(place, total, arrived, later, top, bottom):
+    tokens, columns = total.shape[1:]
+    (_, early), (_, late) = CHUNKS
     shape = (tokens, columns)
     return pl.pallas_call(
-        values_kernel,
+        far_values_kernel,
         grid=(1,),
         out_shape=[pltpu.HBM(shape, F32 if k == 0 else BF16) for k in range(RING)],
-        in_specs=[scalars(), pl.BlockSpec((RING, tokens, RING * CHUNKS[0][1]), lambda i: (0, 0, 0))]
-        + [pl.BlockSpec(w.shape, lambda i: (0, 0)) for w in (*later, *weights[:2])]
-        + [pl.BlockSpec((weights[0].shape[0] // 2, columns), lambda i: (1, 0))] * 2
-        + [pl.BlockSpec(weights[4].shape, lambda i: (0, 0))]
-        + [pl.BlockSpec(memory_space=pl.ANY)] * len(needed),
+        in_specs=[
+            scalars(),
+            pl.BlockSpec(total.shape, lambda i: (0, 0, 0)),
+            pl.BlockSpec((RING, tokens, early), lambda i: (0, 0, 2)),
+        ]
+        + [pl.BlockSpec((tokens, late), lambda i: (0, 2))] * RING
+        + [pl.BlockSpec((early, columns), lambda i: (1, 0)), pl.BlockSpec((late, columns), lambda i: (1, 0))],
         out_specs=[pl.BlockSpec(shape, lambda i: (0, 0))] * RING,
         compiler_params=params_of(),
         cost_estimate=COST,
-        name="values_partial",
-    )(place, arrived, *later, *weights, *needed)
+        name="far_values",
+    )(place, total, arrived, *later, top, bottom)
 
 
 def fragment_kernel(place, weights, anchor, moment, after, keep, send, state):
@@ -503,7 +524,6 @@
 
     own_0, left, right, keep_left, keep_right = first_gradient(arrived, before, after)
     left_0, right_0 = shift_z(left, -1), shift_z(right, 1)
-    ring_weights = [weights_half, before, right_0, left_0, after]
     own_1, left, right, next_left, next_right = later_gradient(place, later, arrived)
     left, right = join(keep_left, keep_right, left_0, right_0, left, right)
     near = jnp.concatenate([near, swap_rep(near, 8)])
@@ -514,7 +534,8 @@
     last_left, last_right = shift_z(last_left, -1), shift_z(last_right, 1)
     pieces = ([own_0, left_0, right_0, left_1, right_1], [own_1, left_1, right_1, last_left, last_right])
 
-    partial = values_partial(place, arrived, later, ring_weights, (own_1,))
+    partial = near_values(place, arrived, later, (weights_half, before, after), (own_1,))
+    partial = far_values(place, partial, arrived, later, right_0, left_0)
     value_rows = values_sum(factor, [partial[0]] + [shift_y(partial[k], -k) for k in (1, 2, 3)])
 
     clock = inner_step.astype(F32)

time: 126 us -> 130 us (1.032)
  the two profiles are of different devices: /device:TPU:32 before, /device:TPU:2 now
where the time goes in v5:
time: 130 us; the launch traced here: 128 us
  starting transfers between devices  54.4 us (42%)
  Pallas kernels  43.7 us (34%)
  waiting for transfers between devices  16.6 us (13%)
  local copies, waits for them, and re-layouts  6.77 us (5%)
  other arithmetic  3.89 us (3%)
  between operations  2.39 us (2%)
    ppermute x8, starting transfers between devices, shift_z(): return lax.ppermute(array, 'shard', pairs)  33.8 us
    ppermute x6, starting transfers between devices, shift_y(): return lax.ppermute(array, 'shard', pairs)  8.22 us
    ppermute x8, waiting for transfers between devices, shift_z(): return lax.ppermute(array, 'shard', pairs)  8.07 us
    ppermute x7, waiting for transfers between devices, swap_rep(): return lax.ppermute(array, 'rep', [(r, r ^ bit) for r in range(16)])  8.03 us
    ppermute x7, starting transfers between devices, swap_rep(): return lax.ppermute(array, 'rep', [(r, r ^ bit) for r in range(16)])  7.59 us
    pallas_call x2, Pallas kernels, adam(): pl.pallas_call(functools.partial(adam_kernel, chunk), grid=(1,), out_shap...  6.82 us
    pallas_call x1, Pallas kernels, near_values(): pl.pallas_call(near_values_kernel, grid=(1,), out_shape=pltpu.HBM(shape,...  5.78 us
    unnamed x36, local copies, waits for them, and re-layouts  5.5 us
  transfers between devices with their start and end apart: 22, of which 7 were waited for; matrix products, arithmetic and copies ran while one was open for 4% of the time, Pallas kernels for 28%

profile of v5, /device:TPU:2, one launch (start us, length us, event | category | flops | bytes accessed | tf_op | source)
XLA Modules:
  0.0 127.7 jit_solution(11257662780755038442)
XLA Ops:
  1.9 4.8 %first_pack.1 = (bf16[4,256,1536]{2,1,0:T(8,128)(2,1)}, f32[256,1]{1,0:T(8,128)}) custom-call(s32[4]{0:T(128)} %pad_add_fusion.place, bf16[256,8192]{1,0:T(8,128)(2,1)} %bitcast.32, f32[1,8192]{1,0:T(1,128)} %bitcast.47, bf16[256,512]{1,0:T(8,128)(2,1)} %bitcast.54), custom_call_target="tpu_custom_call" | custom-call | flops 1 | bytes 1 | tf_op jit(solution)/shard_map/first_pack/pallas_call | solution.py:85
  6.7 4.8 %all-to-all-start = ((bf16[4,256,1536]{2,1,0:T(8,128)(2,1)}), bf16[4,256,1536]{2,1,0:T(8,128)(2,1)}, u32[]{:S(2)}, u32[]{:S(2)}) async-start(bf16[4,256,1536]{2,1,0:T(8,128)(2,1)} %get-tuple-element.42), calls=%async_computation | async-start | bytes 6291456 | tf_op jit(solution)/shard_map/all_to_all | solution.py:34
  19.7 3.3 %collective-permute-start.7 = (bf16[512,512]{1,0:T(8,128)(2,1)}, bf16[512,512]{1,0:T(8,128)(2,1)S(1)}, u32[]{:S(2)}, u32[]{:S(2)}) collective-permute-start(bf16[512,512]{1,0:T(8,128)(2,1)} %bitcast_convert_fusion.refs_4_), channel_id=1, source_target_pairs={{0,1},{1,2},{2,3},{3,0},{4,5},{5,6},{6,7},{7,4},{8,9},{9,10},{10,1... | collective-permute-start | bytes 1572872 | tf_op jit(solution)/shard_map/ppermute | solution.py:39
  23.0 2.1 %collective-permute-start.8 = (bf16[512,512]{1,0:T(8,128)(2,1)}, bf16[512,512]{1,0:T(8,128)(2,1)S(1)}, u32[]{:S(2)}, u32[]{:S(2)}) collective-permute-start(bf16[512,512]{1,0:T(8,128)(2,1)} %bitcast_convert_fusion.refs_4_), channel_id=1, source_target_pairs={{0,3},{1,0},{2,1},{3,2},{4,7},{5,4},{6,5},{7,6},{8,11},{9,8},{10,9... | collective-permute-start | bytes 1572872 | tf_op jit(solution)/shard_map/ppermute | solution.py:39
  25.8 3.7 %collective-permute-done.2 = f32[2,2,32,128]{3,2,1,0:T(8,128)S(1)} collective-permute-done((f32[2,2,32,128]{3,2,1,0:T(8,128)S(1)}, f32[2,2,32,128]{3,2,1,0:T(8,128)S(1)}, u32[]{:S(2)}, u32[]{:S(2)}) %collective-permute-start.2) | collective-permute-done | bytes 65568 | tf_op jit(solution)/shard_map/ppermute | solution.py:43
  30.2 2.1 %collective-permute-start.3 = (f32[2,32,128]{2,1,0:T(8,128)S(1)}, f32[2,32,128]{2,1,0:T(8,128)S(1)}, u32[]{:S(2)}, u32[]{:S(2)}) collective-permute-start(f32[2,32,128]{2,1,0:T(8,128)S(1)} %get-tuple-element.78), channel_id=1, source_target_pairs={{0,128},{16,144},{32,160},{48,176},{64,192},{80,208},{96,224},{112... | collective-permute-start | bytes 98312 | tf_op jit(solution)/shard_map/ppermute | solution.py:43
  32.9 2.7 %collective-permute-done.3.other = f32[2,32,128]{2,1,0:T(8,128)S(1)} collective-permute-done((f32[2,32,128]{2,1,0:T(8,128)S(1)}, f32[2,32,128]{2,1,0:T(8,128)S(1)}, u32[]{:S(2)}, u32[]{:S(2)}) %collective-permute-start.3) | collective-permute-done | bytes 32800 | tf_op jit(solution)/shard_map/ppermute | solution.py:43
  37.8 5.0 %later_pack.1 = (bf16[256,1024]{1,0:T(8,128)(2,1)}, bf16[256,1024]{1,0:T(8,128)(2,1)}, bf16[256,1024]{1,0:T(8,128)(2,1)}, bf16[256,1024]{1,0:T(8,128)(2,1)}) custom-call(s32[4]{0:T(128)} %pad_add_fusion.place, bf16[256,8192]{1,0:T(8,128)(2,1)} %bitcast.33, bf16[256,8192]{1,0:T(8,128)(2,1)} %bitcast.34, bf16[256,8192]{1,0:T(8,128)(2,1)} %bitcast.35, ...), custom_call_target="tpu_custom_call" | custom-call | flops 1 | bytes 1 | tf_op jit(solution)/shard_map/later_pack/pallas_call | solution.py:126
  44.8 2.7 %collective-permute-start.5 = (bf16[256,1024]{1,0:T(8,128)(2,1)}, bf16[256,1024]{1,0:T(8,128)(2,1)}, u32[]{:S(2)}, u32[]{:S(2)}) collective-permute-start(bf16[256,1024]{1,0:T(8,128)(2,1)} %get-tuple-element.50), channel_id=1, source_target_pairs={{0,8},{1,9},{2,10},{3,11},{4,12},{5,13},{6,14},{7,15},{8,0},{9,1},... | collective-permute-start | bytes 1572872 | tf_op jit(solution)/shard_map/ppermute | solution.py:48
  51.9 4.3 %first_gradient.1 = (f32[256,512]{1,0:T(8,128)}, bf16[512,512]{1,0:T(8,128)(2,1)}, bf16[512,512]{1,0:T(8,128)(2,1)}, f32[128,512]{1,0:T(8,128)}, f32[128,512]{1,0:T(8,128)}) custom-call(bf16[4,256,1536]{2,1,0:T(8,128)(2,1)} %all-to-all-done.refs_4_.arrived.normed.cot, bf16[4,256,1536]{2,1,0:T(8,128)(2,1)} %all-to-all-done.refs_4_.arrived.normed.cot, ...), custom_call_target="tpu_custom_call" | custom-call | flops 1 | bytes 1 | tf_op jit(solution)/shard_map/first_gradient/pallas_call | solution.py:182
  56.2 2.4 %collective-permute-start.9 = (bf16[512,512]{1,0:T(8,128)(2,1)}, bf16[512,512]{1,0:T(8,128)(2,1)S(1)}, u32[]{:S(2)}, u32[]{:S(2)}) collective-permute-start(bf16[512,512]{1,0:T(8,128)(2,1)} %get-tuple-element.53), channel_id=1, source_target_pairs={{0,1},{1,2},{2,3},{3,0},{4,5},{5,6},{6,7},{7,4},{8,9},{9,10},{10,1... | collective-permute-start | bytes 1572872 | tf_op jit(solution)/shard_map/ppermute | solution.py:39
  58.7 10.6 %collective-permute-start.10 = (bf16[512,512]{1,0:T(8,128)(2,1)}, bf16[512,512]{1,0:T(8,128)(2,1)S(1)}, u32[]{:S(2)}, u32[]{:S(2)}) collective-permute-start(bf16[512,512]{1,0:T(8,128)(2,1)} %get-tuple-element.54), channel_id=1, source_target_pairs={{0,3},{1,0},{2,1},{3,2},{4,7},{5,4},{6,5},{7,6},{8,11},{9,8},{10,9... | collective-permute-start | bytes 1572872 | tf_op jit(solution)/shard_map/ppermute | solution.py:39
  69.3 2.2 %collective-permute-start.18 = (f32[2,32,128]{2,1,0:T(8,128)S(1)}, f32[2,32,128]{2,1,0:T(8,128)S(1)}, u32[]{:S(2)}, u32[]{:S(2)}) collective-permute-start(f32[2,32,128]{2,1,0:T(8,128)S(1)} %copy-done.10), channel_id=1, source_target_pairs={{0,128},{16,144},{32,160},{48,176},{64,192},{80,208},{96,224},{112... | collective-permute-start | bytes 98312 | tf_op jit(solution)/shard_map/ppermute | solution.py:43
  71.9 4.0 %later_gradient.1 = (f32[256,512]{1,0:T(8,128)}, bf16[384,512]{1,0:T(8,128)(2,1)}, bf16[384,512]{1,0:T(8,128)(2,1)}, f32[128,512]{1,0:T(8,128)}, f32[128,512]{1,0:T(8,128)}) custom-call(s32[4]{0:T(128)} %pad_add_fusion.place, bf16[256,1024]{1,0:T(8,128)(2,1)} %get-tuple-element.48.refs_0_, bf16[256,1024]{1,0:T(8,128)(2,1)} %copy-done.3, ...), custom_call_target="tpu_custom_call" | custom-call | flops 1 | bytes 1 | tf_op jit(solution)/shard_map/later_gradient/pallas_call | solution.py:217
  76.0 6.1 %collective-permute-done.9.refs_4_.from_right.right = bf16[512,512]{1,0:T(8,128)(2,1)S(1)} collective-permute-done((bf16[512,512]{1,0:T(8,128)(2,1)}, bf16[512,512]{1,0:T(8,128)(2,1)S(1)}, u32[]{:S(2)}, u32[]{:S(2)}) %collective-permute-start.9) | collective-permute-done | bytes 524320 | tf_op jit(solution)/shard_map/ppermute | solution.py:39
  84.9 3.2 %collective-permute-start.14 = (bf16[384,512]{1,0:T(8,128)(2,1)}, bf16[384,512]{1,0:T(8,128)(2,1)S(1)}, u32[]{:S(2)}, u32[]{:S(2)}) collective-permute-start(bf16[384,512]{1,0:T(8,128)(2,1)} %get-tuple-element.63), channel_id=1, source_target_pairs={{0,3},{1,0},{2,1},{3,2},{4,7},{5,4},{6,5},{7,6},{8,11},{9,8},{10,9... | collective-permute-start | bytes 1179656 | tf_op jit(solution)/shard_map/ppermute | solution.py:39
  88.1 6.4 %collective-permute-start.15 = (bf16[384,512]{1,0:T(8,128)(2,1)}, bf16[384,512]{1,0:T(8,128)(2,1)S(1)}, u32[]{:S(2)}, u32[]{:S(2)}) collective-permute-start(bf16[384,512]{1,0:T(8,128)(2,1)} %get-tuple-element.64), channel_id=1, source_target_pairs={{0,1},{1,2},{2,3},{3,0},{4,5},{5,6},{6,7},{7,4},{8,9},{9,10},{10,1... | collective-permute-start | bytes 1179656 | tf_op jit(solution)/shard_map/ppermute | solution.py:39
  94.5 5.8 %near_values.1.total = f32[4,256,512]{2,1,0:T(8,128)} custom-call(s32[4]{0:T(128)} %pad_add_fusion.place, bf16[4,256,1536]{2,1,0:T(8,128)(2,1)} %all-to-all-done.refs_4_.arrived.normed.cot, bf16[256,1024]{1,0:T(8,128)(2,1)} %get-tuple-element.48.refs_0_, bf16[256,1024]{1,0:T(8,128)(2,1)} %copy-done.3, bf16[256,1024]{1,0:T(8,128)(2,1)} %collective-permute-done.5.refs_2_, ...), custom_call_target="tpu_custom_call" | custom-call | flops 1 | bytes 1 | tf_op jit(solution)/shard_map/near_values/pallas_call | solution.py:273
  100.8 3.5 %far_values.1 = (f32[256,512]{1,0:T(8,128)}, bf16[256,512]{1,0:T(8,128)(2,1)}, bf16[256,512]{1,0:T(8,128)(2,1)}, bf16[256,512]{1,0:T(8,128)(2,1)}) custom-call(s32[4]{0:T(128)} %pad_add_fusion.place, f32[4,256,512]{2,1,0:T(8,128)} %near_values.1.total, bf16[4,256,1536]{2,1,0:T(8,128)(2,1)} %all-to-all-done.refs_4_.arrived.normed.cot, ...), custom_call_target="tpu_custom_call" | custom-call | flops 1 | bytes 1 | tf_op jit(solution)/shard_map/far_values/pallas_call | solution.py:301
  109.3 2.2 %collective-permute-start.16 = (bf16[128,512]{1,0:T(8,128)(2,1)}, bf16[128,512]{1,0:T(8,128)(2,1)S(1)}, u32[]{:S(2)}, u32[]{:S(2)}) collective-permute-start(bf16[128,512]{1,0:T(8,128)(2,1)} %get-tuple-element.67), channel_id=1, source_target_pairs={{0,3},{1,0},{2,1},{3,2},{4,7},{5,4},{6,5},{7,6},{8,11},{9,8},{10,9... | collective-permute-start | bytes 393224 | tf_op jit(solution)/shard_map/ppermute | solution.py:39
  111.5 3.6 %collective-permute-start.17 = (bf16[128,512]{1,0:T(8,128)(2,1)}, bf16[128,512]{1,0:T(8,128)(2,1)S(1)}, u32[]{:S(2)}, u32[]{:S(2)}) collective-permute-start(bf16[128,512]{1,0:T(8,128)(2,1)} %get-tuple-element.68), channel_id=1, source_target_pairs={{0,1},{1,2},{2,3},{3,0},{4,5},{5,6},{6,7},{7,4},{8,9},{9,10},{10,1... | collective-permute-start | bytes 393224 | tf_op jit(solution)/shard_map/ppermute | solution.py:39
  117.4 2.1 %values_sum.1 = bf16[256,512]{1,0:T(8,128)(2,1)} custom-call(f32[256,512]{1,0:T(8,128)} %get-tuple-element.55.own, bf16[256,512]{1,0:T(8,128)(2,1)} %copy-done.11, bf16[256,512]{1,0:T(8,128)(2,1)} %copy-done.12, bf16[256,512]{1,0:T(8,128)(2,1)} %copy-done.13), custom_call_target="tpu_custom_call" | custom-call | flops 1 | bytes 1 | tf_op jit(solution)/shard_map/values_sum/pallas_call | solution.py:413
  120.2 3.4 %adam.2 = (f32[512,512]{1,0:T(8,128)}, f32[512,512]{1,0:T(8,128)}, f32[512,512]{1,0:T(8,128)}) custom-call(s32[4]{0:T(128)} %pad_add_fusion.place, f32[4]{0:T(128)} %pad_maximum_fusion.2.rates, f32[512,512]{1,0:T(8,128)} %bitcast.38, f32[512,512]{1,0:T(8,128)} %bitcast.40, f32[512,512]{1,0:T(8,128)} %bitcast.42, f32[256,512]{1,0:T(8,128)} %get-tuple-element.69.own, ...), custom_call_target="tpu_custom_call" | custom-call | flops 1 | bytes 1 | tf_op jit(solution)/shard_map/adam/pallas_call | solution.py:464
  124.3 3.4 %adam.3 = (f32[512,512]{1,0:T(8,128)}, f32[512,512]{1,0:T(8,128)}, f32[512,512]{1,0:T(8,128)}) custom-call(s32[4]{0:T(128)} %pad_add_fusion.place, f32[4]{0:T(128)} %pad_maximum_fusion.2.rates, f32[512,512]{1,0:T(8,128)} %bitcast.39, f32[512,512]{1,0:T(8,128)} %bitcast.41, ...), custom_call_target="tpu_custom_call", output_to_operand_aliasing={{0}: (12, {}), {1}: (13, {}), {2}: (14, {})} | custom-call | flops 1 | bytes 1 | tf_op jit(solution)/shard_map/adam/pallas_call | solution.py:464
  (81 shorter events, 30.8 us)
Async XLA Ops:
  6.7 44.2 %all-to-all-start = ((bf16[4,256,1536]{2,1,0:T(8,128)(2,1)}), bf16[4,256,1536]{2,1,0:T(8,128)(2,1)}, u32[]{:S(2)}, u32[]{:S(2)}) async-start(bf16[4,256,1536]{2,1,0:T(8,128)(2,1)} %get-tuple-element.42), calls=%async_computation | async-start | bytes 6291456 | tf_op jit(solution)/shard_map/all_to_all | solution.py:34
  13.6 1.6 %collective-permute-start = (f32[8,32,128]{2,1,0:T(8,128)}, f32[8,32,128]{2,1,0:T(8,128)S(1)}, u32[]{:S(2)}, u32[]{:S(2)}) collective-permute-start(f32[8,32,128]{2,1,0:T(8,128)} %get-tuple-element.45), channel_id=1, source_target_pairs={{0,16},{16,0},{32,48},{48,32},{64,80},{80,64},{96,112},{112,96},{1... | collective-permute-start | bytes 393224 | tf_op jit(solution)/shard_map/ppermute | solution.py:43
  16.8 8.3 %collective-permute-start.1 = (f32[10,32,128]{2,1,0:T(8,128)S(1)}, f32[10,32,128]{2,1,0:T(8,128)S(1)}, u32[]{:S(2)}, u32[]{:S(2)}) collective-permute-start(f32[10,32,128]{2,1,0:T(8,128)S(1)} %pad_maximum_fusion), channel_id=1, source_target_pairs={{0,32},{16,48},{32,0},{48,16},{64,96},{80,112},{96,64},{112,80},{1... | collective-permute-start | bytes 491528 | tf_op jit(solution)/shard_map/ppermute | solution.py:43
  19.7 31.2 %collective-permute-start.7 = (bf16[512,512]{1,0:T(8,128)(2,1)}, bf16[512,512]{1,0:T(8,128)(2,1)S(1)}, u32[]{:S(2)}, u32[]{:S(2)}) collective-permute-start(bf16[512,512]{1,0:T(8,128)(2,1)} %bitcast_convert_fusion.refs_4_), channel_id=1, source_target_pairs={{0,1},{1,2},{2,3},{3,0},{4,5},{5,6},{6,7},{7,4},{8,9},{9,10},{10,1... | collective-permute-start | bytes 1572872 | tf_op jit(solution)/shard_map/ppermute | solution.py:39
  23.0 27.9 %collective-permute-start.8 = (bf16[512,512]{1,0:T(8,128)(2,1)}, bf16[512,512]{1,0:T(8,128)(2,1)S(1)}, u32[]{:S(2)}, u32[]{:S(2)}) collective-permute-start(bf16[512,512]{1,0:T(8,128)(2,1)} %bitcast_convert_fusion.refs_4_), channel_id=1, source_target_pairs={{0,3},{1,0},{2,1},{3,2},{4,7},{5,4},{6,5},{7,6},{8,11},{9,8},{10,9... | collective-permute-start | bytes 1572872 | tf_op jit(solution)/shard_map/ppermute | solution.py:39
  25.2 4.4 %collective-permute-start.2 = (f32[2,2,32,128]{3,2,1,0:T(8,128)S(1)}, f32[2,2,32,128]{3,2,1,0:T(8,128)S(1)}, u32[]{:S(2)}, u32[]{:S(2)}) collective-permute-start(f32[2,2,32,128]{3,2,1,0:T(8,128)S(1)} %dynamic-slice_bitcast_fusion), channel_id=1, source_target_pairs={{0,64},{16,80},{32,96},{48,112},{64,0},{80,16},{96,32},{112,48},{1... | collective-permute-start | bytes 196616 | tf_op jit(solution)/shard_map/ppermute | solution.py:43
  30.2 5.4 %collective-permute-start.3 = (f32[2,32,128]{2,1,0:T(8,128)S(1)}, f32[2,32,128]{2,1,0:T(8,128)S(1)}, u32[]{:S(2)}, u32[]{:S(2)}) collective-permute-start(f32[2,32,128]{2,1,0:T(8,128)S(1)} %get-tuple-element.78), channel_id=1, source_target_pairs={{0,128},{16,144},{32,160},{48,176},{64,192},{80,208},{96,224},{112... | collective-permute-start | bytes 98312 | tf_op jit(solution)/shard_map/ppermute | solution.py:43
  42.8 26.5 %collective-permute-start.4 = (bf16[256,1024]{1,0:T(8,128)(2,1)}, bf16[256,1024]{1,0:T(8,128)(2,1)S(1)}, u32[]{:S(2)}, u32[]{:S(2)}) collective-permute-start(bf16[256,1024]{1,0:T(8,128)(2,1)} %get-tuple-element.49), channel_id=1, source_target_pairs={{0,4},{1,5},{2,6},{3,7},{4,8},{5,9},{6,10},{7,11},{8,12},{9,13},{1... | collective-permute-start | bytes 1572872 | tf_op jit(solution)/shard_map/ppermute | solution.py:48
  44.8 27.1 %collective-permute-start.5 = (bf16[256,1024]{1,0:T(8,128)(2,1)}, bf16[256,1024]{1,0:T(8,128)(2,1)}, u32[]{:S(2)}, u32[]{:S(2)}) collective-permute-start(bf16[256,1024]{1,0:T(8,128)(2,1)} %get-tuple-element.50), channel_id=1, source_target_pairs={{0,8},{1,9},{2,10},{3,11},{4,12},{5,13},{6,14},{7,15},{8,0},{9,1},... | collective-permute-start | bytes 1572872 | tf_op jit(solution)/shard_map/ppermute | solution.py:48
  47.5 21.7 %copy-start.10 = (f32[2,32,128]{2,1,0:T(8,128)S(1)}, f32[2,32,128]{2,1,0:T(8,128)}, u32[]{:S(2)}) copy-start(f32[2,32,128]{2,1,0:T(8,128)} %get-tuple-element.47.refs_9_) | copy-start | bytes 98308
  47.5 24.4 %collective-permute-start.6 = (bf16[256,1024]{1,0:T(8,128)(2,1)}, bf16[256,1024]{1,0:T(8,128)(2,1)}, u32[]{:S(2)}, u32[]{:S(2)}) collective-permute-start(bf16[256,1024]{1,0:T(8,128)(2,1)} %get-tuple-element.51), channel_id=1, source_target_pairs={{0,12},{1,13},{2,14},{3,15},{4,0},{5,1},{6,2},{7,3},{8,4},{9,5},{1... | collective-permute-start | bytes 1572872 | tf_op jit(solution)/shard_map/ppermute | solution.py:48
  56.2 25.9 %collective-permute-start.9 = (bf16[512,512]{1,0:T(8,128)(2,1)}, bf16[512,512]{1,0:T(8,128)(2,1)S(1)}, u32[]{:S(2)}, u32[]{:S(2)}) collective-permute-start(bf16[512,512]{1,0:T(8,128)(2,1)} %get-tuple-element.53), channel_id=1, source_target_pairs={{0,1},{1,2},{2,3},{3,0},{4,5},{5,6},{6,7},{7,4},{8,9},{9,10},{10,1... | collective-permute-start | bytes 1572872 | tf_op jit(solution)/shard_map/ppermute | solution.py:39
  58.7 23.4 %collective-permute-start.10 = (bf16[512,512]{1,0:T(8,128)(2,1)}, bf16[512,512]{1,0:T(8,128)(2,1)S(1)}, u32[]{:S(2)}, u32[]{:S(2)}) collective-permute-start(bf16[512,512]{1,0:T(8,128)(2,1)} %get-tuple-element.54), channel_id=1, source_target_pairs={{0,3},{1,0},{2,1},{3,2},{4,7},{5,4},{6,5},{7,6},{8,11},{9,8},{10,9... | collective-permute-start | bytes 1572872 | tf_op jit(solution)/shard_map/ppermute | solution.py:39
  69.3 25.2 %collective-permute-start.18 = (f32[2,32,128]{2,1,0:T(8,128)S(1)}, f32[2,32,128]{2,1,0:T(8,128)S(1)}, u32[]{:S(2)}, u32[]{:S(2)}) collective-permute-start(f32[2,32,128]{2,1,0:T(8,128)S(1)} %copy-done.10), channel_id=1, source_target_pairs={{0,128},{16,144},{32,160},{48,176},{64,192},{80,208},{96,224},{112... | collective-permute-start | bytes 98312 | tf_op jit(solution)/shard_map/ppermute | solution.py:43
  84.9 21.6 %collective-permute-start.14 = (bf16[384,512]{1,0:T(8,128)(2,1)}, bf16[384,512]{1,0:T(8,128)(2,1)S(1)}, u32[]{:S(2)}, u32[]{:S(2)}) collective-permute-start(bf16[384,512]{1,0:T(8,128)(2,1)} %get-tuple-element.63), channel_id=1, source_target_pairs={{0,3},{1,0},{2,1},{3,2},{4,7},{5,4},{6,5},{7,6},{8,11},{9,8},{10,9... | collective-permute-start | bytes 1179656 | tf_op jit(solution)/shard_map/ppermute | solution.py:39
  88.1 18.5 %collective-permute-start.15 = (bf16[384,512]{1,0:T(8,128)(2,1)}, bf16[384,512]{1,0:T(8,128)(2,1)S(1)}, u32[]{:S(2)}, u32[]{:S(2)}) collective-permute-start(bf16[384,512]{1,0:T(8,128)(2,1)} %get-tuple-element.64), channel_id=1, source_target_pairs={{0,1},{1,2},{2,3},{3,0},{4,5},{5,6},{6,7},{7,4},{8,9},{9,10},{10,1... | collective-permute-start | bytes 1179656 | tf_op jit(solution)/shard_map/ppermute | solution.py:39
  100.3 4.3 %collective-permute-start.19 = (f32[4,32,128]{2,1,0:T(8,128)S(1)}, f32[4,32,128]{2,1,0:T(8,128)S(1)}, u32[]{:S(2)}, u32[]{:S(2)}) collective-permute-start(f32[4,32,128]{2,1,0:T(8,128)S(1)} %pad_maximum_fusion.1), channel_id=1, source_target_pairs={{0,64},{16,80},{32,96},{48,112},{64,0},{80,16},{96,32},{112,48},{1... | collective-permute-start | bytes 196616 | tf_op jit(solution)/shard_map/ppermute | solution.py:43
  104.4 7.1 %collective-permute-start.11 = (bf16[256,512]{1,0:T(8,128)(2,1)}, bf16[256,512]{1,0:T(8,128)(2,1)S(1)}, u32[]{:S(2)}, u32[]{:S(2)}) collective-permute-start(bf16[256,512]{1,0:T(8,128)(2,1)} %get-tuple-element.56), channel_id=1, source_target_pairs={{0,12},{1,13},{2,14},{3,15},{4,0},{5,1},{6,2},{7,3},{8,4},{9,5},{1... | collective-permute-start | bytes 786440 | tf_op jit(solution)/shard_map/ppermute | solution.py:48
  104.4 12.3 %collective-permute-start.12 = (bf16[256,512]{1,0:T(8,128)(2,1)}, bf16[256,512]{1,0:T(8,128)(2,1)S(1)}, u32[]{:S(2)}, u32[]{:S(2)}) collective-permute-start(bf16[256,512]{1,0:T(8,128)(2,1)} %get-tuple-element.57), channel_id=1, source_target_pairs={{0,8},{1,9},{2,10},{3,11},{4,12},{5,13},{6,14},{7,15},{8,0},{9,1},... | collective-permute-start | bytes 786440 | tf_op jit(solution)/shard_map/ppermute | solution.py:48
  104.5 12.1 %collective-permute-start.13 = (bf16[256,512]{1,0:T(8,128)(2,1)}, bf16[256,512]{1,0:T(8,128)(2,1)S(1)}, u32[]{:S(2)}, u32[]{:S(2)}) collective-permute-start(bf16[256,512]{1,0:T(8,128)(2,1)} %get-tuple-element.58), channel_id=1, source_target_pairs={{0,4},{1,5},{2,6},{3,7},{4,8},{5,9},{6,10},{7,11},{8,12},{9,13},{1... | collective-permute-start | bytes 786440 | tf_op jit(solution)/shard_map/ppermute | solution.py:48
  106.5 13.1 %copy-start.8 = (f32[8,32,128]{2,1,0:T(8,128)}, f32[8,32,128]{2,1,0:T(8,128)S(1)}, u32[]{:S(2)}) copy-start(f32[8,32,128]{2,1,0:T(8,128)S(1)} %constant_dynamic-update-slice_fusion.near) | copy-start | bytes 393220
  106.5 13.0 %collective-permute-start.20 = (f32[8,32,128]{2,1,0:T(8,128)S(1)}, f32[8,32,128]{2,1,0:T(8,128)S(1)}, u32[]{:S(2)}, u32[]{:S(2)}) collective-permute-start(f32[8,32,128]{2,1,0:T(8,128)S(1)} %constant_dynamic-update-slice_fusion.near), channel_id=1, source_target_pairs={{0,16},{16,0},{32,48},{48,32},{64,80},{80,64},{96,112},{112,96},{1... | collective-permute-start | bytes 393224 | tf_op jit(solution)/shard_map/ppermute | solution.py:43
  109.3 14.3 %collective-permute-start.16 = (bf16[128,512]{1,0:T(8,128)(2,1)}, bf16[128,512]{1,0:T(8,128)(2,1)S(1)}, u32[]{:S(2)}, u32[]{:S(2)}) collective-permute-start(bf16[128,512]{1,0:T(8,128)(2,1)} %get-tuple-element.67), channel_id=1, source_target_pairs={{0,3},{1,0},{2,1},{3,2},{4,7},{5,4},{6,5},{7,6},{8,11},{9,8},{10,9... | collective-permute-start | bytes 393224 | tf_op jit(solution)/shard_map/ppermute | solution.py:39
  111.5 12.1 %collective-permute-start.17 = (bf16[128,512]{1,0:T(8,128)(2,1)}, bf16[128,512]{1,0:T(8,128)(2,1)S(1)}, u32[]{:S(2)}, u32[]{:S(2)}) collective-permute-start(bf16[128,512]{1,0:T(8,128)(2,1)} %get-tuple-element.68), channel_id=1, source_target_pairs={{0,1},{1,2},{2,3},{3,0},{4,5},{5,6},{6,7},{7,4},{8,9},{9,10},{10,1... | collective-permute-start | bytes 393224 | tf_op jit(solution)/shard_map/ppermute | solution.py:39
  (15 other events, 29.3 us)
